TPU v7x, 32 devices: a whole 2x2x4 slice. The times are simulated.
32 devices in a mesh: groups: 2 (over y), adapter: 4 (over z), tensor: 2 (over x), section: 2 (over core).
Axes of the slice: x: 2, y: 2, z: 4, core: 2. Of those that a mesh axis runs over, the one named last changes fastest.
Arguments:
- activations: bfloat16 [1024, 8192], P(('groups', 'adapter', 'section'), 'tensor'), parts along dimension 0, may hold values from -6 to 6
- adapter_ids: int32 [1024, 1], P(('groups', 'adapter', 'section')), parts along dimension 0, may hold values from 0 to 7; in each aligned block of 64 rows (0 to 63, 64 to 127, ...) at most 16 rows name the same one
- base_weight: bfloat16 [8192, 8192], P('tensor', 'adapter'), may hold values from -0.0625 to 0.0625
- shrink_weight: bfloat16 [8, 8192, 64], P('adapter', 'tensor'), may hold values from -0.0625 to 0.0625
- expand_weight: bfloat16 [8, 64, 8192], P('adapter', None, 'tensor'), may hold values from -0.75 to 0.75
Outputs:
- projected: bfloat16 [1024, 8192], P(('groups', 'adapter', 'section'), 'tensor'), parts along dimension 0
There are 2 independent parts, one for each index of `groups`. A program takes and returns all parts, laid end to end along the dimension named above; an argument that names none is the same for every part. Nothing has to cross between parts.
Inputs may be any that keep to these rules, and one draw needn't show every extreme that they name: `adapter_ids`: in each aligned block of 64 rows (the rows of one device), no adapter is named by more than 16 rows; in some blocks one adapter is named by exactly 16 rows.
All inputs are finite; a program needn't handle non-finite values.
Results may differ from a plain program's by a relative error of at most 0.0034.
Values may be sent and summed in bfloat16 or wider, within the bound.
No kernel may reach another device: no remote copies, remote signals or barrier semaphores. Data moves between devices by JAX's collectives and lax.ppermute only.
A program may use at most 64 MiB of HBM per device.

v0:
```python
import jax
import jax.numpy as jnp
from jax import lax
from jax.sharding import PartitionSpec as P

adapter_scale_factor = 0.5


def ranks_of(block_ids):
    count = block_ids.shape[-1]
    earlier = lax.broadcasted_iota(jnp.int32, (count, count), 1) < lax.broadcasted_iota(
        jnp.int32, (count, count), 0
    )
    same = block_ids[..., :, None] == block_ids[..., None, :]
    return jnp.sum(jnp.logical_and(same, earlier).astype(jnp.int32), axis=-1)


def body(activations, adapter_ids, base_weight, shrink_weight, expand_weight):
    row_ids = adapter_ids[:, 0]
    tok_rows = activations.shape[0]
    feat_part = activations.shape[1]
    output_slice = expand_weight.shape[2]
    out_cols = base_weight.shape[1]
    n_adapt = lax.axis_size("adapter")
    local_count = shrink_weight.shape[0]
    most_rows = max(2, 2 * tok_rows // (local_count * n_adapt))
    resident_slot_list = local_count * most_rows
    all_slots = n_adapt * resident_slot_list
    home_slot = row_ids * most_rows + ranks_of(row_ids)
    home_map = (
        lax.broadcasted_iota(jnp.int32, (all_slots, tok_rows), 0) == home_slot[None, :]
    ).astype(jnp.bfloat16)
    base_part = jnp.dot(
        lax.all_gather(activations, "adapter", axis=0, tiled=True),
        base_weight,
        preferred_element_type=jnp.float32,
    )
    outgoing = jnp.dot(home_map, activations, preferred_element_type=jnp.float32).astype(
        jnp.bfloat16
    )
    outgoing = outgoing.reshape(n_adapt, resident_slot_list, feat_part)
    arrived = lax.all_to_all(outgoing, "adapter", split_axis=0, concat_axis=0, tiled=True)
    sender_slots = arrived.shape[0]
    grouped = arrived.reshape(sender_slots, local_count, most_rows, feat_part)
    partial_rank = jnp.einsum(
        "sjrd,jdk->sjrk", grouped, shrink_weight, preferred_element_type=jnp.float32
    )
    shrunk = lax.psum(partial_rank, "tensor").astype(jnp.bfloat16)
    expanded_rows = jnp.einsum(
        "sjrk,jkn->sjrn", shrunk, expand_weight, preferred_element_type=jnp.float32
    )
    final_outputs = (
        (adapter_scale_factor * expanded_rows)
        .astype(jnp.bfloat16)
        .reshape(sender_slots, resident_slot_list, output_slice)
    )
    returned = lax.all_to_all(final_outputs, "adapter", split_axis=0, concat_axis=0, tiled=True)
    delta = jnp.einsum(
        "st,sd->td",
        home_map,
        returned.reshape(all_slots, output_slice),
        preferred_element_type=jnp.float32,
    )
    base_blocks = base_part.reshape(n_adapt, tok_rows, out_cols)
    moved = lax.all_to_all(base_blocks, "adapter", split_axis=0, concat_axis=2, tiled=True)
    moved = moved.reshape(tok_rows, out_cols * n_adapt)
    base = lax.psum_scatter(moved, "tensor", scatter_dimension=1, tiled=True)
    return (base + delta).astype(jnp.bfloat16)


def solution(mesh):
    in_specs = (
        P(("groups", "adapter", "section"), "tensor"),
        P(("groups", "adapter", "section"), None),
        P("tensor", "adapter"),
        P("adapter", "tensor", None),
        P("adapter", None, "tensor"),
    )
    out_specs = P(("groups", "adapter", "section"), "tensor")
    return jax.shard_map(body, mesh=mesh, in_specs=in_specs, out_specs=out_specs, check_vma=False)
```

profile of v0, /device:TPU:10, one launch (start us, length us, event | category | flops | bytes accessed | tf_op | source)
XLA Modules:
  0.0 196.7 jit_solution(9083657730559539545)
XLA Ops:
  6.5 0.0 copy-start
  6.5 0.0 all-gather.2.cloned.1.call-start
  6.5 0.7 all-gather.2.cloned.1.call-update
  7.3 47.2 %all-gather.2.cloned.1.call-done = bf16[256,4096]{1,0:T(8,128)(2,1)} async-done(((bf16[64,4096]{1,0:T(8,128)(2,1)}), bf16[256,4096]{1,0:T(8,128)(2,1)}) %all-gather.2.cloned.1.call-update) | async-done | bytes 2097168 | tf_op jit(solution)/shard_map/all_gather | solution.py:34
  54.4 12.2 %fusion.10 = f32[256,2048]{1,0:T(8,128)} fusion(bf16[256,4096]{1,0:T(8,128)(2,1)} %all-gather.2.cloned.1.call-done, bf16[4096,2048]{1,0:T(8,128)(2,1)} %param.7), kind=kOutput, calls=%fused_computation.18 | convolution fusion | flops 4294967296 | bytes 20971520 | tf_op jit(solution)/shard_map/dot_general | solution.py:33
  66.6 0.0 copy-start.3
  66.6 5.9 %all-to-all-start = ((f32[4,64,2048]{2,1,0:T(8,128)}), f32[4,64,2048]{2,1,0:T(8,128)S(1)}, u32[]{:S(2)}, u32[]{:S(2)}) async-start(f32[4,64,2048]{2,1,0:T(8,128)} %bitcast.38), calls=%async_computation | async-start | bytes 4194304 | tf_op jit(solution)/shard_map/all_to_all | solution.py:65
  72.5 0.0 reduce-scatter.2.cloned.1.call-start
  72.5 0.0 copy-done.3
  72.5 0.2 convert_reduce_fusion
  72.7 45.0 %all-to-all-done = f32[4,64,2048]{2,1,0:T(8,128)S(1)} async-done(((f32[4,64,2048]{2,1,0:T(8,128)}), f32[4,64,2048]{2,1,0:T(8,128)S(1)}, u32[]{:S(2)}, u32[]{:S(2)}) %all-to-all-start) | async-done | bytes 2097184 | tf_op jit(solution)/shard_map/all_to_all | solution.py:65
  117.7 1.4 copy.11
  119.0 2.5 %copy.16 = f32[8,8,4,2048]{3,1,2,0:T(8,128)} copy(f32[8,8,4,2048]{3,2,1,0:T(4,128)S(1)} %bitcast.34) | data formatting | bytes 4194304
  121.6 0.0 copy-start.1
  121.6 0.0 reduce-scatter.2.cloned.1.call-update
  121.6 0.0 copy-start.2
  121.6 1.0 copy-done.1
  122.6 0.4 convolution_convert_fusion
  123.1 29.2 %all_to_all.25 = bf16[4,32,4096]{2,1,0:T(8,128)(2,1)S(1)} all-to-all(bf16[4,32,4096]{2,1,0:T(8,128)(2,1)S(1)} %bitcast.37), channel_id=1, replica_groups=mesh['groups'=2,'adapter'=4,'tensor'=2,'section'=2] {'adapter'}, dimensions={0} | all-to-all | bytes 2097152 | tf_op jit(solution)/shard_map/all_to_all | solution.py:42
  152.2 0.0 copy-done.2
  152.2 0.4 convolution_bitcast_fusion
  152.7 8.2 %psum.7 = bf16[4,2,16,64]{3,2,0,1:T(8,128)(2,1)S(1)} all-reduce(f32[4,2,16,64]{3,2,0,1:T(8,128)S(1)} %convolution_bitcast_fusion), channel_id=1, replica_groups=mesh['groups'=2,'adapter'=4,'tensor'=2,'section'=2] {'tensor'}, use_global_device_ids=true, to_apply=%region_2.0 | all-reduce | flops 8192 | bytes 49152 | tf_op jit(solution)/shard_map/psum | solution.py:48
  160.9 0.0 copy-done
  160.9 0.4 fusion.1
  161.3 0.1 copy.13
  161.4 26.0 %all_to_all.26 = bf16[4,32,4096]{2,1,0:T(8,128)(2,1)S(1)} all-to-all(bf16[4,32,4096]{2,1,0:T(8,128)(2,1)S(1)} %bitcast.36), channel_id=1, replica_groups=mesh['groups'=2,'adapter'=4,'tensor'=2,'section'=2] {'adapter'}, dimensions={0} | all-to-all | bytes 2097152 | tf_op jit(solution)/shard_map/all_to_all | solution.py:57
  187.5 0.0 reduce-scatter.2.cloned.1.call-done
  187.5 2.4 %fusion.2 = bf16[64,4096]{1,0:T(8,128)(2,1)} fusion(f32[64,4096]{1,0:T(8,128)} %reduce-scatter.2.cloned.1.call-done, bf16[128,4096]{1,0:T(8,128)(2,1)S(1)} %bitcast.35, s32[64]{0:T(128)S(1)} %multiply_add_fusion), kind=kOutput, calls=%fused_computation.5 | convolution fusion | flops 67641344 | bytes 2621696 | tf_op jit(solution)/shard_map/st,sd->td/dot_general | solution.py:58
  (1 shorter events, 0.0 us)
Async XLA Ops:
  6.5 154.4 %copy-start = (bf16[2,64,4096]{2,1,0:T(8,128)(2,1)S(1)}, bf16[2,64,4096]{2,1,0:T(8,128)(2,1)}, u32[]{:S(2)}) copy-start(bf16[2,64,4096]{2,1,0:T(8,128)(2,1)} %param.9) | copy-start | bytes 3145732
  6.5 47.9 %all-gather.2.cloned.1.call-start = ((), (), s32[]{:S(2)}) async-start(), calls=%async_computation.4 | async-start | bytes 2621440 | tf_op jit(solution)/shard_map/all_gather | solution.py:34
  66.6 5.9 %copy-start.3 = (s32[64,1]{0,1:T(1,128)S(1)}, s32[64,1]{0,1:T(1,128)}, u32[]{:S(2)}) copy-start(s32[64,1]{0,1:T(1,128)} %param.6) | copy-start | bytes 772
  66.6 51.1 %all-to-all-start = ((f32[4,64,2048]{2,1,0:T(8,128)}), f32[4,64,2048]{2,1,0:T(8,128)S(1)}, u32[]{:S(2)}, u32[]{:S(2)}) async-start(f32[4,64,2048]{2,1,0:T(8,128)} %bitcast.38), calls=%async_computation | async-start | bytes 4194304 | tf_op jit(solution)/shard_map/all_to_all | solution.py:65
  72.5 115.0 %reduce-scatter.2.cloned.1.call-start = ((), (), s32[]{:S(2)}) async-start(), calls=%async_computation.5 | async-start | bytes 3145728 | tf_op jit(solution)/shard_map/reduce_scatter | solution.py:67
  121.6 1.0 copy-start.1
  121.6 30.6 %copy-start.2 = (bf16[2,4096,64]{1,2,0:T(8,128)(2,1)S(1)}, bf16[2,4096,64]{1,2,0:T(8,128)(2,1)}, u32[]{:S(2)}) copy-start(bf16[2,4096,64]{1,2,0:T(8,128)(2,1)} %param.8) | copy-start | bytes 3145732
Sparse Core Ops, SparseCore 0:
  8.9 45.4 all-gather.1
  121.7 32.6 reduce-scatter.1
where the time goes:
time: 200 us; the launch traced here: 197 us
  waiting for transfers between devices  92.9 us (46%)
  blocking collectives  63.5 us (32%)
  matrix products  15.8 us (8%)
  between operations  13.5 us (7%)
  starting transfers between devices  5.85 us (3%)
  local copies, waits for them, and re-layouts  4.98 us (2%)
    all_gather x1, waiting for transfers between devices, body(): lax.all_gather(activations, 'adapter', axis=0, tiled=True)  47.2 us
    all_to_all x1, waiting for transfers between devices, body(): lax.all_to_all(base_blocks, 'adapter', split_axis=0, concat_axis=2, tiled...  45 us
    all_to_all x1, blocking collectives, body(): lax.all_to_all(outgoing, 'adapter', split_axis=0, concat_axis=0, tiled=True)  29.2 us
    all_to_all x1, blocking collectives, body(): lax.all_to_all(final_outputs, 'adapter', split_axis=0, concat_axis=0, til...  26 us
    dot_general x1, matrix products, body(): jnp.dot(lax.all_gather(activations, 'adapter', axis=0, tiled=True), base_...  12.2 us
    psum x1, blocking collectives, body(): shrunk = lax.psum(partial_rank, 'tensor').astype(jnp.bfloat16)  8.22 us
    all_to_all x1, starting transfers between devices, body(): lax.all_to_all(base_blocks, 'adapter', split_axis=0, concat_axis=2, tiled...  5.85 us
  transfers between devices with their start and end apart: 3, of which 2 were waited for; matrix products, arithmetic and copies ran while one was open for 1% of the time, Pallas kernels for 0%

commit v1 on v0

--- a/solution.py
+++ b/solution.py
@@ -1,9 +1,14 @@
+import functools
+
 import jax
 import jax.numpy as jnp
 from jax import lax
+from jax.experimental import pallas as pl
+from jax.experimental.pallas import tpu as pltpu
 from jax.sharding import PartitionSpec as P
 
 adapter_scale_factor = 0.5
+VMEM_LIMIT = 24 * 1024 * 1024
 
 
 def ranks_of(block_ids):
@@ -15,7 +20,11 @@
     return jnp.sum(jnp.logical_and(same, earlier).astype(jnp.int32), axis=-1)
 
 
-def body(activations, adapter_ids, base_weight, shrink_weight, expand_weight):
+def most_rows_of(tok_rows, adapters):
+    return max(2, 2 * tok_rows // adapters)
+
+
+def body_any(activations, adapter_ids, base_weight, shrink_weight, expand_weight):
     row_ids = adapter_ids[:, 0]
     tok_rows = activations.shape[0]
     feat_part = activations.shape[1]
@@ -23,7 +32,7 @@
     out_cols = base_weight.shape[1]
     n_adapt = lax.axis_size("adapter")
     local_count = shrink_weight.shape[0]
-    most_rows = max(2, 2 * tok_rows // (local_count * n_adapt))
+    most_rows = most_rows_of(tok_rows, local_count * n_adapt)
     resident_slot_list = local_count * most_rows
     all_slots = n_adapt * resident_slot_list
     home_slot = row_ids * most_rows + ranks_of(row_ids)
@@ -68,6 +77,190 @@
     return (base + delta).astype(jnp.bfloat16)
 
 
+VM = pl.BlockSpec(memory_space=pltpu.VMEM)
+SM = pl.BlockSpec(memory_space=pltpu.SMEM)
+F32 = jnp.float32
+BF16 = jnp.bfloat16
+
+
+def stage_kernel(n_in, *refs):
+    x_refs, (w_ref, s_ref, p32_ref, p16_ref, sh_ref) = refs[:n_in], refs[n_in:]
+    x = x_refs[0][...]
+    for other in x_refs[1:]:
+        x = x + other[...]
+    sh_ref[...] = lax.dot_general(
+        x, s_ref[...], (((1,), (1,)), ((), ())), preferred_element_type=F32
+    )
+    cols = w_ref.shape[1]
+    step = 256
+    for j in range(0, cols, step):
+        part = jnp.dot(x, w_ref[:, j : j + step], preferred_element_type=F32)
+        p32_ref[:, j : j + step] = part
+        p16_ref[:, j : j + step] = part.astype(BF16)
+
+
+def stage(xs, w, s_t):
+    rows, depth = xs[0].shape
+    cols = w.shape[1]
+    return pl.pallas_call(
+        functools.partial(stage_kernel, len(xs)),
+        in_specs=[VM] * (len(xs) + 2),
+        out_specs=[VM] * 3,
+        out_shape=[
+            jax.ShapeDtypeStruct((rows, cols), F32),
+            jax.ShapeDtypeStruct((rows, cols), BF16),
+            jax.ShapeDtypeStruct((rows, s_t.shape[0]), F32),
+        ],
+        compiler_params=pltpu.CompilerParams(vmem_limit_bytes=VMEM_LIMIT),
+        cost_estimate=pl.CostEstimate(
+            flops=2 * rows * depth * cols, bytes_accessed=depth * cols * 2, transcendentals=0
+        ),
+    )(*xs, w, s_t)
+
+
+def delta_kernel(k, most, meta_ref, slots_ref, e_ref, *refs):
+    ins, outs = refs[: 2 * k], refs[2 * k :]
+    local, rank, width = e_ref.shape
+    first = meta_ref[0] * (local * most)
+    table = slots_ref[...]
+    which = lax.broadcasted_iota(jnp.int32, table.shape, 0)
+    rows = table.shape[1]
+    slot = lax.broadcasted_iota(jnp.int32, (local * most, rows), 0) + first
+    for i in range(k):
+        shrunk = (ins[2 * i][...] + ins[2 * i + 1][...]).astype(BF16)
+        home = jnp.sum(jnp.where(which == meta_ref[1 + i], table, 0), axis=0, keepdims=True)
+        pick = (slot == home).astype(BF16)
+        chosen = jnp.dot(pick, shrunk, preferred_element_type=F32).astype(BF16)
+        for j in range(local):
+            lines = slice(j * most, (j + 1) * most)
+            wide = jnp.dot(
+                chosen[lines, j * rank : (j + 1) * rank], e_ref[j], preferred_element_type=F32
+            )
+            outs[i][lines, :] = (adapter_scale_factor * wide).astype(BF16)
+
+
+def deltas(meta, slots, e, pairs, most):
+    k = len(pairs)
+    local, _, width = e.shape
+    flat = [a for pair in pairs for a in pair]
+    return pl.pallas_call(
+        functools.partial(delta_kernel, k, most),
+        in_specs=[SM] + [VM] * (2 + 2 * k),
+        out_specs=[VM] * k,
+        out_shape=[jax.ShapeDtypeStruct((local * most, width), BF16)] * k,
+        compiler_params=pltpu.CompilerParams(vmem_limit_bytes=VMEM_LIMIT),
+        cost_estimate=pl.CostEstimate(
+            flops=k * 2 * local * most * 64 * width, bytes_accessed=4 << 20, transcendentals=0
+        ),
+    )(meta, slots, e, *flat)
+
+
+def final_kernel(meta_ref, slot_ref, own32_ref, own16_ref, b1, b2, b3, d0, d1, d2, d3, o_ref, base):
+    rows, quarter = own32_ref.shape
+    spots = d0.shape[0]
+    slot = slot_ref[...]
+    lane = lax.broadcasted_iota(jnp.int32, (rows, spots), 1)
+    picks = [(slot == lane + meta_ref[k] * spots).astype(BF16) for k in range(4)]
+    for q in range(2):
+        cols = slice(q * quarter, (q + 1) * quarter)
+        source = meta_ref[4 + q]
+
+        @pl.when(source == 0)
+        def _():
+            base[...] = own32_ref[...] + own16_ref[...].astype(F32)
+
+        for k, ref in ((1, b1), (2, b2), (3, b3)):
+
+            @pl.when(source == k)
+            def _():
+                base[...] = ref[...].astype(F32)
+
+        total = base[...]
+        for pick, d in zip(picks, (d0, d1, d2, d3)):
+            total = total + jnp.dot(pick, d[:, cols], preferred_element_type=F32)
+        o_ref[:, cols] = total.astype(BF16)
+
+
+def body_four(activations, adapter_ids, base_weight, shrink_weight, expand_weight):
+    row_ids = adapter_ids[:, 0]
+    rows = activations.shape[0]
+    local, _, rank = shrink_weight.shape
+    quarter = base_weight.shape[1]
+    most = most_rows_of(rows, local * 4)
+    me = lax.axis_index("adapter")
+    half = lax.axis_index("tensor")
+    both = ("adapter", "tensor")
+
+    def along(x, pairs):
+        return lax.ppermute(x, "adapter", pairs)
+
+    held = ((1, 3, 0, 2), (3, 2, 1, 0), (2, 0, 3, 1))
+
+    def back(k):
+        return [(a, held[k - 1][a]) for a in range(4)]
+
+    def pick(table):
+        return sum(jnp.where(me == a, table[a], 0) for a in range(4))
+
+    planes = [[h for h in range(4)]]
+    for k in (1, 2, 3):
+        planes.append([held[k - 1].index(h) for h in range(4)])
+    plane_of = [pick(p) for p in planes]
+    source = [sum(jnp.where(plane_of[k] == 2 * half + q, k, 0) for k in range(4)) for q in (0, 1)]
+    meta_home = jnp.stack(plane_of + source).astype(jnp.int32)
+    meta_owner = jnp.stack([me, me] + [pick(h) for h in held]).astype(jnp.int32)
+
+    home_slot = row_ids * most + ranks_of(row_ids)
+    slots = lax.all_gather(home_slot[None, :], "adapter", axis=0, tiled=True)
+
+    x = activations
+    s_t = jnp.swapaxes(shrink_weight, 1, 2).reshape(local * rank, -1)
+    w = base_weight
+    got_a = along(x, [(0, 2), (3, 1), (1, 0), (2, 3)])
+    p32_0, p16_0, s_0 = stage([x], w, s_t)
+    x_later, p16_0 = lax.optimization_barrier((x, p16_0))
+    got_c = along(x_later, [(0, 1), (3, 2), (2, 0), (1, 3)])
+    got_b = along(x_later, [(1, 2), (2, 1)])
+    got_f = along(got_a, [(1, 0), (2, 3)])
+
+    p32_1, p16_1, s_1 = stage([got_a], w, s_t)
+    p32_2, p16_2, s_2 = stage([got_f, got_b], w, s_t)
+    p32_3, p16_3, s_3 = stage([got_c], w, s_t)
+
+    def to_half(p):
+        return lax.ppermute(
+            p, both, [(2 * a + 1 - a // 2, 2 * a + a // 2) for a in range(4)]
+        )
+
+    def home_base(p, k):
+        return lax.ppermute(
+            p, both, [(2 * a + a // 2, 2 * h + a // 2) for a, h in back(k)]
+        )
+
+    def flip(s):
+        return lax.ppermute(s, "tensor", [(0, 1), (1, 0)])
+
+    own16 = to_half(p16_0)
+    bases = []
+    for k, p32, p16 in ((1, p32_1, p16_1), (2, p32_2, p16_2), (3, p32_3, p16_3)):
+        bases.append(home_base((p32 + to_half(p16)).astype(BF16), k))
+
+    e = expand_weight
+    d_0, d_1 = deltas(meta_owner[0:3], slots, e, [(s_0, flip(s_0)), (s_1, flip(s_1))], most)
+    (d_2,) = deltas(meta_owner[jnp.array([0, 3])], slots, e, [(s_2, flip(s_2))], most)
+    (d_3,) = deltas(meta_owner[jnp.array([0, 4])], slots, e, [(s_3, flip(s_3))], most)
+    d_1, d_2, d_3 = along(d_1, back(1)), along(d_2, back(2)), along(d_3, back(3))
+
+    return pl.pallas_call(
+        final_kernel,
+        in_specs=[SM] + [VM] * 10,
+        out_specs=VM,
+        out_shape=jax.ShapeDtypeStruct((rows, 2 * quarter), BF16),
+        scratch_shapes=[pltpu.VMEM((rows, quarter), F32)],
+        compiler_params=pltpu.CompilerParams(vmem_limit_bytes=VMEM_LIMIT),
+    )(meta_home, home_slot[:, None], p32_0, own16, *bases, d_0, d_1, d_2, d_3)
+
+
 def solution(mesh):
     in_specs = (
         P(("groups", "adapter", "section"), "tensor"),
@@ -77,4 +270,6 @@
         P("adapter", None, "tensor"),
     )
     out_specs = P(("groups", "adapter", "section"), "tensor")
+    four = mesh.shape["adapter"] == 4 and mesh.shape["tensor"] == 2
+    body = body_four if four else body_any
     return jax.shard_map(body, mesh=mesh, in_specs=in_specs, out_specs=out_specs, check_vma=False)

time: 200 us -> 140 us (0.70); the launches traced: 197 us -> 139 us
  waiting for transfers between devices: 92.9 us -> 33.8 us
  blocking collectives: 63.5 us -> 11 us
  starting transfers between devices: 5.85 us -> 35.9 us
  local copies, waits for them, and re-layouts: 4.98 us -> 32.4 us
  Pallas kernels: 0 us -> 23.4 us
  matrix products: 15.8 us -> 0 us
  between operations: 13.5 us -> 0.36 us
  other arithmetic: 0.18 us -> 2.39 us
    all_to_all x2 -> x0, blocking collectives: 55.2 us -> none  [the longest x1 29.2 us: body(): lax.all_to_all(outgoing, 'adapter', split_axis=0, concat_axis=0, tiled=True)]
    all_gather x1 -> x0, waiting for transfers between devices: 47.2 us -> none  [body(): lax.all_gather(activations, 'adapter', axis=0, tiled=True)]
    all_to_all x1 -> x0, waiting for transfers between devices: 45 us -> none  [body(): lax.all_to_all(base_blocks, 'adapter', split_axis=0, concat_axis=2, tiled...]
    ppermute x0 -> x18, starting transfers between devices: none -> 35.9 us  [the longest x7 20.4 us: along(): return lax.ppermute(x, 'adapter', pairs)]
    ppermute x0 -> x18, waiting for transfers between devices: none -> 33.8 us  [the longest x7 20.5 us: along(): return lax.ppermute(x, 'adapter', pairs)]
    unnamed x9 -> x53, local copies, waits for them, and re-layouts: 3.54 us -> 30.9 us
    pallas_call x0 -> x8, Pallas kernels: none -> 23.4 us  [the longest x4 17.4 us: stage(): pl.pallas_call(functools.partial(stage_kernel, len(xs)), in_specs=[VM] *...]
    dot_general x5 -> x0, matrix products: 15.8 us -> none  [the longest x1 12.2 us: body(): jnp.dot(lax.all_gather(activations, 'adapter', axis=0, tiled=True), base_...]
  transfers between devices with their start and end apart: 3 -> 18, of which waited for: 2 -> 6; matrix products, arithmetic and copies ran while one was open for 1% -> 3% of each run, Pallas kernels for 0% -> 15%
where the time goes in v1:
time: 140 us; the launch traced here: 139 us
  starting transfers between devices  35.9 us (26%)
  waiting for transfers between devices  33.8 us (24%)
  local copies, waits for them, and re-layouts  32.4 us (23%)
  Pallas kernels  23.4 us (17%)
  blocking collectives  11 us (8%)
  other arithmetic  2.39 us (2%)
    unnamed x53, local copies, waits for them, and re-layouts  30.9 us
    ppermute x7, waiting for transfers between devices, along(): return lax.ppermute(x, 'adapter', pairs)  20.5 us
    ppermute x7, starting transfers between devices, along(): return lax.ppermute(x, 'adapter', pairs)  20.4 us
    pallas_call x4, Pallas kernels, stage(): pl.pallas_call(functools.partial(stage_kernel, len(xs)), in_specs=[VM] *...  17.4 us
    all_gather x1, blocking collectives, body_four(): slots = lax.all_gather(home_slot[None, :], 'adapter', axis=0, tiled=True)  11 us
    ppermute x4, starting transfers between devices, to_half(): lax.ppermute(p, both, [(2 * a + 1 - a // 2, 2 * a + a // 2) for a in rang...  9.56 us
    ppermute x3, waiting for transfers between devices, home_base(): lax.ppermute(p, both, [(2 * a + a // 2, 2 * h + a // 2) for a, h in back(...  7.38 us
    ppermute x4, waiting for transfers between devices, flip(): return lax.ppermute(s, 'tensor', [(0, 1), (1, 0)])  5.94 us
  transfers between devices with their start and end apart: 18, of which 6 were waited for; matrix products, arithmetic and copies ran while one was open for 3% of the time, Pallas kernels for 15%

profile of v1, /device:TPU:10, one launch (start us, length us, event | category | flops | bytes accessed | tf_op | source)
XLA Modules:
  0.0 139.3 jit_solution(1213262907887602240)
XLA Ops:
  0.0 0.4 collective-permute-start.1
  0.5 5.8 %copy-done = bf16[4096,2048]{1,0:T(8,128)(2,1)S(1)} copy-done((bf16[4096,2048]{1,0:T(8,128)(2,1)S(1)}, bf16[4096,2048]{1,0:T(8,128)(2,1)}, u32[]{:S(2)}) %copy-start) | copy-done | bytes 16777240
  6.2 1.2 copy-done.3
  7.5 4.5 %shard_map.73 = (f32[64,2048]{1,0:T(8,128)S(1)}, bf16[64,2048]{1,0:T(8,128)(2,1)S(1)}, f32[64,128]{1,0:T(8,128)S(1)}) custom-call(bf16[64,4096]{1,0:T(8,128)(2,1)} %refs_0_.1, bf16[4096,2048]{1,0:T(8,128)(2,1)S(1)} %copy-done, bf16[128,4096]{1,0:T(8,128)(2,1)S(1)} %bitcast.21), custom_call_target="tpu_custom_call" | custom-call | flops 1073741824 | bytes 16777216 | tf_op jit(solution)/shard_map/pallas_call | solution.py:105
  11.9 0.0 copy-start.9
  12.0 0.8 copy-done.9
  12.7 0.7 copy-done.23
  13.4 4.6 %collective-permute-start.5 = (bf16[64,4096]{1,0:T(8,128)(2,1)}, bf16[64,4096]{1,0:T(8,128)(2,1)S(1)}, u32[]{:S(2)}, u32[]{:S(2)}) collective-permute-start(bf16[64,4096]{1,0:T(8,128)(2,1)} %refs_0_.1), channel_id=1, source_target_pairs={{4,8},{8,4},{5,9},{9,5},{6,10},{10,6},{7,11},{11,7},{20,24},{24,20... | collective-permute-start | bytes 1572872 | tf_op jit(solution)/shard_map/ppermute | solution.py:195
  18.0 0.1 collective-permute-start.8
  18.1 0.6 collective-permute-start.11
  18.7 0.1 copy.18
  18.8 0.2 convert_reduce_fusion
  19.0 0.1 copy.20
  19.1 0.1 multiply_reduce_fusion
  19.3 5.8 %copy-done.1 = bf16[4096,2048]{1,0:T(8,128)(2,1)S(1)} copy-done((bf16[4096,2048]{1,0:T(8,128)(2,1)S(1)}, bf16[4096,2048]{1,0:T(8,128)(2,1)}, u32[]{:S(2)}) %copy-start.1) | copy-done | bytes 16777240
  25.0 4.1 %shard_map.74 = (f32[64,2048]{1,0:T(8,128)S(1)}, bf16[64,2048]{1,0:T(8,128)(2,1)}, f32[64,128]{1,0:T(8,128)S(1)}) custom-call(bf16[64,4096]{1,0:T(8,128)(2,1)S(1)} %collective-permute-done.1.refs_0_, bf16[4096,2048]{1,0:T(8,128)(2,1)S(1)} %copy-done.1, bf16[128,4096]{1,0:T(8,128)(2,1)S(1)} %bitcast.22), custom_call_target="tpu_custom_call" | custom-call | flops 1073741824 | bytes 16777216 | tf_op jit(solution)/shard_map/pallas_call | solution.py:105
  29.1 0.8 copy-done.8
  29.9 4.1 %collective-permute-start.2 = (bf16[64,2048]{1,0:T(8,128)(2,1)}, bf16[64,2048]{1,0:T(8,128)(2,1)}, u32[]{:S(2)}, u32[]{:S(2)}) collective-permute-start(bf16[64,2048]{1,0:T(8,128)(2,1)} %get-tuple-element.25), channel_id=1, source_target_pairs={{2,0},{6,4},{8,10},{12,14},{3,1},{7,5},{9,11},{13,15},{18,16},{22,... | collective-permute-start | bytes 786440 | tf_op jit(solution)/shard_map/ppermute | solution.py:231
  34.0 6.5 %collective-permute-done.8.refs_0_ = bf16[64,4096]{1,0:T(8,128)(2,1)} collective-permute-done((bf16[64,4096]{1,0:T(8,128)(2,1)}, bf16[64,4096]{1,0:T(8,128)(2,1)}, u32[]{:S(2)}, u32[]{:S(2)}) %collective-permute-start.8) | collective-permute-done | bytes 524320 | tf_op jit(solution)/shard_map/ppermute | solution.py:195
  40.5 4.4 %shard_map.76 = (f32[64,2048]{1,0:T(8,128)S(1)}, bf16[64,2048]{1,0:T(8,128)(2,1)S(1)}, f32[64,128]{1,0:T(8,128)S(1)}) custom-call(bf16[64,4096]{1,0:T(8,128)(2,1)} %collective-permute-done.8.refs_0_, bf16[4096,2048]{1,0:T(8,128)(2,1)S(1)} %copy-done.1, bf16[128,4096]{1,0:T(8,128)(2,1)S(1)} %bitcast.23), custom_call_target="tpu_custom_call" | custom-call | flops 1073741824 | bytes 16777216 | tf_op jit(solution)/shard_map/pallas_call | solution.py:105
  44.9 0.8 copy-done.6
  45.7 0.7 copy-done.24
  46.4 0.5 collective-permute-start.16
  47.0 1.5 %collective-permute-start.12 = (f32[64,128]{1,0:T(8,128)S(1)}, f32[64,128]{1,0:T(8,128)}, u32[]{:S(2)}, u32[]{:S(2)}) collective-permute-start(f32[64,128]{1,0:T(8,128)S(1)} %get-tuple-element.32.refs_2_), channel_id=1, source_target_pairs={{0,2},{2,0},{1,3},{3,1},{4,6},{6,4},{5,7},{7,5},{8,10},{10,8},{9,1... | collective-permute-start | bytes 98312 | tf_op jit(solution)/shard_map/ppermute | solution.py:241
  48.5 1.9 %collective-permute-done.16.refs_1_ = f32[64,128]{1,0:T(8,128)S(1)} collective-permute-done((f32[64,128]{1,0:T(8,128)S(1)}, f32[64,128]{1,0:T(8,128)S(1)}, u32[]{:S(2)}, u32[]{:S(2)}) %collective-permute-start.16) | collective-permute-done | bytes 32800 | tf_op jit(solution)/shard_map/ppermute | solution.py:241
  50.3 4.9 %collective-permute-start.4 = (bf16[64,4096]{1,0:T(8,128)(2,1)S(1)}, bf16[64,4096]{1,0:T(8,128)(2,1)}, u32[]{:S(2)}, u32[]{:S(2)}) collective-permute-start(bf16[64,4096]{1,0:T(8,128)(2,1)S(1)} %collective-permute-done.1.refs_0_), channel_id=1, source_target_pairs={{4,0},{8,12},{5,1},{9,13},{6,2},{10,14},{7,3},{11,15},{20,16},{24,... | collective-permute-start | bytes 1572872 | tf_op jit(solution)/shard_map/ppermute | solution.py:195
  55.3 0.1 pad_add_fusion.meta_ref
  55.3 0.1 stack.42
  55.4 0.6 gather_fusion
  56.1 0.6 gather_fusion.1
  56.7 11.0 %all-gather = s32[4,1,64]{2,1,0:T(1,128)S(1)} all-gather(s32[1,1,64]{2,1,0:T(1,128)S(1)} %fusion.1), channel_id=1, replica_groups=mesh['groups'=2,'adapter'=4,'tensor'=2,'section'=2] {'adapter'}, dimensions={0}, use_global_device_ids=true | all-gather | bytes 1280 | tf_op jit(solution)/shard_map/all_gather | solution.py:214
  67.7 0.7 copy-done.20
  68.5 0.8 copy-done.22
  69.2 0.9 shard_map.79
  70.2 2.5 %collective-permute-start = (bf16[64,2048]{1,0:T(8,128)(2,1)}, bf16[64,2048]{1,0:T(8,128)(2,1)S(1)}, u32[]{:S(2)}, u32[]{:S(2)}) collective-permute-start(bf16[64,2048]{1,0:T(8,128)(2,1)} %copy-done.23), channel_id=1, source_target_pairs={{2,0},{6,4},{8,10},{12,14},{3,1},{7,5},{9,11},{13,15},{18,16},{22,... | collective-permute-start | bytes 786440 | tf_op jit(solution)/shard_map/ppermute | solution.py:231
  72.6 1.3 collective-permute-start.9
  74.0 1.4 %shard_map.77 = (bf16[32,4096]{1,0:T(8,128)(2,1)S(1)}, bf16[32,4096]{1,0:T(8,128)(2,1)S(1)}) custom-call(s32[3]{0:T(128)S(1)} %pad_add_fusion.meta_ref, s32[4,64]{1,0:T(4,128)S(1)} %bitcast.26, bf16[2,64,4096]{2,1,0:T(8,128)(2,1)S(1)} %copy-done.5, f32[64,128]{1,0:T(8,128)S(1)} %get-tuple-element.31.refs_0_, f32[64,128]{1,0:T(8,128)S(1)} %collective-permute-done.11.refs_1_, ...), custom_call_target="tpu_custom_call" | custom-call | flops 33554432 | bytes 4194304 | tf_op jit(solution)/shard_map/pallas_call | solution.py:146
  75.4 0.1 collective-permute-start.13
  75.4 1.9 %add_convert_fusion.2 = bf16[64,2048]{1,0:T(8,128)(2,1)} fusion(f32[64,2048]{1,0:T(8,128)} %copy-done.8, bf16[64,2048]{1,0:T(8,128)(2,1)} %collective-permute-done.2), kind=kLoop, calls=%fused_computation.4 | loop fusion | flops 393216 | bytes 1048576 | tf_op jit(solution)/shard_map/convert_element_type | solution.py:246
  77.3 2.3 %collective-permute-start.17 = (bf16[32,4096]{1,0:T(8,128)(2,1)S(1)}, bf16[32,4096]{1,0:T(8,128)(2,1)}, u32[]{:S(2)}, u32[]{:S(2)}) collective-permute-start(bf16[32,4096]{1,0:T(8,128)(2,1)S(1)} %shard_map.79), channel_id=1, source_target_pairs={{0,8},{4,0},{8,12},{12,4},{1,9},{5,1},{9,13},{13,5},{2,10},{6,2},{... | collective-permute-start | bytes 786440 | tf_op jit(solution)/shard_map/ppermute | solution.py:195
  79.7 5.8 %copy-done.2 = bf16[4096,2048]{1,0:T(8,128)(2,1)S(1)} copy-done((bf16[4096,2048]{1,0:T(8,128)(2,1)S(1)}, bf16[4096,2048]{1,0:T(8,128)(2,1)}, u32[]{:S(2)}) %copy-start.2) | copy-done | bytes 16777240
  85.4 4.4 %shard_map.75 = (f32[64,2048]{1,0:T(8,128)S(1)}, bf16[64,2048]{1,0:T(8,128)(2,1)S(1)}, f32[64,128]{1,0:T(8,128)S(1)}) custom-call(bf16[64,4096]{1,0:T(8,128)(2,1)} %collective-permute-done.4.refs_0_, bf16[64,4096]{1,0:T(8,128)(2,1)S(1)} %collective-permute-done.5.refs_1_, bf16[4096,2048]{1,0:T(8,128)(2,1)S(1)} %copy-done.2, bf16[128,4096]{1,0:T(8,128)(2,1)S(1)} %bitcast.24), custom_call_target="tpu_custom_call" | custom-call | flops 1073741824 | bytes 16777216 | tf_op jit(solution)/shard_map/pallas_call | solution.py:105
  89.9 1.7 %collective-permute-start.6 = (bf16[64,2048]{1,0:T(8,128)(2,1)S(1)}, bf16[64,2048]{1,0:T(8,128)(2,1)S(1)}, u32[]{:S(2)}, u32[]{:S(2)}) collective-permute-start(bf16[64,2048]{1,0:T(8,128)(2,1)S(1)} %get-tuple-element.28), channel_id=1, source_target_pairs={{2,0},{6,4},{8,10},{12,14},{3,1},{7,5},{9,11},{13,15},{18,16},{22,... | collective-permute-start | bytes 786440 | tf_op jit(solution)/shard_map/ppermute | solution.py:231
  91.6 0.1 collective-permute-start.14
  91.7 4.1 %collective-permute-done.14.refs_1_ = f32[64,128]{1,0:T(8,128)S(1)} collective-permute-done((f32[64,128]{1,0:T(8,128)S(1)}, f32[64,128]{1,0:T(8,128)S(1)}, u32[]{:S(2)}, u32[]{:S(2)}) %collective-permute-start.14) | collective-permute-done | bytes 32800 | tf_op jit(solution)/shard_map/ppermute | solution.py:241
  95.8 0.7 collective-permute-start.3
  96.5 0.9 shard_map.78
  97.4 1.3 collective-permute-start.10
  98.7 0.1 add_convert_fusion.1
  98.8 0.7 copy-done.11
  99.5 8.0 %collective-permute-start.15 = (bf16[32,4096]{1,0:T(8,128)(2,1)S(1)}, bf16[32,4096]{1,0:T(8,128)(2,1)S(1)}, u32[]{:S(2)}, u32[]{:S(2)}) collective-permute-start(bf16[32,4096]{1,0:T(8,128)(2,1)S(1)} %shard_map.78), channel_id=1, source_target_pairs={{0,12},{4,8},{8,4},{12,0},{1,13},{5,9},{9,5},{13,1},{2,14},{6,10},... | collective-permute-start | bytes 786440 | tf_op jit(solution)/shard_map/ppermute | solution.py:195
  107.5 0.7 copy-done.15
  108.2 1.3 collective-permute-start.7
  109.6 0.1 stack.39.meta_ref
  109.7 0.7 copy-done.17
  110.4 4.6 %collective-permute-done.10.b3 = bf16[64,2048]{1,0:T(8,128)(2,1)S(1)} collective-permute-done((bf16[64,2048]{1,0:T(8,128)(2,1)S(1)}, bf16[64,2048]{1,0:T(8,128)(2,1)S(1)}, u32[]{:S(2)}, u32[]{:S(2)}) %collective-permute-start.10) | collective-permute-done | bytes 262176 | tf_op jit(solution)/shard_map/ppermute | solution.py:236
  114.9 14.0 %collective-permute-done.15.d2 = bf16[32,4096]{1,0:T(8,128)(2,1)S(1)} collective-permute-done((bf16[32,4096]{1,0:T(8,128)(2,1)S(1)}, bf16[32,4096]{1,0:T(8,128)(2,1)S(1)}, u32[]{:S(2)}, u32[]{:S(2)}) %collective-permute-start.15) | collective-permute-done | bytes 262176 | tf_op jit(solution)/shard_map/ppermute | solution.py:195
  128.9 2.8 %collective-permute-done.7.b2 = bf16[64,2048]{1,0:T(8,128)(2,1)S(1)} collective-permute-done((bf16[64,2048]{1,0:T(8,128)(2,1)S(1)}, bf16[64,2048]{1,0:T(8,128)(2,1)S(1)}, u32[]{:S(2)}, u32[]{:S(2)}) %collective-permute-start.7) | collective-permute-done | bytes 262176 | tf_op jit(solution)/shard_map/ppermute | solution.py:236
  131.7 1.0 copy-done.10
  132.8 0.9 copy-done.12
  133.7 0.9 copy-done.14
  134.7 0.9 copy-done.16
  135.6 0.9 copy-done.18
  136.6 2.7 %shard_map.80 = bf16[64,4096]{1,0:T(8,128)(2,1)} custom-call(s32[6]{0:T(128)S(1)} %stack.39.meta_ref, s32[64,1]{1,0:T(8,128)S(1)} %get-tuple-element.38.slot_ref, f32[64,2048]{1,0:T(8,128)S(1)} %copy-done.10, bf16[64,2048]{1,0:T(8,128)(2,1)S(1)} %copy-done.12, bf16[64,2048]{1,0:T(8,128)(2,1)S(1)} %copy-done.18, ...), custom_call_target="tpu_custom_call" | custom-call | tf_op jit(solution)/shard_map/pallas_call | solution.py:254
  (50 shorter events, 0.2 us)
Async XLA Ops:
  0.0 18.7 %copy-start.25 = (s32[64,1]{0,1:T(1,128)S(1)}, s32[64,1]{0,1:T(1,128)}, u32[]{:S(2)}) copy-start(s32[64,1]{0,1:T(1,128)} %param.8) | copy-start | bytes 772
  0.0 19.2 %collective-permute-start.1 = (bf16[64,4096]{1,0:T(8,128)(2,1)}, bf16[64,4096]{1,0:T(8,128)(2,1)S(1)}, u32[]{:S(2)}, u32[]{:S(2)}) collective-permute-start(bf16[64,4096]{1,0:T(8,128)(2,1)} %refs_0_.1), channel_id=1, source_target_pairs={{0,8},{12,4},{4,0},{8,12},{1,9},{13,5},{5,1},{9,13},{2,10},{14,6},... | collective-permute-start | bytes 1572872 | tf_op jit(solution)/shard_map/ppermute | solution.py:195
  0.5 5.8 %copy-start = (bf16[4096,2048]{1,0:T(8,128)(2,1)S(1)}, bf16[4096,2048]{1,0:T(8,128)(2,1)}, u32[]{:S(2)}) copy-start(bf16[4096,2048]{1,0:T(8,128)(2,1)} %refs_1_.5) | copy-start | bytes 50331652
  6.2 1.2 copy-start.3
  7.4 11.8 %copy-start.4 = (bf16[2,4096,64]{1,2,0:T(8,128)(2,1)S(1)}, bf16[2,4096,64]{1,2,0:T(8,128)(2,1)}, u32[]{:S(2)}) copy-start(bf16[2,4096,64]{1,2,0:T(8,128)(2,1)} %param.10) | copy-start | bytes 3145732
  11.9 0.8 copy-start.9
  12.7 0.7 copy-start.23
  13.4 63.9 %collective-permute-start.5 = (bf16[64,4096]{1,0:T(8,128)(2,1)}, bf16[64,4096]{1,0:T(8,128)(2,1)S(1)}, u32[]{:S(2)}, u32[]{:S(2)}) collective-permute-start(bf16[64,4096]{1,0:T(8,128)(2,1)} %refs_0_.1), channel_id=1, source_target_pairs={{4,8},{8,4},{5,9},{9,5},{6,10},{10,6},{7,11},{11,7},{20,24},{24,20... | collective-permute-start | bytes 1572872 | tf_op jit(solution)/shard_map/ppermute | solution.py:195
  18.0 22.4 %collective-permute-start.8 = (bf16[64,4096]{1,0:T(8,128)(2,1)}, bf16[64,4096]{1,0:T(8,128)(2,1)}, u32[]{:S(2)}, u32[]{:S(2)}) collective-permute-start(bf16[64,4096]{1,0:T(8,128)(2,1)} %refs_0_.1), channel_id=1, source_target_pairs={{0,4},{12,8},{8,0},{4,12},{1,5},{13,9},{9,1},{5,13},{2,6},{14,10},... | collective-permute-start | bytes 1572872 | tf_op jit(solution)/shard_map/ppermute | solution.py:195
  18.1 52.0 %collective-permute-start.11 = (f32[64,128]{1,0:T(8,128)S(1)}, f32[64,128]{1,0:T(8,128)S(1)}, u32[]{:S(2)}, u32[]{:S(2)}) collective-permute-start(f32[64,128]{1,0:T(8,128)S(1)} %get-tuple-element.31.refs_0_), channel_id=1, source_target_pairs={{0,2},{2,0},{1,3},{3,1},{4,6},{6,4},{5,7},{7,5},{8,10},{10,8},{9,1... | collective-permute-start | bytes 98312 | tf_op jit(solution)/shard_map/ppermute | solution.py:241
  19.3 5.8 %copy-start.1 = (bf16[4096,2048]{1,0:T(8,128)(2,1)S(1)}, bf16[4096,2048]{1,0:T(8,128)(2,1)}, u32[]{:S(2)}) copy-start(bf16[4096,2048]{1,0:T(8,128)(2,1)} %refs_1_.5) | copy-start | bytes 50331652
  25.0 42.7 %copy-start.5 = (bf16[2,64,4096]{2,1,0:T(8,128)(2,1)S(1)}, bf16[2,64,4096]{2,1,0:T(8,128)(2,1)}, u32[]{:S(2)}) copy-start(bf16[2,64,4096]{2,1,0:T(8,128)(2,1)} %e_ref.5) | copy-start | bytes 3145732
  29.1 0.8 copy-start.8
  29.9 45.5 %collective-permute-start.2 = (bf16[64,2048]{1,0:T(8,128)(2,1)}, bf16[64,2048]{1,0:T(8,128)(2,1)}, u32[]{:S(2)}, u32[]{:S(2)}) collective-permute-start(bf16[64,2048]{1,0:T(8,128)(2,1)} %get-tuple-element.25), channel_id=1, source_target_pairs={{2,0},{6,4},{8,10},{12,14},{3,1},{7,5},{9,11},{13,15},{18,16},{22,... | collective-permute-start | bytes 786440 | tf_op jit(solution)/shard_map/ppermute | solution.py:231
  44.9 0.8 copy-start.6
  45.7 0.7 copy-start.24
  46.4 21.3 %copy-start.19 = (f32[64,128]{1,0:T(8,128)}, f32[64,128]{1,0:T(8,128)S(1)}, u32[]{:S(2)}) copy-start(f32[64,128]{1,0:T(8,128)S(1)} %get-tuple-element.36.refs_0_) | copy-start | bytes 98308
  46.4 3.9 %collective-permute-start.16 = (f32[64,128]{1,0:T(8,128)S(1)}, f32[64,128]{1,0:T(8,128)S(1)}, u32[]{:S(2)}, u32[]{:S(2)}) collective-permute-start(f32[64,128]{1,0:T(8,128)S(1)} %get-tuple-element.36.refs_0_), channel_id=1, source_target_pairs={{0,2},{2,0},{1,3},{3,1},{4,6},{6,4},{5,7},{7,5},{8,10},{10,8},{9,1... | collective-permute-start | bytes 98312 | tf_op jit(solution)/shard_map/ppermute | solution.py:241
  47.0 25.7 %collective-permute-start.12 = (f32[64,128]{1,0:T(8,128)S(1)}, f32[64,128]{1,0:T(8,128)}, u32[]{:S(2)}, u32[]{:S(2)}) collective-permute-start(f32[64,128]{1,0:T(8,128)S(1)} %get-tuple-element.32.refs_2_), channel_id=1, source_target_pairs={{0,2},{2,0},{1,3},{3,1},{4,6},{6,4},{5,7},{7,5},{8,10},{10,8},{9,1... | collective-permute-start | bytes 98312 | tf_op jit(solution)/shard_map/ppermute | solution.py:241
  50.3 17.4 %copy-start.21 = (f32[64,128]{1,0:T(8,128)}, f32[64,128]{1,0:T(8,128)S(1)}, u32[]{:S(2)}) copy-start(f32[64,128]{1,0:T(8,128)S(1)} %collective-permute-done.16.refs_1_) | copy-start | bytes 98308
  50.3 29.3 %collective-permute-start.4 = (bf16[64,4096]{1,0:T(8,128)(2,1)S(1)}, bf16[64,4096]{1,0:T(8,128)(2,1)}, u32[]{:S(2)}, u32[]{:S(2)}) collective-permute-start(bf16[64,4096]{1,0:T(8,128)(2,1)S(1)} %collective-permute-done.1.refs_0_), channel_id=1, source_target_pairs={{4,0},{8,12},{5,1},{9,13},{6,2},{10,14},{7,3},{11,15},{20,16},{24,... | collective-permute-start | bytes 1572872 | tf_op jit(solution)/shard_map/ppermute | solution.py:195
  56.7 35.0 %copy-start.7 = (f32[64,2048]{1,0:T(8,128)S(1)}, f32[64,2048]{1,0:T(8,128)}, u32[]{:S(2)}) copy-start(f32[64,2048]{1,0:T(8,128)} %copy-done.6) | copy-start | bytes 1572868
  67.7 0.8 copy-start.20
  68.5 0.8 copy-start.22
  70.2 28.6 %collective-permute-start = (bf16[64,2048]{1,0:T(8,128)(2,1)}, bf16[64,2048]{1,0:T(8,128)(2,1)S(1)}, u32[]{:S(2)}, u32[]{:S(2)}) collective-permute-start(bf16[64,2048]{1,0:T(8,128)(2,1)} %copy-done.23), channel_id=1, source_target_pairs={{2,0},{6,4},{8,10},{12,14},{3,1},{7,5},{9,11},{13,15},{18,16},{22,... | collective-permute-start | bytes 786440 | tf_op jit(solution)/shard_map/ppermute | solution.py:231
  72.6 19.0 %collective-permute-start.9 = (bf16[64,2048]{1,0:T(8,128)(2,1)}, bf16[64,2048]{1,0:T(8,128)(2,1)S(1)}, u32[]{:S(2)}, u32[]{:S(2)}) collective-permute-start(bf16[64,2048]{1,0:T(8,128)(2,1)} %copy-done.24), channel_id=1, source_target_pairs={{2,0},{6,4},{8,10},{12,14},{3,1},{7,5},{9,11},{13,15},{18,16},{22,... | collective-permute-start | bytes 786440 | tf_op jit(solution)/shard_map/ppermute | solution.py:231
  75.4 4.3 %copy-start.13 = (bf16[32,4096]{1,0:T(8,128)(2,1)}, bf16[32,4096]{1,0:T(8,128)(2,1)S(1)}, u32[]{:S(2)}) copy-start(bf16[32,4096]{1,0:T(8,128)(2,1)S(1)} %get-tuple-element.33.d0) | copy-start | bytes 786436
  75.4 32.1 %collective-permute-start.13 = (bf16[32,4096]{1,0:T(8,128)(2,1)S(1)}, bf16[32,4096]{1,0:T(8,128)(2,1)S(1)}, u32[]{:S(2)}, u32[]{:S(2)}) collective-permute-start(bf16[32,4096]{1,0:T(8,128)(2,1)S(1)} %get-tuple-element.34), channel_id=1, source_target_pairs={{0,4},{4,12},{8,0},{12,8},{1,5},{5,13},{9,1},{13,9},{2,6},{6,14},{... | collective-permute-start | bytes 786440 | tf_op jit(solution)/shard_map/ppermute | solution.py:195
  77.3 32.3 %collective-permute-start.17 = (bf16[32,4096]{1,0:T(8,128)(2,1)S(1)}, bf16[32,4096]{1,0:T(8,128)(2,1)}, u32[]{:S(2)}, u32[]{:S(2)}) collective-permute-start(bf16[32,4096]{1,0:T(8,128)(2,1)S(1)} %shard_map.79), channel_id=1, source_target_pairs={{0,8},{4,0},{8,12},{12,4},{1,9},{5,1},{9,13},{13,5},{2,10},{6,2},{... | collective-permute-start | bytes 786440 | tf_op jit(solution)/shard_map/ppermute | solution.py:195
  79.7 5.8 %copy-start.2 = (bf16[4096,2048]{1,0:T(8,128)(2,1)S(1)}, bf16[4096,2048]{1,0:T(8,128)(2,1)}, u32[]{:S(2)}) copy-start(bf16[4096,2048]{1,0:T(8,128)(2,1)} %refs_1_.5) | copy-start | bytes 50331652
  89.9 7.5 %collective-permute-start.6 = (bf16[64,2048]{1,0:T(8,128)(2,1)S(1)}, bf16[64,2048]{1,0:T(8,128)(2,1)S(1)}, u32[]{:S(2)}, u32[]{:S(2)}) collective-permute-start(bf16[64,2048]{1,0:T(8,128)(2,1)S(1)} %get-tuple-element.28), channel_id=1, source_target_pairs={{2,0},{6,4},{8,10},{12,14},{3,1},{7,5},{9,11},{13,15},{18,16},{22,... | collective-permute-start | bytes 786440 | tf_op jit(solution)/shard_map/ppermute | solution.py:231
  91.6 4.2 %collective-permute-start.14 = (f32[64,128]{1,0:T(8,128)S(1)}, f32[64,128]{1,0:T(8,128)S(1)}, u32[]{:S(2)}, u32[]{:S(2)}) collective-permute-start(f32[64,128]{1,0:T(8,128)S(1)} %get-tuple-element.35.refs_0_), channel_id=1, source_target_pairs={{0,2},{2,0},{1,3},{3,1},{4,6},{6,4},{5,7},{7,5},{8,10},{10,8},{9,1... | collective-permute-start | bytes 98312 | tf_op jit(solution)/shard_map/ppermute | solution.py:241
  95.8 13.8 %collective-permute-start.3 = (bf16[64,2048]{1,0:T(8,128)(2,1)}, bf16[64,2048]{1,0:T(8,128)(2,1)S(1)}, u32[]{:S(2)}, u32[]{:S(2)}) collective-permute-start(bf16[64,2048]{1,0:T(8,128)(2,1)} %add_convert_fusion.2), channel_id=1, source_target_pairs={{0,4},{4,12},{10,2},{14,10},{1,5},{5,13},{11,3},{15,11},{16,20},{2... | collective-permute-start | bytes 786440 | tf_op jit(solution)/shard_map/ppermute | solution.py:236
  97.4 17.5 %collective-permute-start.10 = (bf16[64,2048]{1,0:T(8,128)(2,1)S(1)}, bf16[64,2048]{1,0:T(8,128)(2,1)S(1)}, u32[]{:S(2)}, u32[]{:S(2)}) collective-permute-start(bf16[64,2048]{1,0:T(8,128)(2,1)S(1)} %add_convert_fusion), channel_id=1, source_target_pairs={{0,8},{4,0},{10,14},{14,6},{1,9},{5,1},{11,15},{15,7},{16,24},{20,... | collective-permute-start | bytes 786440 | tf_op jit(solution)/shard_map/ppermute | solution.py:236
  98.8 0.7 copy-start.11
  99.5 29.4 %collective-permute-start.15 = (bf16[32,4096]{1,0:T(8,128)(2,1)S(1)}, bf16[32,4096]{1,0:T(8,128)(2,1)S(1)}, u32[]{:S(2)}, u32[]{:S(2)}) collective-permute-start(bf16[32,4096]{1,0:T(8,128)(2,1)S(1)} %shard_map.78), channel_id=1, source_target_pairs={{0,12},{4,8},{8,4},{12,0},{1,13},{5,9},{9,5},{13,1},{2,14},{6,10},... | collective-permute-start | bytes 786440 | tf_op jit(solution)/shard_map/ppermute | solution.py:195
  107.5 0.7 copy-start.15
  108.2 23.5 %collective-permute-start.7 = (bf16[64,2048]{1,0:T(8,128)(2,1)S(1)}, bf16[64,2048]{1,0:T(8,128)(2,1)S(1)}, u32[]{:S(2)}, u32[]{:S(2)}) collective-permute-start(bf16[64,2048]{1,0:T(8,128)(2,1)S(1)} %add_convert_fusion.1), channel_id=1, source_target_pairs={{0,12},{4,8},{10,6},{14,2},{1,13},{5,9},{11,7},{15,3},{16,28},{20,... | collective-permute-start | bytes 786440 | tf_op jit(solution)/shard_map/ppermute | solution.py:236
  109.6 0.7 copy-start.17
  131.7 1.0 copy-start.10
  132.8 0.9 copy-start.12
  133.7 0.9 copy-start.14
  134.7 0.9 copy-start.16
  135.6 0.9 copy-start.18

commit v2 on v1

--- a/solution.py
+++ b/solution.py
@@ -8,7 +8,7 @@
 from jax.sharding import PartitionSpec as P
 
 adapter_scale_factor = 0.5
-VMEM_LIMIT = 24 * 1024 * 1024
+VMEM_LIMIT = 8 * 1024 * 1024
 
 
 def ranks_of(block_ids):
@@ -78,17 +78,81 @@
 
 
 VM = pl.BlockSpec(memory_space=pltpu.VMEM)
-SM = pl.BlockSpec(memory_space=pltpu.SMEM)
 F32 = jnp.float32
 BF16 = jnp.bfloat16
 
 
-def stage_kernel(n_in, *refs):
-    x_refs, (w_ref, s_ref, p32_ref, p16_ref, sh_ref) = refs[:n_in], refs[n_in:]
+def slot_kernel(most, ids_ref, row_ref, col_ref):
+    ids = ids_ref[...]
+    count = ids.shape[1]
+    i = lax.broadcasted_iota(jnp.int32, (count, count), 0)
+    j = lax.broadcasted_iota(jnp.int32, (count, count), 1)
+    wide = jnp.broadcast_to(ids, (count, count))
+    tall = jnp.sum(jnp.where(i == j, wide, 0), axis=1, keepdims=True)
+    same = wide == tall
+    row_ref[...] = ids * most + jnp.sum(
+        jnp.where(same & (i < j), 1, 0), axis=0, keepdims=True
+    )
+    col_ref[...] = tall * most + jnp.sum(
+        jnp.where(same & (j < i), 1, 0), axis=1, keepdims=True
+    )
+
+
+def first_kernel(x_ref, s_ref, w_ref, held_ref, p32_ref, p16_ref, sh_ref, sems):
+    parts = sems.shape[0]
+    step = w_ref.shape[0] // parts
+
+    def copy(i):
+        lines = slice(i * step, (i + 1) * step)
+        return pltpu.make_async_copy(w_ref.at[lines, :], held_ref.at[lines, :], sems.at[i])
+
+    for i in range(parts):
+        copy(i).start()
+    sh_ref[...] = lax.dot_general(
+        x_ref[...], s_ref[...], (((1,), (1,)), ((), ())), preferred_element_type=F32
+    )
+    for i in range(parts):
+        copy(i).wait()
+        lines = slice(i * step, (i + 1) * step)
+        part = jnp.dot(x_ref[:, lines], held_ref[lines, :], preferred_element_type=F32)
+        if i > 0:
+            part = p32_ref[...] + part
+        p32_ref[...] = part
+        if i == parts - 1:
+            p16_ref[...] = part.astype(BF16)
+
+
+def first_stage(x, w, s_t):
+    rows, depth = x.shape
+    cols = w.shape[1]
+    return pl.pallas_call(
+        first_kernel,
+        in_specs=[VM, VM, pl.BlockSpec(memory_space=pl.ANY)],
+        out_specs=[VM] * 4,
+        out_shape=[
+            pltpu.VMEM(w.shape, w.dtype),
+            jax.ShapeDtypeStruct((rows, cols), F32),
+            jax.ShapeDtypeStruct((rows, cols), BF16),
+            jax.ShapeDtypeStruct((rows, s_t.shape[0]), F32),
+        ],
+        scratch_shapes=[pltpu.SemaphoreType.DMA((8,))],
+        compiler_params=pltpu.CompilerParams(vmem_limit_bytes=VMEM_LIMIT),
+        cost_estimate=pl.CostEstimate(
+            flops=2 * rows * depth * cols, bytes_accessed=depth * cols * 2, transcendentals=0
+        ),
+    )(x, s_t, pltpu.with_memory_space_constraint(w, pltpu.HBM))
+
+
+def stage_kernel(n_in, keep, *refs):
+    x_refs, (w_ref, s_ref), rest = refs[:n_in], refs[n_in : n_in + 2], refs[n_in + 2 :]
+    before, (p32_ref, p16_ref, sh_ref) = rest[:-3], rest[-3:]
     x = x_refs[0][...]
     for other in x_refs[1:]:
         x = x + other[...]
-    sh_ref[...] = lax.dot_general(
+    rows = x.shape[0]
+    if keep:
+        sh_ref[: sh_ref.shape[0] - rows, :] = before[0][...]
+    sh_ref[sh_ref.shape[0] - rows :, :] = lax.dot_general(
         x, s_ref[...], (((1,), (1,)), ((), ())), preferred_element_type=F32
     )
     cols = w_ref.shape[1]
@@ -99,37 +163,37 @@
         p16_ref[:, j : j + step] = part.astype(BF16)
 
 
-def stage(xs, w, s_t):
+def stage(xs, w, s_t, before=()):
     rows, depth = xs[0].shape
     cols = w.shape[1]
+    kept = rows + sum(b.shape[0] for b in before)
+    w = pltpu.with_memory_space_constraint(w, pltpu.VMEM)
     return pl.pallas_call(
-        functools.partial(stage_kernel, len(xs)),
-        in_specs=[VM] * (len(xs) + 2),
-        out_specs=[VM] * 3,
+        functools.partial(stage_kernel, len(xs), bool(before)),
+        in_specs=[VM] * (len(xs) + 2 + len(before)),
+        out_specs=[VM, VM, VM],
         out_shape=[
             jax.ShapeDtypeStruct((rows, cols), F32),
             jax.ShapeDtypeStruct((rows, cols), BF16),
-            jax.ShapeDtypeStruct((rows, s_t.shape[0]), F32),
+            jax.ShapeDtypeStruct((kept, s_t.shape[0]), F32),
         ],
         compiler_params=pltpu.CompilerParams(vmem_limit_bytes=VMEM_LIMIT),
         cost_estimate=pl.CostEstimate(
             flops=2 * rows * depth * cols, bytes_accessed=depth * cols * 2, transcendentals=0
         ),
-    )(*xs, w, s_t)
-
-
-def delta_kernel(k, most, meta_ref, slots_ref, e_ref, *refs):
-    ins, outs = refs[: 2 * k], refs[2 * k :]
-    local, rank, width = e_ref.shape
-    first = meta_ref[0] * (local * most)
-    table = slots_ref[...]
-    which = lax.broadcasted_iota(jnp.int32, table.shape, 0)
-    rows = table.shape[1]
+    )(*xs, w, s_t, *before)
+
+
+def delta_kernel(k, most, e_ref, *refs):
+    slots, mine, other, outs = refs[:k], refs[k], refs[k + 1], refs[k + 2 :]
+    local, rank, _ = e_ref.shape
+    first = lax.axis_index("adapter") * (local * most)
+    rows = slots[0].shape[1]
     slot = lax.broadcasted_iota(jnp.int32, (local * most, rows), 0) + first
     for i in range(k):
-        shrunk = (ins[2 * i][...] + ins[2 * i + 1][...]).astype(BF16)
-        home = jnp.sum(jnp.where(which == meta_ref[1 + i], table, 0), axis=0, keepdims=True)
-        pick = (slot == home).astype(BF16)
+        block = slice(i * rows, (i + 1) * rows)
+        shrunk = (mine[block, :] + other[block, :]).astype(BF16)
+        pick = (slot == slots[i][...]).astype(BF16)
         chosen = jnp.dot(pick, shrunk, preferred_element_type=F32).astype(BF16)
         for j in range(local):
             lines = slice(j * most, (j + 1) * most)
@@ -139,39 +203,39 @@
             outs[i][lines, :] = (adapter_scale_factor * wide).astype(BF16)
 
 
-def deltas(meta, slots, e, pairs, most):
-    k = len(pairs)
+def deltas(e, slots, mine, other, most):
+    k = len(slots)
     local, _, width = e.shape
-    flat = [a for pair in pairs for a in pair]
     return pl.pallas_call(
         functools.partial(delta_kernel, k, most),
-        in_specs=[SM] + [VM] * (2 + 2 * k),
+        in_specs=[VM] * (3 + k),
         out_specs=[VM] * k,
         out_shape=[jax.ShapeDtypeStruct((local * most, width), BF16)] * k,
         compiler_params=pltpu.CompilerParams(vmem_limit_bytes=VMEM_LIMIT),
         cost_estimate=pl.CostEstimate(
             flops=k * 2 * local * most * 64 * width, bytes_accessed=4 << 20, transcendentals=0
         ),
-    )(meta, slots, e, *flat)
-
-
-def final_kernel(meta_ref, slot_ref, own32_ref, own16_ref, b1, b2, b3, d0, d1, d2, d3, o_ref, base):
+    )(e, *slots, mine, other)
+
+
+def final_kernel(planes, slot_ref, own32_ref, own16_ref, b1, b2, b3, d0, d1, d2, d3, o_ref, base):
     rows, quarter = own32_ref.shape
+    me, half = lax.axis_index("adapter"), lax.axis_index("tensor")
+    plane_of = [sum(jnp.where(me == a, p[a], 0) for a in range(4)) for p in planes]
     spots = d0.shape[0]
     slot = slot_ref[...]
     lane = lax.broadcasted_iota(jnp.int32, (rows, spots), 1)
-    picks = [(slot == lane + meta_ref[k] * spots).astype(BF16) for k in range(4)]
+    picks = [(slot == lane + plane_of[k] * spots).astype(BF16) for k in range(4)]
     for q in range(2):
         cols = slice(q * quarter, (q + 1) * quarter)
-        source = meta_ref[4 + q]
-
-        @pl.when(source == 0)
+
+        @pl.when(plane_of[0] == 2 * half + q)
         def _():
             base[...] = own32_ref[...] + own16_ref[...].astype(F32)
 
         for k, ref in ((1, b1), (2, b2), (3, b3)):
 
-            @pl.when(source == k)
+            @pl.when(plane_of[k] == 2 * half + q)
             def _():
                 base[...] = ref[...].astype(F32)
 
@@ -182,13 +246,10 @@
 
 
 def body_four(activations, adapter_ids, base_weight, shrink_weight, expand_weight):
-    row_ids = adapter_ids[:, 0]
     rows = activations.shape[0]
     local, _, rank = shrink_weight.shape
     quarter = base_weight.shape[1]
     most = most_rows_of(rows, local * 4)
-    me = lax.axis_index("adapter")
-    half = lax.axis_index("tensor")
     both = ("adapter", "tensor")
 
     def along(x, pairs):
@@ -198,33 +259,37 @@
 
     def back(k):
         return [(a, held[k - 1][a]) for a in range(4)]
-
-    def pick(table):
-        return sum(jnp.where(me == a, table[a], 0) for a in range(4))
 
     planes = [[h for h in range(4)]]
     for k in (1, 2, 3):
         planes.append([held[k - 1].index(h) for h in range(4)])
-    plane_of = [pick(p) for p in planes]
-    source = [sum(jnp.where(plane_of[k] == 2 * half + q, k, 0) for k in range(4)) for q in (0, 1)]
-    meta_home = jnp.stack(plane_of + source).astype(jnp.int32)
-    meta_owner = jnp.stack([me, me] + [pick(h) for h in held]).astype(jnp.int32)
-
-    home_slot = row_ids * most + ranks_of(row_ids)
-    slots = lax.all_gather(home_slot[None, :], "adapter", axis=0, tiled=True)
-
     x = activations
+    got_a = along(x, [(0, 2), (3, 1), (1, 0), (2, 3)])
+
+    slot_row, slot_col = pl.pallas_call(
+        functools.partial(slot_kernel, most),
+        in_specs=[VM],
+        out_specs=[VM, VM],
+        out_shape=[
+            jax.ShapeDtypeStruct((1, rows), jnp.int32),
+            jax.ShapeDtypeStruct((rows, 1), jnp.int32),
+        ],
+        compiler_params=pltpu.CompilerParams(vmem_limit_bytes=VMEM_LIMIT),
+    )(adapter_ids.reshape(1, rows))
+    slots = [slot_row]
+    for k in (1, 2, 3):
+        slots.append(along(slot_row, [(h, a) for a, h in back(k)]))
+
     s_t = jnp.swapaxes(shrink_weight, 1, 2).reshape(local * rank, -1)
-    w = base_weight
-    got_a = along(x, [(0, 2), (3, 1), (1, 0), (2, 3)])
-    p32_0, p16_0, s_0 = stage([x], w, s_t)
-    x_later, p16_0 = lax.optimization_barrier((x, p16_0))
+    w, p32_0, p16_0, s_0 = first_stage(x, base_weight, s_t)
+    x_later, s_0 = lax.optimization_barrier((x, s_0))
     got_c = along(x_later, [(0, 1), (3, 2), (2, 0), (1, 3)])
     got_b = along(x_later, [(1, 2), (2, 1)])
     got_f = along(got_a, [(1, 0), (2, 3)])
 
-    p32_1, p16_1, s_1 = stage([got_a], w, s_t)
-    p32_2, p16_2, s_2 = stage([got_f, got_b], w, s_t)
+    p32_1, p16_1, s_1 = stage([got_a], w, s_t, [s_0])
+    p32_2, p16_2, s_2 = stage([got_f, got_b], w, s_t, [s_1])
+    got_c, s_2 = lax.optimization_barrier((got_c, s_2))
     p32_3, p16_3, s_3 = stage([got_c], w, s_t)
 
     def to_half(p):
@@ -246,19 +311,18 @@
         bases.append(home_base((p32 + to_half(p16)).astype(BF16), k))
 
     e = expand_weight
-    d_0, d_1 = deltas(meta_owner[0:3], slots, e, [(s_0, flip(s_0)), (s_1, flip(s_1))], most)
-    (d_2,) = deltas(meta_owner[jnp.array([0, 3])], slots, e, [(s_2, flip(s_2))], most)
-    (d_3,) = deltas(meta_owner[jnp.array([0, 4])], slots, e, [(s_3, flip(s_3))], most)
+    d_0, d_1, d_2 = deltas(e, slots[0:3], s_2, flip(s_2), most)
+    (d_3,) = deltas(e, slots[3:4], s_3, flip(s_3), most)
     d_1, d_2, d_3 = along(d_1, back(1)), along(d_2, back(2)), along(d_3, back(3))
 
     return pl.pallas_call(
-        final_kernel,
-        in_specs=[SM] + [VM] * 10,
+        functools.partial(final_kernel, planes),
+        in_specs=[VM] * 10,
         out_specs=VM,
         out_shape=jax.ShapeDtypeStruct((rows, 2 * quarter), BF16),
         scratch_shapes=[pltpu.VMEM((rows, quarter), F32)],
         compiler_params=pltpu.CompilerParams(vmem_limit_bytes=VMEM_LIMIT),
-    )(meta_home, home_slot[:, None], p32_0, own16, *bases, d_0, d_1, d_2, d_3)
+    )(slot_col, p32_0, own16, *bases, d_0, d_1, d_2, d_3)
 
 
 def solution(mesh):

time: 140 us -> 109 us (0.78)
  local copies, waits for them, and re-layouts: 32.4 us -> 1.23 us
  waiting for transfers between devices: 33.8 us -> 47 us
  blocking collectives: 11 us -> 0 us
  starting transfers between devices: 35.9 us -> 38.4 us
  Pallas kernels: 23.4 us -> 21.1 us
  other arithmetic: 2.39 us -> 0.17 us
    unnamed x53 -> x6, local copies, waits for them, and re-layouts: 30.9 us -> 1.23 us
    ppermute x7 -> x10, waiting for transfers between devices: 20.5 us -> 43.7 us  [along(): return lax.ppermute(x, 'adapter', pairs)]
    all_gather x1 -> x0, blocking collectives: 11 us -> none  [body_four(): slots = lax.all_gather(home_slot[None, :], 'adapter', axis=0, tiled=True)]
    ppermute x4, starting transfers between devices: 9.56 us -> 17.6 us  [to_half(): lax.ppermute(p, both, [(2 * a + 1 - a // 2, 2 * a + a // 2) for a in rang...]
    ppermute x4 -> x2, waiting for transfers between devices: 5.94 us -> 0.24 us  [flip(): return lax.ppermute(s, 'tensor', [(0, 1), (1, 0)])]
    ppermute x7 -> x10, starting transfers between devices: 20.4 us -> 15.4 us  [along(): return lax.ppermute(x, 'adapter', pairs)]
    ppermute x3, waiting for transfers between devices: 7.38 us -> 3.12 us  [home_base(): lax.ppermute(p, both, [(2 * a + a // 2, 2 * h + a // 2) for a, h in back(...]
    pallas_call x8, Pallas kernels: 23.4 us -> 21.1 us  [the longest x3 10.1 us: stage(): pl.pallas_call(functools.partial(stage_kernel, len(xs), bool(before)), in...]
  transfers between devices with their start and end apart: 18 -> 19, of which waited for: 6 -> 8; matrix products, arithmetic and copies ran while one was open for 3% -> 0% of each run, Pallas kernels for 15% -> 18%
where the time goes in v2:
time: 109 us; the launch traced here: 108 us
  waiting for transfers between devices  47 us (43%)
  starting transfers between devices  38.4 us (35%)
  Pallas kernels  21.1 us (19%)
  local copies, waits for them, and re-layouts  1.23 us (1%)
    ppermute x10, waiting for transfers between devices, along(): return lax.ppermute(x, 'adapter', pairs)  43.7 us
    ppermute x4, starting transfers between devices, to_half(): lax.ppermute(p, both, [(2 * a + 1 - a // 2, 2 * a + a // 2) for a in rang...  17.6 us
    ppermute x10, starting transfers between devices, along(): return lax.ppermute(x, 'adapter', pairs)  15.4 us
    pallas_call x3, Pallas kernels, stage(): pl.pallas_call(functools.partial(stage_kernel, len(xs), bool(before)), in...  10.1 us
    pallas_call x1, Pallas kernels, first_stage(): pl.pallas_call(first_kernel, in_specs=[VM, VM, pl.BlockSpec(memory_space=...  7.83 us
    ppermute x3, starting transfers between devices, home_base(): lax.ppermute(p, both, [(2 * a + a // 2, 2 * h + a // 2) for a, h in back(...  3.26 us
    ppermute x3, waiting for transfers between devices, home_base(): lax.ppermute(p, both, [(2 * a + a // 2, 2 * h + a // 2) for a, h in back(...  3.12 us
  transfers between devices with their start and end apart: 19, of which 8 were waited for; matrix products, arithmetic and copies ran while one was open for 0% of the time, Pallas kernels for 18%

profile of v2, /device:TPU:10, one launch (start us, length us, event | category | flops | bytes accessed | tf_op | source)
XLA Modules:
  0.0 108.3 jit_solution(1976179362062109500)
XLA Ops:
  0.0 0.4 collective-permute-start.1
  0.5 0.0 copy-start
  0.5 1.2 %copy-done = bf16[2,4096,64]{1,2,0:T(8,128)(2,1)S(1)} copy-done((bf16[2,4096,64]{1,2,0:T(8,128)(2,1)S(1)}, bf16[2,4096,64]{1,2,0:T(8,128)(2,1)}, u32[]{:S(2)}) %copy-start) | copy-done | bytes 1048600
  1.7 0.0 copy-start.2
  1.7 7.8 %shard_map.56 = (bf16[4096,2048]{1,0:T(8,128)(2,1)S(1)}, f32[64,2048]{1,0:T(8,128)S(1)}, bf16[64,2048]{1,0:T(8,128)(2,1)S(1)}, f32[64,128]{1,0:T(8,128)S(1)}) custom-call(bf16[64,4096]{1,0:T(8,128)(2,1)} %x_ref.1, bf16[128,4096]{1,0:T(8,128)(2,1)S(1)} %bitcast.4, bf16[4096,2048]{1,0:T(8,128)(2,1)} %w_ref.1), custom_call_target="tpu_custom_call" | custom-call | flops 1073741824 | bytes 16777216 | tf_op jit(solution)/shard_map/pallas_call | solution.py:128
  9.5 4.6 %collective-permute-start.5 = (bf16[64,4096]{1,0:T(8,128)(2,1)}, bf16[64,4096]{1,0:T(8,128)(2,1)S(1)}, u32[]{:S(2)}, u32[]{:S(2)}) collective-permute-start(bf16[64,4096]{1,0:T(8,128)(2,1)} %x_ref.1), channel_id=1, source_target_pairs={{4,8},{8,4},{5,9},{9,5},{6,10},{10,6},{7,11},{11,7},{20,24},{24,20... | collective-permute-start | bytes 1572872 | tf_op jit(solution)/shard_map/ppermute | solution.py:256
  14.1 0.6 collective-permute-done.1.refs_0_
  14.8 1.7 %collective-permute-start.4 = (bf16[64,4096]{1,0:T(8,128)(2,1)S(1)}, bf16[64,4096]{1,0:T(8,128)(2,1)S(1)}, u32[]{:S(2)}, u32[]{:S(2)}) collective-permute-start(bf16[64,4096]{1,0:T(8,128)(2,1)S(1)} %collective-permute-done.1.refs_0_), channel_id=1, source_target_pairs={{4,0},{8,12},{5,1},{9,13},{6,2},{10,14},{7,3},{11,15},{20,16},{24,... | collective-permute-start | bytes 1572872 | tf_op jit(solution)/shard_map/ppermute | solution.py:256
  16.5 1.3 %collective-permute-start.8 = (bf16[64,4096]{1,0:T(8,128)(2,1)}, bf16[64,4096]{1,0:T(8,128)(2,1)S(1)}, u32[]{:S(2)}, u32[]{:S(2)}) collective-permute-start(bf16[64,4096]{1,0:T(8,128)(2,1)} %x_ref.1), channel_id=1, source_target_pairs={{0,4},{12,8},{8,0},{4,12},{1,5},{13,9},{9,1},{5,13},{2,6},{14,10},... | collective-permute-start | bytes 1572872 | tf_op jit(solution)/shard_map/ppermute | solution.py:256
  17.8 3.4 %shard_map.57 = (f32[64,2048]{1,0:T(8,128)S(1)}, bf16[64,2048]{1,0:T(8,128)(2,1)S(1)}, f32[128,128]{1,0:T(8,128)S(1)}) custom-call(bf16[64,4096]{1,0:T(8,128)(2,1)S(1)} %collective-permute-done.1.refs_0_, bf16[4096,2048]{1,0:T(8,128)(2,1)S(1)} %get-tuple-element.30.refs_1_.refs_2_, bf16[128,4096]{1,0:T(8,128)(2,1)S(1)} %bitcast.5, ...), custom_call_target="tpu_custom_call" | custom-call | flops 1073741824 | bytes 16777216 | tf_op jit(solution)/shard_map/pallas_call | solution.py:171
  21.2 2.5 %collective-permute-start.2 = (bf16[64,2048]{1,0:T(8,128)(2,1)S(1)}, bf16[64,2048]{1,0:T(8,128)(2,1)S(1)}, u32[]{:S(2)}, u32[]{:S(2)}) collective-permute-start(bf16[64,2048]{1,0:T(8,128)(2,1)S(1)} %get-tuple-element.34), channel_id=1, source_target_pairs={{2,0},{6,4},{8,10},{12,14},{3,1},{7,5},{9,11},{13,15},{18,16},{22,... | collective-permute-start | bytes 786440 | tf_op jit(solution)/shard_map/ppermute | solution.py:296
  23.6 0.0 copy-done.2
  23.6 0.2 shard_map.55
  23.8 0.8 collective-permute-start.11
  24.6 2.5 %collective-permute-done.5.refs_1_ = bf16[64,4096]{1,0:T(8,128)(2,1)S(1)} collective-permute-done((bf16[64,4096]{1,0:T(8,128)(2,1)}, bf16[64,4096]{1,0:T(8,128)(2,1)S(1)}, u32[]{:S(2)}, u32[]{:S(2)}) %collective-permute-start.5) | collective-permute-done | bytes 524320 | tf_op jit(solution)/shard_map/ppermute | solution.py:256
  27.1 0.0 collective-permute-start.16
  27.1 10.9 %collective-permute-done.4.refs_0_ = bf16[64,4096]{1,0:T(8,128)(2,1)S(1)} collective-permute-done((bf16[64,4096]{1,0:T(8,128)(2,1)S(1)}, bf16[64,4096]{1,0:T(8,128)(2,1)S(1)}, u32[]{:S(2)}, u32[]{:S(2)}) %collective-permute-start.4) | collective-permute-done | bytes 524320 | tf_op jit(solution)/shard_map/ppermute | solution.py:256
  38.0 0.0 copy-start.1
  38.0 3.4 %shard_map.58 = (f32[64,2048]{1,0:T(8,128)S(1)}, bf16[64,2048]{1,0:T(8,128)(2,1)S(1)}, f32[192,128]{1,0:T(8,128)S(1)}) custom-call(bf16[64,4096]{1,0:T(8,128)(2,1)S(1)} %collective-permute-done.4.refs_0_, bf16[64,4096]{1,0:T(8,128)(2,1)S(1)} %collective-permute-done.5.refs_1_, bf16[4096,2048]{1,0:T(8,128)(2,1)S(1)} %get-tuple-element.30.refs_1_.refs_2_, ...), custom_call_target="tpu_custom_call" | custom-call | flops 1073741824 | bytes 16777216 | tf_op jit(solution)/shard_map/pallas_call | solution.py:171
  41.4 2.6 %collective-permute-start.6 = (bf16[64,2048]{1,0:T(8,128)(2,1)S(1)}, bf16[64,2048]{1,0:T(8,128)(2,1)S(1)}, u32[]{:S(2)}, u32[]{:S(2)}) collective-permute-start(bf16[64,2048]{1,0:T(8,128)(2,1)S(1)} %get-tuple-element.38), channel_id=1, source_target_pairs={{2,0},{6,4},{8,10},{12,14},{3,1},{7,5},{9,11},{13,15},{18,16},{22,... | collective-permute-start | bytes 786440 | tf_op jit(solution)/shard_map/ppermute | solution.py:296
  44.0 0.0 collective-permute-done.8.refs_0_
  44.0 0.1 collective-permute-start.13
  44.1 3.4 %shard_map.59 = (f32[64,2048]{1,0:T(8,128)S(1)}, bf16[64,2048]{1,0:T(8,128)(2,1)S(1)}, f32[64,128]{1,0:T(8,128)S(1)}) custom-call(bf16[64,4096]{1,0:T(8,128)(2,1)S(1)} %collective-permute-done.8.refs_0_, bf16[4096,2048]{1,0:T(8,128)(2,1)S(1)} %get-tuple-element.30.refs_1_.refs_2_, bf16[128,4096]{1,0:T(8,128)(2,1)S(1)} %bitcast.7), custom_call_target="tpu_custom_call" | custom-call | flops 1073741824 | bytes 16777216 | tf_op jit(solution)/shard_map/pallas_call | solution.py:171
  47.5 0.0 collective-permute-done.2
  47.5 2.1 %collective-permute-start.17 = (f32[64,128]{1,0:T(8,128)S(1)}, f32[64,128]{1,0:T(8,128)S(1)}, u32[]{:S(2)}, u32[]{:S(2)}) collective-permute-start(f32[64,128]{1,0:T(8,128)S(1)} %get-tuple-element.48.refs_1_), channel_id=1, source_target_pairs={{0,2},{2,0},{1,3},{3,1},{4,6},{6,4},{5,7},{7,5},{8,10},{10,8},{9,1... | collective-permute-start | bytes 98312 | tf_op jit(solution)/shard_map/ppermute | solution.py:306
  49.5 0.1 add_convert_fusion.2
  49.6 0.0 collective-permute-done.16.refs_0_
  49.6 2.0 %collective-permute-start.12 = (s32[1,64]{1,0:T(1,128)S(1)}, s32[1,64]{1,0:T(1,128)S(1)}, u32[]{:S(2)}, u32[]{:S(2)}) collective-permute-start(s32[1,64]{1,0:T(1,128)S(1)} %get-tuple-element.43.refs_0_), channel_id=1, source_target_pairs={{12,0},{8,4},{4,8},{0,12},{13,1},{9,5},{5,9},{1,13},{14,2},{10,6},... | collective-permute-start | bytes 776 | tf_op jit(solution)/shard_map/ppermute | solution.py:256
  51.7 0.2 collective-permute-done.17.refs_2_
  51.9 4.4 %collective-permute-start = (bf16[64,2048]{1,0:T(8,128)(2,1)S(1)}, bf16[64,2048]{1,0:T(8,128)(2,1)S(1)}, u32[]{:S(2)}, u32[]{:S(2)}) collective-permute-start(bf16[64,2048]{1,0:T(8,128)(2,1)S(1)} %get-tuple-element.29), channel_id=1, source_target_pairs={{2,0},{6,4},{8,10},{12,14},{3,1},{7,5},{9,11},{13,15},{18,16},{22,... | collective-permute-start | bytes 786440 | tf_op jit(solution)/shard_map/ppermute | solution.py:296
  56.3 0.0 copy-done.1
  56.3 0.4 shard_map.61
  56.7 0.0 collective-permute-done.11.refs_1_
  56.7 0.7 collective-permute-start.3
  57.4 0.0 collective-permute-done.12.refs_2_
  57.4 8.1 %collective-permute-start.9 = (bf16[64,2048]{1,0:T(8,128)(2,1)S(1)}, bf16[64,2048]{1,0:T(8,128)(2,1)S(1)}, u32[]{:S(2)}, u32[]{:S(2)}) collective-permute-start(bf16[64,2048]{1,0:T(8,128)(2,1)S(1)} %get-tuple-element.42), channel_id=1, source_target_pairs={{2,0},{6,4},{8,10},{12,14},{3,1},{7,5},{9,11},{13,15},{18,16},{22,... | collective-permute-start | bytes 786440 | tf_op jit(solution)/shard_map/ppermute | solution.py:296
  65.5 0.0 collective-permute-done.13.refs_4_
  65.5 0.1 collective-permute-start.18
  65.6 0.9 shard_map.60
  66.5 0.0 collective-permute-done.6
  66.5 3.0 %collective-permute-start.14 = (bf16[32,4096]{1,0:T(8,128)(2,1)S(1)}, bf16[32,4096]{1,0:T(8,128)(2,1)S(1)}, u32[]{:S(2)}, u32[]{:S(2)}) collective-permute-start(bf16[32,4096]{1,0:T(8,128)(2,1)S(1)} %get-tuple-element.46), channel_id=1, source_target_pairs={{0,4},{4,12},{8,0},{12,8},{1,5},{5,13},{9,1},{13,9},{2,6},{6,14},{... | collective-permute-start | bytes 786440 | tf_op jit(solution)/shard_map/ppermute | solution.py:256
  69.5 0.0 collective-permute-done.9
  69.5 1.5 %collective-permute-start.15 = (bf16[32,4096]{1,0:T(8,128)(2,1)S(1)}, bf16[32,4096]{1,0:T(8,128)(2,1)S(1)}, u32[]{:S(2)}, u32[]{:S(2)}) collective-permute-start(bf16[32,4096]{1,0:T(8,128)(2,1)S(1)} %get-tuple-element.47), channel_id=1, source_target_pairs={{0,12},{4,8},{8,4},{12,0},{1,13},{5,9},{9,5},{13,1},{2,14},{6,10},... | collective-permute-start | bytes 786440 | tf_op jit(solution)/shard_map/ppermute | solution.py:256
  71.0 0.1 add_convert_fusion
  71.1 0.0 collective-permute-done.own16_ref
  71.1 1.3 %collective-permute-start.7 = (bf16[64,2048]{1,0:T(8,128)(2,1)S(1)}, bf16[64,2048]{1,0:T(8,128)(2,1)S(1)}, u32[]{:S(2)}, u32[]{:S(2)}) collective-permute-start(bf16[64,2048]{1,0:T(8,128)(2,1)S(1)} %add_convert_fusion.1), channel_id=1, source_target_pairs={{0,12},{4,8},{10,6},{14,2},{1,13},{5,9},{11,7},{15,3},{16,28},{20,... | collective-permute-start | bytes 786440 | tf_op jit(solution)/shard_map/ppermute | solution.py:301
  72.4 0.0 collective-permute-done.3.b1
  72.4 1.3 %collective-permute-start.10 = (bf16[64,2048]{1,0:T(8,128)(2,1)S(1)}, bf16[64,2048]{1,0:T(8,128)(2,1)S(1)}, u32[]{:S(2)}, u32[]{:S(2)}) collective-permute-start(bf16[64,2048]{1,0:T(8,128)(2,1)S(1)} %add_convert_fusion), channel_id=1, source_target_pairs={{0,8},{4,0},{10,14},{14,6},{1,9},{5,1},{11,15},{15,7},{16,24},{20,... | collective-permute-start | bytes 786440 | tf_op jit(solution)/shard_map/ppermute | solution.py:301
  73.7 2.1 %collective-permute-done.18.d3 = bf16[32,4096]{1,0:T(8,128)(2,1)S(1)} collective-permute-done((bf16[32,4096]{1,0:T(8,128)(2,1)S(1)}, bf16[32,4096]{1,0:T(8,128)(2,1)S(1)}, u32[]{:S(2)}, u32[]{:S(2)}) %collective-permute-start.18) | collective-permute-done | bytes 262176 | tf_op jit(solution)/shard_map/ppermute | solution.py:256
  75.8 5.5 %collective-permute-done.14.d1 = bf16[32,4096]{1,0:T(8,128)(2,1)S(1)} collective-permute-done((bf16[32,4096]{1,0:T(8,128)(2,1)S(1)}, bf16[32,4096]{1,0:T(8,128)(2,1)S(1)}, u32[]{:S(2)}, u32[]{:S(2)}) %collective-permute-start.14) | collective-permute-done | bytes 262176 | tf_op jit(solution)/shard_map/ppermute | solution.py:256
  81.4 22.0 %collective-permute-done.15.d2 = bf16[32,4096]{1,0:T(8,128)(2,1)S(1)} collective-permute-done((bf16[32,4096]{1,0:T(8,128)(2,1)S(1)}, bf16[32,4096]{1,0:T(8,128)(2,1)S(1)}, u32[]{:S(2)}, u32[]{:S(2)}) %collective-permute-start.15) | collective-permute-done | bytes 262176 | tf_op jit(solution)/shard_map/ppermute | solution.py:256
  103.4 3.1 %collective-permute-done.7.b2 = bf16[64,2048]{1,0:T(8,128)(2,1)S(1)} collective-permute-done((bf16[64,2048]{1,0:T(8,128)(2,1)S(1)}, bf16[64,2048]{1,0:T(8,128)(2,1)S(1)}, u32[]{:S(2)}, u32[]{:S(2)}) %collective-permute-start.7) | collective-permute-done | bytes 262176 | tf_op jit(solution)/shard_map/ppermute | solution.py:301
  106.5 0.0 collective-permute-done.10.b3
  106.5 1.8 %shard_map.62 = bf16[64,4096]{1,0:T(8,128)(2,1)} custom-call(s32[64,1]{1,0:T(8,128)S(1)} %get-tuple-element.27.slot_ref, f32[64,2048]{1,0:T(8,128)S(1)} %get-tuple-element.28.own32_ref, bf16[64,2048]{1,0:T(8,128)(2,1)S(1)} %collective-permute-done.own16_ref, bf16[64,2048]{1,0:T(8,128)(2,1)S(1)} %collective-permute-done.3.b1, ...), custom_call_target="tpu_custom_call" | custom-call | tf_op jit(solution)/shard_map/pallas_call | solution.py:318
  (1 shorter events, 0.0 us)
Async XLA Ops:
  0.0 14.8 %collective-permute-start.1 = (bf16[64,4096]{1,0:T(8,128)(2,1)}, bf16[64,4096]{1,0:T(8,128)(2,1)S(1)}, u32[]{:S(2)}, u32[]{:S(2)}) collective-permute-start(bf16[64,4096]{1,0:T(8,128)(2,1)} %x_ref.1), channel_id=1, source_target_pairs={{0,8},{12,4},{4,0},{8,12},{1,9},{13,5},{5,1},{9,13},{2,10},{14,6},... | collective-permute-start | bytes 1572872 | tf_op jit(solution)/shard_map/ppermute | solution.py:256
  0.5 1.2 %copy-start = (bf16[2,4096,64]{1,2,0:T(8,128)(2,1)S(1)}, bf16[2,4096,64]{1,2,0:T(8,128)(2,1)}, u32[]{:S(2)}) copy-start(bf16[2,4096,64]{1,2,0:T(8,128)(2,1)} %param.8) | copy-start | bytes 3145732
  1.7 22.0 %copy-start.2 = (s32[64,1]{0,1:T(1,128)S(1)}, s32[64,1]{0,1:T(1,128)}, u32[]{:S(2)}) copy-start(s32[64,1]{0,1:T(1,128)} %param.6) | copy-start | bytes 772
  9.5 17.6 %collective-permute-start.5 = (bf16[64,4096]{1,0:T(8,128)(2,1)}, bf16[64,4096]{1,0:T(8,128)(2,1)S(1)}, u32[]{:S(2)}, u32[]{:S(2)}) collective-permute-start(bf16[64,4096]{1,0:T(8,128)(2,1)} %x_ref.1), channel_id=1, source_target_pairs={{4,8},{8,4},{5,9},{9,5},{6,10},{10,6},{7,11},{11,7},{20,24},{24,20... | collective-permute-start | bytes 1572872 | tf_op jit(solution)/shard_map/ppermute | solution.py:256
  14.8 23.2 %collective-permute-start.4 = (bf16[64,4096]{1,0:T(8,128)(2,1)S(1)}, bf16[64,4096]{1,0:T(8,128)(2,1)S(1)}, u32[]{:S(2)}, u32[]{:S(2)}) collective-permute-start(bf16[64,4096]{1,0:T(8,128)(2,1)S(1)} %collective-permute-done.1.refs_0_), channel_id=1, source_target_pairs={{4,0},{8,12},{5,1},{9,13},{6,2},{10,14},{7,3},{11,15},{20,16},{24,... | collective-permute-start | bytes 1572872 | tf_op jit(solution)/shard_map/ppermute | solution.py:256
  16.5 27.5 %collective-permute-start.8 = (bf16[64,4096]{1,0:T(8,128)(2,1)}, bf16[64,4096]{1,0:T(8,128)(2,1)S(1)}, u32[]{:S(2)}, u32[]{:S(2)}) collective-permute-start(bf16[64,4096]{1,0:T(8,128)(2,1)} %x_ref.1), channel_id=1, source_target_pairs={{0,4},{12,8},{8,0},{4,12},{1,5},{13,9},{9,1},{5,13},{2,6},{14,10},... | collective-permute-start | bytes 1572872 | tf_op jit(solution)/shard_map/ppermute | solution.py:256
  21.2 26.3 %collective-permute-start.2 = (bf16[64,2048]{1,0:T(8,128)(2,1)S(1)}, bf16[64,2048]{1,0:T(8,128)(2,1)S(1)}, u32[]{:S(2)}, u32[]{:S(2)}) collective-permute-start(bf16[64,2048]{1,0:T(8,128)(2,1)S(1)} %get-tuple-element.34), channel_id=1, source_target_pairs={{2,0},{6,4},{8,10},{12,14},{3,1},{7,5},{9,11},{13,15},{18,16},{22,... | collective-permute-start | bytes 786440 | tf_op jit(solution)/shard_map/ppermute | solution.py:296
  23.8 32.8 %collective-permute-start.11 = (s32[1,64]{1,0:T(1,128)S(1)}, s32[1,64]{1,0:T(1,128)S(1)}, u32[]{:S(2)}, u32[]{:S(2)}) collective-permute-start(s32[1,64]{1,0:T(1,128)S(1)} %get-tuple-element.43.refs_0_), channel_id=1, source_target_pairs={{4,0},{12,4},{0,8},{8,12},{5,1},{13,5},{1,9},{9,13},{6,2},{14,6},{... | collective-permute-start | bytes 776 | tf_op jit(solution)/shard_map/ppermute | solution.py:256
  27.1 22.5 %collective-permute-start.16 = (s32[1,64]{1,0:T(1,128)S(1)}, s32[1,64]{1,0:T(1,128)S(1)}, u32[]{:S(2)}, u32[]{:S(2)}) collective-permute-start(s32[1,64]{1,0:T(1,128)S(1)} %get-tuple-element.43.refs_0_), channel_id=1, source_target_pairs={{8,0},{0,4},{12,8},{4,12},{9,1},{1,5},{13,9},{5,13},{10,2},{2,6},{... | collective-permute-start | bytes 776 | tf_op jit(solution)/shard_map/ppermute | solution.py:256
  38.0 18.3 %copy-start.1 = (bf16[2,64,4096]{2,1,0:T(8,128)(2,1)S(1)}, bf16[2,64,4096]{2,1,0:T(8,128)(2,1)}, u32[]{:S(2)}) copy-start(bf16[2,64,4096]{2,1,0:T(8,128)(2,1)} %e_ref.3) | copy-start | bytes 3145732
  41.4 25.1 %collective-permute-start.6 = (bf16[64,2048]{1,0:T(8,128)(2,1)S(1)}, bf16[64,2048]{1,0:T(8,128)(2,1)S(1)}, u32[]{:S(2)}, u32[]{:S(2)}) collective-permute-start(bf16[64,2048]{1,0:T(8,128)(2,1)S(1)} %get-tuple-element.38), channel_id=1, source_target_pairs={{2,0},{6,4},{8,10},{12,14},{3,1},{7,5},{9,11},{13,15},{18,16},{22,... | collective-permute-start | bytes 786440 | tf_op jit(solution)/shard_map/ppermute | solution.py:296
  44.0 21.5 %collective-permute-start.13 = (f32[192,128]{1,0:T(8,128)S(1)}, f32[192,128]{1,0:T(8,128)S(1)}, u32[]{:S(2)}, u32[]{:S(2)}) collective-permute-start(f32[192,128]{1,0:T(8,128)S(1)} %get-tuple-element.44.refs_3_), channel_id=1, source_target_pairs={{0,2},{2,0},{1,3},{3,1},{4,6},{6,4},{5,7},{7,5},{8,10},{10,8},{9,1... | collective-permute-start | bytes 294920 | tf_op jit(solution)/shard_map/ppermute | solution.py:306
  47.5 4.4 %collective-permute-start.17 = (f32[64,128]{1,0:T(8,128)S(1)}, f32[64,128]{1,0:T(8,128)S(1)}, u32[]{:S(2)}, u32[]{:S(2)}) collective-permute-start(f32[64,128]{1,0:T(8,128)S(1)} %get-tuple-element.48.refs_1_), channel_id=1, source_target_pairs={{0,2},{2,0},{1,3},{3,1},{4,6},{6,4},{5,7},{7,5},{8,10},{10,8},{9,1... | collective-permute-start | bytes 98312 | tf_op jit(solution)/shard_map/ppermute | solution.py:306
  49.6 7.8 %collective-permute-start.12 = (s32[1,64]{1,0:T(1,128)S(1)}, s32[1,64]{1,0:T(1,128)S(1)}, u32[]{:S(2)}, u32[]{:S(2)}) collective-permute-start(s32[1,64]{1,0:T(1,128)S(1)} %get-tuple-element.43.refs_0_), channel_id=1, source_target_pairs={{12,0},{8,4},{4,8},{0,12},{13,1},{9,5},{5,9},{1,13},{14,2},{10,6},... | collective-permute-start | bytes 776 | tf_op jit(solution)/shard_map/ppermute | solution.py:256
  51.9 19.2 %collective-permute-start = (bf16[64,2048]{1,0:T(8,128)(2,1)S(1)}, bf16[64,2048]{1,0:T(8,128)(2,1)S(1)}, u32[]{:S(2)}, u32[]{:S(2)}) collective-permute-start(bf16[64,2048]{1,0:T(8,128)(2,1)S(1)} %get-tuple-element.29), channel_id=1, source_target_pairs={{2,0},{6,4},{8,10},{12,14},{3,1},{7,5},{9,11},{13,15},{18,16},{22,... | collective-permute-start | bytes 786440 | tf_op jit(solution)/shard_map/ppermute | solution.py:296
  56.7 15.7 %collective-permute-start.3 = (bf16[64,2048]{1,0:T(8,128)(2,1)S(1)}, bf16[64,2048]{1,0:T(8,128)(2,1)S(1)}, u32[]{:S(2)}, u32[]{:S(2)}) collective-permute-start(bf16[64,2048]{1,0:T(8,128)(2,1)S(1)} %add_convert_fusion.2), channel_id=1, source_target_pairs={{0,4},{4,12},{10,2},{14,10},{1,5},{5,13},{11,3},{15,11},{16,20},{2... | collective-permute-start | bytes 786440 | tf_op jit(solution)/shard_map/ppermute | solution.py:301
  57.4 12.1 %collective-permute-start.9 = (bf16[64,2048]{1,0:T(8,128)(2,1)S(1)}, bf16[64,2048]{1,0:T(8,128)(2,1)S(1)}, u32[]{:S(2)}, u32[]{:S(2)}) collective-permute-start(bf16[64,2048]{1,0:T(8,128)(2,1)S(1)} %get-tuple-element.42), channel_id=1, source_target_pairs={{2,0},{6,4},{8,10},{12,14},{3,1},{7,5},{9,11},{13,15},{18,16},{22,... | collective-permute-start | bytes 786440 | tf_op jit(solution)/shard_map/ppermute | solution.py:296
  65.5 10.3 %collective-permute-start.18 = (bf16[32,4096]{1,0:T(8,128)(2,1)S(1)}, bf16[32,4096]{1,0:T(8,128)(2,1)S(1)}, u32[]{:S(2)}, u32[]{:S(2)}) collective-permute-start(bf16[32,4096]{1,0:T(8,128)(2,1)S(1)} %shard_map.61), channel_id=1, source_target_pairs={{0,8},{4,0},{8,12},{12,4},{1,9},{5,1},{9,13},{13,5},{2,10},{6,2},{... | collective-permute-start | bytes 786440 | tf_op jit(solution)/shard_map/ppermute | solution.py:256
  66.5 14.8 %collective-permute-start.14 = (bf16[32,4096]{1,0:T(8,128)(2,1)S(1)}, bf16[32,4096]{1,0:T(8,128)(2,1)S(1)}, u32[]{:S(2)}, u32[]{:S(2)}) collective-permute-start(bf16[32,4096]{1,0:T(8,128)(2,1)S(1)} %get-tuple-element.46), channel_id=1, source_target_pairs={{0,4},{4,12},{8,0},{12,8},{1,5},{5,13},{9,1},{13,9},{2,6},{6,14},{... | collective-permute-start | bytes 786440 | tf_op jit(solution)/shard_map/ppermute | solution.py:256
  69.5 33.8 %collective-permute-start.15 = (bf16[32,4096]{1,0:T(8,128)(2,1)S(1)}, bf16[32,4096]{1,0:T(8,128)(2,1)S(1)}, u32[]{:S(2)}, u32[]{:S(2)}) collective-permute-start(bf16[32,4096]{1,0:T(8,128)(2,1)S(1)} %get-tuple-element.47), channel_id=1, source_target_pairs={{0,12},{4,8},{8,4},{12,0},{1,13},{5,9},{9,5},{13,1},{2,14},{6,10},... | collective-permute-start | bytes 786440 | tf_op jit(solution)/shard_map/ppermute | solution.py:256
  71.1 35.4 %collective-permute-start.7 = (bf16[64,2048]{1,0:T(8,128)(2,1)S(1)}, bf16[64,2048]{1,0:T(8,128)(2,1)S(1)}, u32[]{:S(2)}, u32[]{:S(2)}) collective-permute-start(bf16[64,2048]{1,0:T(8,128)(2,1)S(1)} %add_convert_fusion.1), channel_id=1, source_target_pairs={{0,12},{4,8},{10,6},{14,2},{1,13},{5,9},{11,7},{15,3},{16,28},{20,... | collective-permute-start | bytes 786440 | tf_op jit(solution)/shard_map/ppermute | solution.py:301
  72.4 34.1 %collective-permute-start.10 = (bf16[64,2048]{1,0:T(8,128)(2,1)S(1)}, bf16[64,2048]{1,0:T(8,128)(2,1)S(1)}, u32[]{:S(2)}, u32[]{:S(2)}) collective-permute-start(bf16[64,2048]{1,0:T(8,128)(2,1)S(1)} %add_convert_fusion), channel_id=1, source_target_pairs={{0,8},{4,0},{10,14},{14,6},{1,9},{5,1},{11,15},{15,7},{16,24},{20,... | collective-permute-start | bytes 786440 | tf_op jit(solution)/shard_map/ppermute | solution.py:301

commit v3 on v0

--- a/solution.py
+++ b/solution.py
@@ -1,9 +1,14 @@
+import functools
+
 import jax
 import jax.numpy as jnp
 from jax import lax
+from jax.experimental import pallas as pl
+from jax.experimental.pallas import tpu as pltpu
 from jax.sharding import PartitionSpec as P
 
 adapter_scale_factor = 0.5
+VMEM_LIMIT = 8 * 1024 * 1024
 
 
 def ranks_of(block_ids):
@@ -15,7 +20,11 @@
     return jnp.sum(jnp.logical_and(same, earlier).astype(jnp.int32), axis=-1)
 
 
-def body(activations, adapter_ids, base_weight, shrink_weight, expand_weight):
+def most_rows_of(tok_rows, adapters):
+    return max(2, 2 * tok_rows // adapters)
+
+
+def body_any(activations, adapter_ids, base_weight, shrink_weight, expand_weight):
     row_ids = adapter_ids[:, 0]
     tok_rows = activations.shape[0]
     feat_part = activations.shape[1]
@@ -23,7 +32,7 @@
     out_cols = base_weight.shape[1]
     n_adapt = lax.axis_size("adapter")
     local_count = shrink_weight.shape[0]
-    most_rows = max(2, 2 * tok_rows // (local_count * n_adapt))
+    most_rows = most_rows_of(tok_rows, local_count * n_adapt)
     resident_slot_list = local_count * most_rows
     all_slots = n_adapt * resident_slot_list
     home_slot = row_ids * most_rows + ranks_of(row_ids)
@@ -68,6 +77,318 @@
     return (base + delta).astype(jnp.bfloat16)
 
 
+VM = pl.BlockSpec(memory_space=pltpu.VMEM)
+HB = pl.BlockSpec(memory_space=pl.ANY)
+F32 = jnp.float32
+BF16 = jnp.bfloat16
+LANES = 128
+PARAMS = pltpu.CompilerParams(vmem_limit_bytes=VMEM_LIMIT)
+
+
+def hbm(x):
+    return pltpu.with_memory_space_constraint(x, pltpu.HBM)
+
+
+def vmem(x):
+    return pltpu.with_memory_space_constraint(x, pltpu.VMEM)
+
+
+def cost(flops, nbytes):
+    return pl.CostEstimate(flops=flops, bytes_accessed=nbytes, transcendentals=0)
+
+
+def pack_kernel(most, ids_ref, x_ref, packed_ref, col_ref, sem):
+    depth = x_ref.shape[1]
+    copy = pltpu.make_async_copy(x_ref, packed_ref.at[:, :depth], sem)
+    copy.start()
+    ids = ids_ref[...]
+    count = ids.shape[1]
+    i = lax.broadcasted_iota(jnp.int32, (count, count), 0)
+    j = lax.broadcasted_iota(jnp.int32, (count, count), 1)
+    wide = jnp.broadcast_to(ids, (count, count))
+    tall = jnp.sum(jnp.where(i == j, wide, 0), axis=1, keepdims=True)
+    col = tall * most + jnp.sum(jnp.where((wide == tall) & (j < i), 1, 0), axis=1, keepdims=True)
+    col_ref[...] = col
+    packed_ref[:, depth:] = jnp.broadcast_to(col.astype(F32), (count, LANES)).astype(BF16)
+    copy.wait()
+
+
+def shrink(x_ref_tail, sums, most, local, rank):
+    rows = sums.shape[0]
+    slot = x_ref_tail[:, 0:1].astype(F32)
+    i = lax.broadcasted_iota(jnp.int32, (rows, rows), 0)
+    j = lax.broadcasted_iota(jnp.int32, (rows, rows), 1)
+    line = jnp.sum(jnp.where(i == j, slot, 0.0), axis=0, keepdims=True).astype(jnp.int32)
+    spots = local * most
+    first = lax.axis_index("adapter") * spots
+    want = lax.broadcasted_iota(jnp.int32, (spots, rows), 0) + first
+    chosen = jnp.dot(
+        (want == line).astype(F32),
+        sums,
+        preferred_element_type=F32,
+        precision=lax.Precision.HIGHEST,
+    )
+    return [
+        chosen[k * most : (k + 1) * most, k * rank : (k + 1) * rank] for k in range(local)
+    ]
+
+
+def put_shrunk(parts, top, send_ref, own_ref, most, rank):
+    rows = own_ref.shape[0]
+    wide = send_ref.shape[1]
+    at = wide - LANES
+    for k, part in enumerate(parts):
+        lines = slice(k * most, (k + 1) * most)
+        own_ref[lines, :] = part
+        high = part.astype(BF16)
+        low = (part - high.astype(F32)).astype(BF16)
+        send_ref[top + k * most : top + (k + 1) * most, at:] = jnp.concatenate([high, low], axis=1)
+    send_ref[top + rows :, at:] = jnp.zeros((send_ref.shape[0] - top - rows, LANES), BF16)
+
+
+def put_base(total, top, send_ref, keep_ref):
+    rows, width = keep_ref.shape
+    half = lax.axis_index("tensor")
+    for c in range(2):
+
+        @pl.when(half == c)
+        def _():
+            keep_ref[...] = total[:, c * width : (c + 1) * width]
+            send_ref[top : top + rows, :width] = total[
+                :, (1 - c) * width : (2 - c) * width
+            ].astype(BF16)
+
+
+def first_kernel(
+    dims, x_ref, s_hbm, w_hbm, w_ref, s_ref, send_ref, keep_ref, own_ref, total, sems
+):
+    most, local, rank = dims
+    parts = sems.shape[0] - 1
+    step = w_hbm.shape[0] // parts
+    copies = []
+    for i in range(parts):
+        lines = slice(i * step, (i + 1) * step)
+        copies.append(
+            pltpu.make_async_copy(w_hbm.at[lines, :], w_ref.at[lines, :], sems.at[i])
+        )
+        copies[i].start()
+    down = pltpu.make_async_copy(s_hbm, s_ref, sems.at[parts])
+    down.start()
+    for i in range(parts):
+        copies[i].wait()
+        lines = slice(i * step, (i + 1) * step)
+        part = jnp.dot(x_ref[:, lines], w_ref[lines, :], preferred_element_type=F32)
+        total[...] = part if i == 0 else total[...] + part
+    down.wait()
+    depth = w_ref.shape[0]
+    sums = lax.dot_general(
+        x_ref[:, :depth], s_ref[...], (((1,), (1,)), ((), ())), preferred_element_type=F32
+    )
+    chosen = shrink(x_ref[:, depth:], sums, most, local, rank)
+    put_shrunk(chosen, 0, send_ref, own_ref, most, rank)
+    put_base(total, 0, send_ref, keep_ref)
+
+
+def stage_kernel(dims, n_in, keep_first, *refs):
+    most, local, rank = dims
+    x_refs, (w_ref, s_ref) = refs[:n_in], refs[n_in : n_in + 2]
+    before, (send_ref, keep_ref, own_ref, total) = refs[n_in + 2 : -4], refs[-4:]
+    depth = w_ref.shape[0]
+    x, tail = x_refs[0][:, :depth], x_refs[0][:, depth:]
+    for other in x_refs[1:]:
+        x, tail = x + other[:, :depth], tail + other[:, depth:]
+    top = 0
+    if keep_first:
+        top = before[0].shape[0]
+        send_ref[:top, :] = before[0][...]
+    sums = lax.dot_general(
+        x, s_ref[...], (((1,), (1,)), ((), ())), preferred_element_type=F32
+    )
+    for j in range(0, w_ref.shape[1], 256):
+        cols = slice(j, j + 256)
+        total[:, cols] = jnp.dot(x, w_ref[:, cols], preferred_element_type=F32)
+    put_shrunk(shrink(tail, sums, most, local, rank), top, send_ref, own_ref, most, rank)
+    put_base(total, top, send_ref, keep_ref)
+
+
+def stage_shapes(rows, sent_rows, cols, spots, rank):
+    return [
+        pltpu.VMEM((sent_rows, cols // 2 + LANES), BF16),
+        pltpu.VMEM((rows, cols // 2), F32),
+        pltpu.VMEM((spots, rank), F32),
+    ]
+
+
+def first_stage(dims, x, s_t, w):
+    rows = x.shape[0]
+    depth, cols = w.shape
+    most, local, rank = dims
+    return pl.pallas_call(
+        functools.partial(first_kernel, dims),
+        in_specs=[VM, HB, HB],
+        out_specs=[VM] * 5,
+        out_shape=[pltpu.VMEM(w.shape, BF16), pltpu.VMEM(s_t.shape, BF16)]
+        + stage_shapes(rows, rows, cols, local * most, rank),
+        scratch_shapes=[pltpu.VMEM((rows, cols), F32), pltpu.SemaphoreType.DMA((9,))],
+        compiler_params=PARAMS,
+        cost_estimate=cost(2 * rows * depth * cols, depth * cols * 2),
+    )(vmem(x), hbm(s_t), hbm(w))
+
+
+def stage(dims, xs, w, s_t, before=()):
+    rows = xs[0].shape[0]
+    depth, cols = w.shape
+    most, local, rank = dims
+    sent = rows + sum(b.shape[0] for b in before)
+    return pl.pallas_call(
+        functools.partial(stage_kernel, dims, len(xs), bool(before)),
+        in_specs=[VM] * (len(xs) + 2 + len(before)),
+        out_specs=[VM] * 3,
+        out_shape=stage_shapes(rows, sent, cols, local * most, rank),
+        scratch_shapes=[pltpu.VMEM((rows, cols), F32)],
+        compiler_params=PARAMS,
+        cost_estimate=cost(2 * rows * depth * cols, depth * cols * 2),
+    )(*xs, vmem(w), vmem(s_t), *before)
+
+
+def join_kernel(k, got_ref, e_ref, *refs):
+    ins, outs = refs[: 2 * k], refs[2 * k :]
+    local, rank, _ = e_ref.shape
+    width = got_ref.shape[1] - LANES
+    rows = got_ref.shape[0] // k
+    for i in range(k):
+        keep, own, base, delta = ins[2 * i], ins[2 * i + 1], outs[2 * i], outs[2 * i + 1]
+        lines = slice(i * rows, (i + 1) * rows)
+        spots = own.shape[0]
+        most = spots // local
+        terms = got_ref[i * rows : i * rows + spots, width:].astype(F32)
+        total = (own[...] + terms[:, :rank] + terms[:, rank : 2 * rank]).astype(BF16)
+        base[...] = (keep[...] + got_ref[lines, :width].astype(F32)).astype(BF16)
+        for j in range(local):
+            put = slice(j * most, (j + 1) * most)
+            wide = jnp.dot(total[put], e_ref[j], preferred_element_type=F32)
+            delta[put, :] = (adapter_scale_factor * wide).astype(BF16)
+
+
+def join(got, e, pairs):
+    k = len(pairs)
+    shapes = []
+    for keep, own in pairs:
+        shapes += [
+            pltpu.VMEM(keep.shape, BF16),
+            pltpu.VMEM((own.shape[0], e.shape[2]), BF16),
+        ]
+    return pl.pallas_call(
+        functools.partial(join_kernel, k),
+        in_specs=[VM] * (2 + 2 * k),
+        out_specs=[VM] * (2 * k),
+        out_shape=shapes,
+        compiler_params=PARAMS,
+        cost_estimate=cost(1 << 28, 4 << 20),
+    )(got, e, *[a for pair in pairs for a in pair])
+
+
+def final_kernel(planes, slot_ref, *refs):
+    straight, crossed, d_refs = refs[0:4], refs[4:8], refs[8:12]
+    o_ref, base = refs[12:]
+    rows, width = straight[0].shape
+    me, half = lax.axis_index("adapter"), lax.axis_index("tensor")
+    plane_of = [sum(jnp.where(me == a, p[a], 0) for a in range(4)) for p in planes]
+    spots = d_refs[0].shape[0]
+    slot = slot_ref[...]
+    lane = lax.broadcasted_iota(jnp.int32, (rows, spots), 1)
+    picks = [(slot == lane + plane_of[k] * spots).astype(BF16) for k in range(4)]
+    for q in range(2):
+        for k in range(4):
+
+            @pl.when(plane_of[k] == 2 * half + q)
+            def _():
+                base[2 * q] = straight[k][...]
+                base[2 * q + 1] = crossed[k][...]
+
+    for q in range(2):
+        for c in range(2):
+            cols = slice((2 * q + c) * width, (2 * q + c + 1) * width)
+            term = jnp.where(half == c, base[2 * q].astype(F32), base[2 * q + 1].astype(F32))
+            for pick, d in zip(picks, d_refs):
+                term = term + jnp.dot(pick, d[:, cols], preferred_element_type=F32)
+            o_ref[:, cols] = term.astype(BF16)
+
+
+def body_four(activations, adapter_ids, base_weight, shrink_weight, expand_weight):
+    rows, depth = activations.shape
+    local, _, rank = shrink_weight.shape
+    cols = base_weight.shape[1]
+    most = most_rows_of(rows, local * 4)
+    dims = (most, local, rank)
+    both = ("adapter", "tensor")
+
+    def along(x, pairs):
+        return lax.ppermute(x, "adapter", pairs)
+
+    held = ((1, 3, 0, 2), (3, 2, 1, 0), (2, 0, 3, 1))
+
+    def back(k):
+        return [(a, held[k - 1][a] if k else a) for a in range(4)]
+
+    planes = [list(range(4))]
+    for k in (1, 2, 3):
+        planes.append([held[k - 1].index(h) for h in range(4)])
+
+    packed, slot_col = pl.pallas_call(
+        functools.partial(pack_kernel, most),
+        in_specs=[VM, HB],
+        out_specs=[VM, VM],
+        out_shape=[
+            pltpu.VMEM((rows, depth + LANES), BF16),
+            jax.ShapeDtypeStruct((rows, 1), jnp.int32),
+        ],
+        scratch_shapes=[pltpu.SemaphoreType.DMA],
+        compiler_params=PARAMS,
+    )(adapter_ids.reshape(1, rows), hbm(activations))
+
+    got_a = along(packed, [(0, 2), (3, 1), (1, 0), (2, 3)])
+    s_t = jnp.swapaxes(shrink_weight, 1, 2).reshape(local * rank, -1)
+    w, s_t, send_0, keep_0, own_0 = first_stage(dims, packed, s_t, base_weight)
+    packed, own_0 = lax.optimization_barrier((packed, own_0))
+    got_b = along(packed, [(1, 2), (2, 1)])
+    got_f = along(got_a, [(1, 0), (2, 3)])
+
+    def flip(s):
+        return lax.ppermute(s, "tensor", [(0, 1), (1, 0)])
+
+    def home(base, k):
+        straight = [(2 * a + a // 2, 2 * h + a // 2) for a, h in back(k)]
+        crossed = [(2 * a + 1 - a // 2, 2 * h + a // 2) for a, h in back(k)]
+        return (
+            lax.ppermute(base, both, straight) if k else base,
+            lax.ppermute(base, both, crossed),
+        )
+
+    e = expand_weight
+    send_1, keep_1, own_1 = stage(dims, [got_a], w, s_t, [send_0])
+    packed, send_1 = lax.optimization_barrier((packed, send_1))
+    got_c = along(packed, [(0, 1), (3, 2), (2, 0), (1, 3)])
+    base_0, d_0, base_1, d_1 = join(flip(send_1), e, [(keep_0, own_0), (keep_1, own_1)])
+    got_b, d_1 = lax.optimization_barrier((got_b, d_1))
+    send_2, keep_2, own_2 = stage(dims, [got_f, got_b], w, s_t)
+    base_2, d_2 = join(flip(send_2), e, [(keep_2, own_2)])
+    got_c, keep_2 = lax.optimization_barrier((got_c, keep_2))
+    send_3, keep_3, own_3 = stage(dims, [got_c], w, s_t)
+    base_3, d_3 = join(flip(send_3), e, [(keep_3, own_3)])
+    ways = [home(b, k) for k, b in enumerate((base_0, base_1, base_2, base_3))]
+    d_1, d_2, d_3 = along(d_1, back(1)), along(d_2, back(2)), along(d_3, back(3))
+
+    return pl.pallas_call(
+        functools.partial(final_kernel, planes),
+        in_specs=[VM] * 13,
+        out_specs=VM,
+        out_shape=jax.ShapeDtypeStruct((rows, 2 * cols), BF16),
+        scratch_shapes=[pltpu.VMEM((4, rows, cols // 2), BF16)],
+        compiler_params=PARAMS,
+    )(slot_col, *[u for u, _ in ways], *[v for _, v in ways], d_0, d_1, d_2, d_3)
+
+
 def solution(mesh):
     in_specs = (
         P(("groups", "adapter", "section"), "tensor"),
@@ -77,4 +398,6 @@
         P("adapter", None, "tensor"),
     )
     out_specs = P(("groups", "adapter", "section"), "tensor")
+    four = mesh.shape["adapter"] == 4 and mesh.shape["tensor"] == 2
+    body = body_four if four else body_any
     return jax.shard_map(body, mesh=mesh, in_specs=in_specs, out_specs=out_specs, check_vma=False)

time: 200 us -> 95.5 us (0.48)
  the two profiles are of different devices: /device:TPU:10 before, /device:TPU:2 now
where the time goes in v3:
time: 95.5 us; the launch traced here: 95.2 us
  waiting for transfers between devices  41.5 us (43%)
  starting transfers between devices  31.2 us (33%)
  Pallas kernels  21.7 us (23%)
    ppermute x3, waiting for transfers between devices, home(): lax.ppermute(base, both, straight)  17 us
    ppermute x7, waiting for transfers between devices, along(): return lax.ppermute(x, 'adapter', pairs)  14.7 us
    ppermute x4, starting transfers between devices, home(): lax.ppermute(base, both, crossed)  14 us
    ppermute x7, starting transfers between devices, along(): return lax.ppermute(x, 'adapter', pairs)  11.4 us
    pallas_call x3, Pallas kernels, stage(): pl.pallas_call(functools.partial(stage_kernel, dims, len(xs), bool(before...  10.5 us
    pallas_call x1, Pallas kernels, first_stage(): pl.pallas_call(functools.partial(first_kernel, dims), in_specs=[VM, HB, H...  7.43 us
    ppermute x3, waiting for transfers between devices, flip(): return lax.ppermute(s, 'tensor', [(0, 1), (1, 0)])  6.8 us
    ppermute x3, starting transfers between devices, home(): lax.ppermute(base, both, straight)  3.24 us
  transfers between devices with their start and end apart: 17, of which 6 were waited for; matrix products, arithmetic and copies ran while one was open for 0% of the time, Pallas kernels for 16%

profile of v3, /device:TPU:2, one launch (start us, length us, event | category | flops | bytes accessed | tf_op | source)
XLA Modules:
  0.0 95.2 jit_solution(3357882059367152628)
XLA Ops:
  0.0 0.0 copy-start.1
  0.0 0.7 copy-done.1
  0.7 1.1 %shard_map.55 = (bf16[64,4224]{1,0:T(8,128)(2,1)S(1)}, s32[64,1]{1,0:T(8,128)S(1)}) custom-call(s32[1,64]{1,0:T(1,128)S(1)} %bitcast.4, bf16[64,4096]{1,0:T(8,128)(2,1)} %x_ref.1), custom_call_target="tpu_custom_call" | custom-call | tf_op jit(solution)/shard_map/pallas_call | solution.py:338
  1.7 2.6 %collective-permute-start = (bf16[64,4224]{1,0:T(8,128)(2,1)S(1)}, bf16[64,4224]{1,0:T(8,128)(2,1)S(1)}, u32[]{:S(2)}, u32[]{:S(2)}) collective-permute-start(bf16[64,4224]{1,0:T(8,128)(2,1)S(1)} %get-tuple-element.57.x_ref), channel_id=1, source_target_pairs={{0,8},{12,4},{4,0},{8,12},{1,9},{13,5},{5,1},{9,13},{2,10},{14,6},... | collective-permute-start | bytes 1622024 | tf_op jit(solution)/shard_map/ppermute | solution.py:327
  4.4 0.0 copy-start
  4.4 7.4 %shard_map.56 = (bf16[4096,2048]{1,0:T(8,128)(2,1)S(1)}, bf16[128,4096]{1,0:T(8,128)(2,1)S(1)}, bf16[64,1152]{1,0:T(8,128)(2,1)S(1)}, f32[64,1024]{1,0:T(8,128)S(1)}, f32[32,64]{1,0:T(8,128)S(1)}) custom-call(bf16[64,4224]{1,0:T(8,128)(2,1)S(1)} %get-tuple-element.57.x_ref, bf16[128,4096]{1,0:T(8,128)(2,1)} %bitcast.5, bf16[4096,2048]{1,0:T(8,128)(2,1)} %w_hbm.1), custom_call_target="tpu_custom_call" | custom-call | flops 1073741824 | bytes 16777216 | tf_op jit(solution)/shard_map/pallas_call | solution.py:226
  11.8 0.7 collective-permute-start.4
  12.5 3.4 %collective-permute-done.refs_0_ = bf16[64,4224]{1,0:T(8,128)(2,1)S(1)} collective-permute-done((bf16[64,4224]{1,0:T(8,128)(2,1)S(1)}, bf16[64,4224]{1,0:T(8,128)(2,1)S(1)}, u32[]{:S(2)}, u32[]{:S(2)}) %collective-permute-start) | collective-permute-done | bytes 540704 | tf_op jit(solution)/shard_map/ppermute | solution.py:327
  15.9 1.3 %collective-permute-start.3 = (bf16[64,4224]{1,0:T(8,128)(2,1)S(1)}, bf16[64,4224]{1,0:T(8,128)(2,1)S(1)}, u32[]{:S(2)}, u32[]{:S(2)}) collective-permute-start(bf16[64,4224]{1,0:T(8,128)(2,1)S(1)} %collective-permute-done.refs_0_), channel_id=1, source_target_pairs={{4,0},{8,12},{5,1},{9,13},{6,2},{10,14},{7,3},{11,15},{20,16},{24,... | collective-permute-start | bytes 1622024 | tf_op jit(solution)/shard_map/ppermute | solution.py:327
  17.2 3.5 %shard_map.57 = (bf16[128,1152]{1,0:T(8,128)(2,1)S(1)}, f32[64,1024]{1,0:T(8,128)S(1)}, f32[32,64]{1,0:T(8,128)S(1)}) custom-call(bf16[64,4224]{1,0:T(8,128)(2,1)S(1)} %collective-permute-done.refs_0_, bf16[4096,2048]{1,0:T(8,128)(2,1)S(1)} %get-tuple-element.40.refs_1_.refs_2_, bf16[128,4096]{1,0:T(8,128)(2,1)S(1)} %get-tuple-element.41.refs_2_.refs_3_, ...), custom_call_target="tpu_custom_call" | custom-call | flops 1073741824 | bytes 16777216 | tf_op jit(solution)/shard_map/pallas_call | solution.py:243
  20.7 2.7 %collective-permute-start.7 = (bf16[64,4224]{1,0:T(8,128)(2,1)S(1)}, bf16[64,4224]{1,0:T(8,128)(2,1)S(1)}, u32[]{:S(2)}, u32[]{:S(2)}) collective-permute-start(bf16[64,4224]{1,0:T(8,128)(2,1)S(1)} %get-tuple-element.57.x_ref), channel_id=1, source_target_pairs={{0,4},{12,8},{8,0},{4,12},{1,5},{13,9},{9,1},{5,13},{2,6},{14,10},... | collective-permute-start | bytes 1622024 | tf_op jit(solution)/shard_map/ppermute | solution.py:327
  23.4 0.5 collective-permute-start.1
  23.9 6.8 %collective-permute-done.1.got_ref = bf16[128,1152]{1,0:T(8,128)(2,1)S(1)} collective-permute-done((bf16[128,1152]{1,0:T(8,128)(2,1)S(1)}, bf16[128,1152]{1,0:T(8,128)(2,1)S(1)}, u32[]{:S(2)}, u32[]{:S(2)}) %collective-permute-start.1) | collective-permute-done | bytes 294944 | tf_op jit(solution)/shard_map/ppermute | solution.py:358
  30.7 0.0 copy-done
  30.7 0.5 shard_map.58
  31.2 0.0 collective-permute-done.4.refs_1_
  31.2 11.3 %collective-permute-done.3.refs_0_ = bf16[64,4224]{1,0:T(8,128)(2,1)S(1)} collective-permute-done((bf16[64,4224]{1,0:T(8,128)(2,1)S(1)}, bf16[64,4224]{1,0:T(8,128)(2,1)S(1)}, u32[]{:S(2)}, u32[]{:S(2)}) %collective-permute-start.3) | collective-permute-done | bytes 540704 | tf_op jit(solution)/shard_map/ppermute | solution.py:327
  42.5 3.5 %shard_map.59 = (bf16[64,1152]{1,0:T(8,128)(2,1)S(1)}, f32[64,1024]{1,0:T(8,128)S(1)}, f32[32,64]{1,0:T(8,128)S(1)}) custom-call(bf16[64,4224]{1,0:T(8,128)(2,1)S(1)} %collective-permute-done.3.refs_0_, bf16[64,4224]{1,0:T(8,128)(2,1)S(1)} %collective-permute-done.4.refs_1_, bf16[4096,2048]{1,0:T(8,128)(2,1)S(1)} %get-tuple-element.40.refs_1_.refs_2_, ...), custom_call_target="tpu_custom_call" | custom-call | flops 1073741824 | bytes 16777216 | tf_op jit(solution)/shard_map/pallas_call | solution.py:243
  46.0 0.0 collective-permute-done.7.refs_0_
  46.0 3.5 %shard_map.61 = (bf16[64,1152]{1,0:T(8,128)(2,1)S(1)}, f32[64,1024]{1,0:T(8,128)S(1)}, f32[32,64]{1,0:T(8,128)S(1)}) custom-call(bf16[64,4224]{1,0:T(8,128)(2,1)S(1)} %collective-permute-done.7.refs_0_, bf16[4096,2048]{1,0:T(8,128)(2,1)S(1)} %get-tuple-element.40.refs_1_.refs_2_, bf16[128,4096]{1,0:T(8,128)(2,1)S(1)} %get-tuple-element.41.refs_2_.refs_3_), custom_call_target="tpu_custom_call" | custom-call | flops 1073741824 | bytes 16777216 | tf_op jit(solution)/shard_map/pallas_call | solution.py:243
  49.5 0.6 collective-permute-start.8
  50.1 1.5 %collective-permute-start.5 = (bf16[64,1152]{1,0:T(8,128)(2,1)S(1)}, bf16[64,1152]{1,0:T(8,128)(2,1)S(1)}, u32[]{:S(2)}, u32[]{:S(2)}) collective-permute-start(bf16[64,1152]{1,0:T(8,128)(2,1)S(1)} %get-tuple-element.53), channel_id=1, source_target_pairs={{0,2},{2,0},{1,3},{3,1},{4,6},{6,4},{5,7},{7,5},{8,10},{10,8},{9,1... | collective-permute-start | bytes 442376 | tf_op jit(solution)/shard_map/ppermute | solution.py:358
  51.6 0.0 collective-permute-start.14
  51.6 2.4 %collective-permute-start.10 = (bf16[64,1024]{1,0:T(8,128)(2,1)S(1)}, bf16[64,1024]{1,0:T(8,128)(2,1)S(1)}, u32[]{:S(2)}, u32[]{:S(2)}) collective-permute-start(bf16[64,1024]{1,0:T(8,128)(2,1)S(1)} %get-tuple-element.49.refs_0_), channel_id=1, source_target_pairs={{2,0},{6,4},{8,10},{12,14},{3,1},{7,5},{9,11},{13,15},{18,16},{22,... | collective-permute-start | bytes 393224 | tf_op jit(solution)/shard_map/ppermute | solution.py:365
  54.0 4.7 %collective-permute-start.11 = (bf16[64,1024]{1,0:T(8,128)(2,1)S(1)}, bf16[64,1024]{1,0:T(8,128)(2,1)S(1)}, u32[]{:S(2)}, u32[]{:S(2)}) collective-permute-start(bf16[64,1024]{1,0:T(8,128)(2,1)S(1)} %get-tuple-element.50), channel_id=1, source_target_pairs={{2,4},{6,12},{8,2},{12,10},{3,5},{7,13},{9,3},{13,11},{18,20},{22,... | collective-permute-start | bytes 393224 | tf_op jit(solution)/shard_map/ppermute | solution.py:365
  58.7 0.0 collective-permute-done.8.got_ref
  58.8 1.3 %collective-permute-start.2 = (bf16[64,1024]{1,0:T(8,128)(2,1)S(1)}, bf16[64,1024]{1,0:T(8,128)(2,1)S(1)}, u32[]{:S(2)}, u32[]{:S(2)}) collective-permute-start(bf16[64,1024]{1,0:T(8,128)(2,1)S(1)} %get-tuple-element.50), channel_id=1, source_target_pairs={{0,4},{4,12},{10,2},{14,10},{1,5},{5,13},{11,3},{15,11},{16,20},{2... | collective-permute-start | bytes 393224 | tf_op jit(solution)/shard_map/ppermute | solution.py:364
  60.1 0.3 shard_map.62
  60.4 0.0 collective-permute-done.5.got_ref
  60.4 3.6 %collective-permute-start.16 = (bf16[32,4096]{1,0:T(8,128)(2,1)S(1)}, bf16[32,4096]{1,0:T(8,128)(2,1)S(1)}, u32[]{:S(2)}, u32[]{:S(2)}) collective-permute-start(bf16[32,4096]{1,0:T(8,128)(2,1)S(1)} %get-tuple-element.66), channel_id=1, source_target_pairs={{0,8},{4,0},{8,12},{12,4},{1,9},{5,1},{9,13},{13,5},{2,10},{6,2},{... | collective-permute-start | bytes 786440 | tf_op jit(solution)/shard_map/ppermute | solution.py:327
  64.0 0.3 shard_map.60
  64.3 0.0 collective-permute-done.10.refs_4_
  64.3 1.3 %collective-permute-start.13 = (bf16[64,1024]{1,0:T(8,128)(2,1)S(1)}, bf16[64,1024]{1,0:T(8,128)(2,1)S(1)}, u32[]{:S(2)}, u32[]{:S(2)}) collective-permute-start(bf16[64,1024]{1,0:T(8,128)(2,1)S(1)} %get-tuple-element.62), channel_id=1, source_target_pairs={{2,8},{6,0},{8,14},{12,6},{3,9},{7,1},{9,15},{13,7},{18,24},{22,16... | collective-permute-start | bytes 393224 | tf_op jit(solution)/shard_map/ppermute | solution.py:365
  65.6 0.0 collective-permute-done.11.refs_5_
  65.6 0.5 collective-permute-start.15
  66.1 12.5 %collective-permute-done.2.refs_1_ = bf16[64,1024]{1,0:T(8,128)(2,1)S(1)} collective-permute-done((bf16[64,1024]{1,0:T(8,128)(2,1)S(1)}, bf16[64,1024]{1,0:T(8,128)(2,1)S(1)}, u32[]{:S(2)}, u32[]{:S(2)}) %collective-permute-start.2) | collective-permute-done | bytes 131104 | tf_op jit(solution)/shard_map/ppermute | solution.py:364
  78.6 0.7 collective-permute-start.9
  79.3 0.0 collective-permute-done.14.refs_9_
  79.3 5.6 %collective-permute-start.12 = (bf16[64,1024]{1,0:T(8,128)(2,1)S(1)}, bf16[64,1024]{1,0:T(8,128)(2,1)S(1)}, u32[]{:S(2)}, u32[]{:S(2)}) collective-permute-start(bf16[64,1024]{1,0:T(8,128)(2,1)S(1)} %get-tuple-element.56), channel_id=1, source_target_pairs={{2,12},{6,8},{8,6},{12,2},{3,13},{7,9},{9,7},{13,3},{18,28},{22,24... | collective-permute-start | bytes 393224 | tf_op jit(solution)/shard_map/ppermute | solution.py:365
  84.9 0.0 collective-permute-done.13.refs_7_
  84.9 1.3 %collective-permute-start.6 = (bf16[64,1024]{1,0:T(8,128)(2,1)S(1)}, bf16[64,1024]{1,0:T(8,128)(2,1)S(1)}, u32[]{:S(2)}, u32[]{:S(2)}) collective-permute-start(bf16[64,1024]{1,0:T(8,128)(2,1)S(1)} %get-tuple-element.56), channel_id=1, source_target_pairs={{0,12},{4,8},{10,6},{14,2},{1,13},{5,9},{11,7},{15,3},{16,28},{20,... | collective-permute-start | bytes 393224 | tf_op jit(solution)/shard_map/ppermute | solution.py:364
  86.2 0.0 collective-permute-done.9.refs_3_
  86.2 2.9 %collective-permute-done.12.refs_6_ = bf16[64,1024]{1,0:T(8,128)(2,1)S(1)} collective-permute-done((bf16[64,1024]{1,0:T(8,128)(2,1)S(1)}, bf16[64,1024]{1,0:T(8,128)(2,1)S(1)}, u32[]{:S(2)}, u32[]{:S(2)}) %collective-permute-start.12) | collective-permute-done | bytes 131104 | tf_op jit(solution)/shard_map/ppermute | solution.py:365
  89.1 4.5 %collective-permute-done.6.refs_2_ = bf16[64,1024]{1,0:T(8,128)(2,1)S(1)} collective-permute-done((bf16[64,1024]{1,0:T(8,128)(2,1)S(1)}, bf16[64,1024]{1,0:T(8,128)(2,1)S(1)}, u32[]{:S(2)}, u32[]{:S(2)}) %collective-permute-start.6) | collective-permute-done | bytes 131104 | tf_op jit(solution)/shard_map/ppermute | solution.py:364
  93.6 0.0 collective-permute-done.16.refs_11_
  93.6 0.0 collective-permute-done.15.refs_10_
  93.6 1.6 %shard_map.63 = bf16[64,4096]{1,0:T(8,128)(2,1)} custom-call(s32[64,1]{1,0:T(8,128)S(1)} %get-tuple-element.36.slot_ref, bf16[64,1024]{1,0:T(8,128)(2,1)S(1)} %get-tuple-element.49.refs_0_, bf16[64,1024]{1,0:T(8,128)(2,1)S(1)} %collective-permute-done.2.refs_1_, bf16[64,1024]{1,0:T(8,128)(2,1)S(1)} %collective-permute-done.6.refs_2_, ...), custom_call_target="tpu_custom_call" | custom-call | tf_op jit(solution)/shard_map/pallas_call | solution.py:382
Async XLA Ops:
  0.0 0.7 copy-start.1
  1.7 14.2 %collective-permute-start = (bf16[64,4224]{1,0:T(8,128)(2,1)S(1)}, bf16[64,4224]{1,0:T(8,128)(2,1)S(1)}, u32[]{:S(2)}, u32[]{:S(2)}) collective-permute-start(bf16[64,4224]{1,0:T(8,128)(2,1)S(1)} %get-tuple-element.57.x_ref), channel_id=1, source_target_pairs={{0,8},{12,4},{4,0},{8,12},{1,9},{13,5},{5,1},{9,13},{2,10},{14,6},... | collective-permute-start | bytes 1622024 | tf_op jit(solution)/shard_map/ppermute | solution.py:327
  4.4 26.4 %copy-start = (bf16[2,64,4096]{2,1,0:T(8,128)(2,1)S(1)}, bf16[2,64,4096]{2,1,0:T(8,128)(2,1)}, u32[]{:S(2)}) copy-start(bf16[2,64,4096]{2,1,0:T(8,128)(2,1)} %e_ref.5) | copy-start | bytes 3145732
  11.8 19.4 %collective-permute-start.4 = (bf16[64,4224]{1,0:T(8,128)(2,1)S(1)}, bf16[64,4224]{1,0:T(8,128)(2,1)S(1)}, u32[]{:S(2)}, u32[]{:S(2)}) collective-permute-start(bf16[64,4224]{1,0:T(8,128)(2,1)S(1)} %get-tuple-element.57.x_ref), channel_id=1, source_target_pairs={{4,8},{8,4},{5,9},{9,5},{6,10},{10,6},{7,11},{11,7},{20,24},{24,20... | collective-permute-start | bytes 1622024 | tf_op jit(solution)/shard_map/ppermute | solution.py:327
  15.9 26.6 %collective-permute-start.3 = (bf16[64,4224]{1,0:T(8,128)(2,1)S(1)}, bf16[64,4224]{1,0:T(8,128)(2,1)S(1)}, u32[]{:S(2)}, u32[]{:S(2)}) collective-permute-start(bf16[64,4224]{1,0:T(8,128)(2,1)S(1)} %collective-permute-done.refs_0_), channel_id=1, source_target_pairs={{4,0},{8,12},{5,1},{9,13},{6,2},{10,14},{7,3},{11,15},{20,16},{24,... | collective-permute-start | bytes 1622024 | tf_op jit(solution)/shard_map/ppermute | solution.py:327
  20.7 25.3 %collective-permute-start.7 = (bf16[64,4224]{1,0:T(8,128)(2,1)S(1)}, bf16[64,4224]{1,0:T(8,128)(2,1)S(1)}, u32[]{:S(2)}, u32[]{:S(2)}) collective-permute-start(bf16[64,4224]{1,0:T(8,128)(2,1)S(1)} %get-tuple-element.57.x_ref), channel_id=1, source_target_pairs={{0,4},{12,8},{8,0},{4,12},{1,5},{13,9},{9,1},{5,13},{2,6},{14,10},... | collective-permute-start | bytes 1622024 | tf_op jit(solution)/shard_map/ppermute | solution.py:327
  23.4 7.3 %collective-permute-start.1 = (bf16[128,1152]{1,0:T(8,128)(2,1)S(1)}, bf16[128,1152]{1,0:T(8,128)(2,1)S(1)}, u32[]{:S(2)}, u32[]{:S(2)}) collective-permute-start(bf16[128,1152]{1,0:T(8,128)(2,1)S(1)} %get-tuple-element.44), channel_id=1, source_target_pairs={{0,2},{2,0},{1,3},{3,1},{4,6},{6,4},{5,7},{7,5},{8,10},{10,8},{9,1... | collective-permute-start | bytes 884744 | tf_op jit(solution)/shard_map/ppermute | solution.py:358
  49.5 9.2 %collective-permute-start.8 = (bf16[64,1152]{1,0:T(8,128)(2,1)S(1)}, bf16[64,1152]{1,0:T(8,128)(2,1)S(1)}, u32[]{:S(2)}, u32[]{:S(2)}) collective-permute-start(bf16[64,1152]{1,0:T(8,128)(2,1)S(1)} %get-tuple-element.59), channel_id=1, source_target_pairs={{0,2},{2,0},{1,3},{3,1},{4,6},{6,4},{5,7},{7,5},{8,10},{10,8},{9,1... | collective-permute-start | bytes 442376 | tf_op jit(solution)/shard_map/ppermute | solution.py:358
  50.1 10.3 %collective-permute-start.5 = (bf16[64,1152]{1,0:T(8,128)(2,1)S(1)}, bf16[64,1152]{1,0:T(8,128)(2,1)S(1)}, u32[]{:S(2)}, u32[]{:S(2)}) collective-permute-start(bf16[64,1152]{1,0:T(8,128)(2,1)S(1)} %get-tuple-element.53), channel_id=1, source_target_pairs={{0,2},{2,0},{1,3},{3,1},{4,6},{6,4},{5,7},{7,5},{8,10},{10,8},{9,1... | collective-permute-start | bytes 442376 | tf_op jit(solution)/shard_map/ppermute | solution.py:358
  51.6 27.7 %collective-permute-start.14 = (bf16[32,4096]{1,0:T(8,128)(2,1)S(1)}, bf16[32,4096]{1,0:T(8,128)(2,1)S(1)}, u32[]{:S(2)}, u32[]{:S(2)}) collective-permute-start(bf16[32,4096]{1,0:T(8,128)(2,1)S(1)} %get-tuple-element.64), channel_id=1, source_target_pairs={{0,4},{4,12},{8,0},{12,8},{1,5},{5,13},{9,1},{13,9},{2,6},{6,14},{... | collective-permute-start | bytes 786440 | tf_op jit(solution)/shard_map/ppermute | solution.py:327
  51.6 12.7 %collective-permute-start.10 = (bf16[64,1024]{1,0:T(8,128)(2,1)S(1)}, bf16[64,1024]{1,0:T(8,128)(2,1)S(1)}, u32[]{:S(2)}, u32[]{:S(2)}) collective-permute-start(bf16[64,1024]{1,0:T(8,128)(2,1)S(1)} %get-tuple-element.49.refs_0_), channel_id=1, source_target_pairs={{2,0},{6,4},{8,10},{12,14},{3,1},{7,5},{9,11},{13,15},{18,16},{22,... | collective-permute-start | bytes 393224 | tf_op jit(solution)/shard_map/ppermute | solution.py:365
  54.0 11.6 %collective-permute-start.11 = (bf16[64,1024]{1,0:T(8,128)(2,1)S(1)}, bf16[64,1024]{1,0:T(8,128)(2,1)S(1)}, u32[]{:S(2)}, u32[]{:S(2)}) collective-permute-start(bf16[64,1024]{1,0:T(8,128)(2,1)S(1)} %get-tuple-element.50), channel_id=1, source_target_pairs={{2,4},{6,12},{8,2},{12,10},{3,5},{7,13},{9,3},{13,11},{18,20},{22,... | collective-permute-start | bytes 393224 | tf_op jit(solution)/shard_map/ppermute | solution.py:365
  58.8 19.9 %collective-permute-start.2 = (bf16[64,1024]{1,0:T(8,128)(2,1)S(1)}, bf16[64,1024]{1,0:T(8,128)(2,1)S(1)}, u32[]{:S(2)}, u32[]{:S(2)}) collective-permute-start(bf16[64,1024]{1,0:T(8,128)(2,1)S(1)} %get-tuple-element.50), channel_id=1, source_target_pairs={{0,4},{4,12},{10,2},{14,10},{1,5},{5,13},{11,3},{15,11},{16,20},{2... | collective-permute-start | bytes 393224 | tf_op jit(solution)/shard_map/ppermute | solution.py:364
  60.4 33.2 %collective-permute-start.16 = (bf16[32,4096]{1,0:T(8,128)(2,1)S(1)}, bf16[32,4096]{1,0:T(8,128)(2,1)S(1)}, u32[]{:S(2)}, u32[]{:S(2)}) collective-permute-start(bf16[32,4096]{1,0:T(8,128)(2,1)S(1)} %get-tuple-element.66), channel_id=1, source_target_pairs={{0,8},{4,0},{8,12},{12,4},{1,9},{5,1},{9,13},{13,5},{2,10},{6,2},{... | collective-permute-start | bytes 786440 | tf_op jit(solution)/shard_map/ppermute | solution.py:327
  64.3 20.6 %collective-permute-start.13 = (bf16[64,1024]{1,0:T(8,128)(2,1)S(1)}, bf16[64,1024]{1,0:T(8,128)(2,1)S(1)}, u32[]{:S(2)}, u32[]{:S(2)}) collective-permute-start(bf16[64,1024]{1,0:T(8,128)(2,1)S(1)} %get-tuple-element.62), channel_id=1, source_target_pairs={{2,8},{6,0},{8,14},{12,6},{3,9},{7,1},{9,15},{13,7},{18,24},{22,16... | collective-permute-start | bytes 393224 | tf_op jit(solution)/shard_map/ppermute | solution.py:365
  65.6 27.9 %collective-permute-start.15 = (bf16[32,4096]{1,0:T(8,128)(2,1)S(1)}, bf16[32,4096]{1,0:T(8,128)(2,1)S(1)}, u32[]{:S(2)}, u32[]{:S(2)}) collective-permute-start(bf16[32,4096]{1,0:T(8,128)(2,1)S(1)} %get-tuple-element.65), channel_id=1, source_target_pairs={{0,12},{4,8},{8,4},{12,0},{1,13},{5,9},{9,5},{13,1},{2,14},{6,10},... | collective-permute-start | bytes 786440 | tf_op jit(solution)/shard_map/ppermute | solution.py:327
  78.6 7.6 %collective-permute-start.9 = (bf16[64,1024]{1,0:T(8,128)(2,1)S(1)}, bf16[64,1024]{1,0:T(8,128)(2,1)S(1)}, u32[]{:S(2)}, u32[]{:S(2)}) collective-permute-start(bf16[64,1024]{1,0:T(8,128)(2,1)S(1)} %get-tuple-element.62), channel_id=1, source_target_pairs={{0,8},{4,0},{10,14},{14,6},{1,9},{5,1},{11,15},{15,7},{16,24},{20,... | collective-permute-start | bytes 393224 | tf_op jit(solution)/shard_map/ppermute | solution.py:364
  79.3 9.8 %collective-permute-start.12 = (bf16[64,1024]{1,0:T(8,128)(2,1)S(1)}, bf16[64,1024]{1,0:T(8,128)(2,1)S(1)}, u32[]{:S(2)}, u32[]{:S(2)}) collective-permute-start(bf16[64,1024]{1,0:T(8,128)(2,1)S(1)} %get-tuple-element.56), channel_id=1, source_target_pairs={{2,12},{6,8},{8,6},{12,2},{3,13},{7,9},{9,7},{13,3},{18,28},{22,24... | collective-permute-start | bytes 393224 | tf_op jit(solution)/shard_map/ppermute | solution.py:365
  84.9 8.7 %collective-permute-start.6 = (bf16[64,1024]{1,0:T(8,128)(2,1)S(1)}, bf16[64,1024]{1,0:T(8,128)(2,1)S(1)}, u32[]{:S(2)}, u32[]{:S(2)}) collective-permute-start(bf16[64,1024]{1,0:T(8,128)(2,1)S(1)} %get-tuple-element.56), channel_id=1, source_target_pairs={{0,12},{4,8},{10,6},{14,2},{1,13},{5,9},{11,7},{15,3},{16,28},{20,... | collective-permute-start | bytes 393224 | tf_op jit(solution)/shard_map/ppermute | solution.py:364

commit v4 on v3

--- a/solution.py
+++ b/solution.py
@@ -231,7 +231,7 @@
         + stage_shapes(rows, rows, cols, local * most, rank),
         scratch_shapes=[pltpu.VMEM((rows, cols), F32), pltpu.SemaphoreType.DMA((9,))],
         compiler_params=PARAMS,
-        cost_estimate=cost(2 * rows * depth * cols, depth * cols * 2),
+        cost_estimate=cost(1, 1),
     )(vmem(x), hbm(s_t), hbm(w))
 
 
@@ -247,50 +247,53 @@
         out_shape=stage_shapes(rows, sent, cols, local * most, rank),
         scratch_shapes=[pltpu.VMEM((rows, cols), F32)],
         compiler_params=PARAMS,
-        cost_estimate=cost(2 * rows * depth * cols, depth * cols * 2),
+        cost_estimate=cost(1, 1),
     )(*xs, vmem(w), vmem(s_t), *before)
 
 
-def join_kernel(k, got_ref, e_ref, *refs):
-    ins, outs = refs[: 2 * k], refs[2 * k :]
+def join_kernel(k, n_mix, got_ref, e_ref, *refs):
+    ins, mixed, outs = refs[: 2 * k], refs[2 * k : 2 * k + n_mix], refs[2 * k + n_mix :]
     local, rank, _ = e_ref.shape
     width = got_ref.shape[1] - LANES
     rows = got_ref.shape[0] // k
+    owner = lax.axis_index("adapter") // 2 == lax.axis_index("tensor")
     for i in range(k):
-        keep, own, base, delta = ins[2 * i], ins[2 * i + 1], outs[2 * i], outs[2 * i + 1]
+        keep, own, delta = ins[2 * i], ins[2 * i + 1], outs[i]
         lines = slice(i * rows, (i + 1) * rows)
         spots = own.shape[0]
         most = spots // local
         terms = got_ref[i * rows : i * rows + spots, width:].astype(F32)
         total = (own[...] + terms[:, :rank] + terms[:, rank : 2 * rank]).astype(BF16)
-        base[...] = (keep[...] + got_ref[lines, :width].astype(F32)).astype(BF16)
+        base = (keep[...] + got_ref[lines, :width].astype(F32)).astype(BF16)
+        if n_mix:
+            outs[k][...] = jnp.where(owner, mixed[0][...], base)
+            outs[k + 1][...] = jnp.where(owner, base, mixed[0][...])
+        else:
+            outs[k + i][...] = base
         for j in range(local):
             put = slice(j * most, (j + 1) * most)
             wide = jnp.dot(total[put], e_ref[j], preferred_element_type=F32)
             delta[put, :] = (adapter_scale_factor * wide).astype(BF16)
 
 
-def join(got, e, pairs):
+def join(got, e, pairs, mix=()):
     k = len(pairs)
-    shapes = []
-    for keep, own in pairs:
-        shapes += [
-            pltpu.VMEM(keep.shape, BF16),
-            pltpu.VMEM((own.shape[0], e.shape[2]), BF16),
-        ]
+    keep, own = pairs[0]
+    wide = pltpu.VMEM((own.shape[0], e.shape[2]), BF16)
     return pl.pallas_call(
-        functools.partial(join_kernel, k),
-        in_specs=[VM] * (2 + 2 * k),
-        out_specs=[VM] * (2 * k),
-        out_shape=shapes,
+        functools.partial(join_kernel, k, len(mix)),
+        in_specs=[VM] * (2 + 2 * k + len(mix)),
+        out_specs=[VM] * (2 * k + len(mix)),
+        out_shape=[wide] * k + [pltpu.VMEM(keep.shape, BF16)] * (k + len(mix)),
         compiler_params=PARAMS,
-        cost_estimate=cost(1 << 28, 4 << 20),
-    )(got, e, *[a for pair in pairs for a in pair])
+        cost_estimate=cost(1, 1),
+    )(got, e, *[a for pair in pairs for a in pair], *mix)
 
 
 def final_kernel(planes, slot_ref, *refs):
-    straight, crossed, d_refs = refs[0:4], refs[4:8], refs[8:12]
-    o_ref, base = refs[12:]
+    own, by_02, by_13, by_31, by_2 = refs[0:5]
+    straight, crossed = (own, by_13, by_02, by_31), (by_02, by_31, by_2, by_13)
+    d_refs, (o_ref, base) = refs[5:9], refs[9:]
     rows, width = straight[0].shape
     me, half = lax.axis_index("adapter"), lax.axis_index("tensor")
     plane_of = [sum(jnp.where(me == a, p[a], 0) for a in range(4)) for p in planes]
@@ -350,43 +353,51 @@
     got_a = along(packed, [(0, 2), (3, 1), (1, 0), (2, 3)])
     s_t = jnp.swapaxes(shrink_weight, 1, 2).reshape(local * rank, -1)
     w, s_t, send_0, keep_0, own_0 = first_stage(dims, packed, s_t, base_weight)
-    packed, own_0 = lax.optimization_barrier((packed, own_0))
+    packed, got_a, own_0 = lax.optimization_barrier((packed, got_a, own_0))
+    got_f = along(got_a, [(1, 0), (2, 3)])
     got_b = along(packed, [(1, 2), (2, 1)])
-    got_f = along(got_a, [(1, 0), (2, 3)])
 
     def flip(s):
         return lax.ppermute(s, "tensor", [(0, 1), (1, 0)])
 
-    def home(base, k):
-        straight = [(2 * a + a // 2, 2 * h + a // 2) for a, h in back(k)]
-        crossed = [(2 * a + 1 - a // 2, 2 * h + a // 2) for a, h in back(k)]
-        return (
-            lax.ppermute(base, both, straight) if k else base,
-            lax.ppermute(base, both, crossed),
-        )
+    def straight(k):
+        return [(2 * a + a // 2, 2 * h + a // 2) for a, h in back(k)]
+
+    def crossed(k):
+        return [(2 * a + 1 - a // 2, 2 * h + a // 2) for a, h in back(k)]
+
+    def home(block, pairs):
+        return lax.ppermute(block, both, pairs)
 
     e = expand_weight
     send_1, keep_1, own_1 = stage(dims, [got_a], w, s_t, [send_0])
-    packed, send_1 = lax.optimization_barrier((packed, send_1))
+    packed, got_f, send_1 = lax.optimization_barrier((packed, got_f, send_1))
     got_c = along(packed, [(0, 1), (3, 2), (2, 0), (1, 3)])
-    base_0, d_0, base_1, d_1 = join(flip(send_1), e, [(keep_0, own_0), (keep_1, own_1)])
-    got_b, d_1 = lax.optimization_barrier((got_b, d_1))
+    got_1 = flip(send_1)
     send_2, keep_2, own_2 = stage(dims, [got_f, got_b], w, s_t)
-    base_2, d_2 = join(flip(send_2), e, [(keep_2, own_2)])
-    got_c, keep_2 = lax.optimization_barrier((got_c, keep_2))
+    d_0, d_1, base_0, base_1 = join(got_1, e, [(keep_0, own_0), (keep_1, own_1)])
+    came_1 = along(d_1, back(1))
+    got_2 = flip(send_2)
+    d_2, mix_02, mix_20 = join(got_2, e, [(keep_2, own_2)], [base_0])
+    came_2 = along(d_2, back(2))
+    got_c, came_1 = lax.optimization_barrier((got_c, came_1))
     send_3, keep_3, own_3 = stage(dims, [got_c], w, s_t)
-    base_3, d_3 = join(flip(send_3), e, [(keep_3, own_3)])
-    ways = [home(b, k) for k, b in enumerate((base_0, base_1, base_2, base_3))]
-    d_1, d_2, d_3 = along(d_1, back(1)), along(d_2, back(2)), along(d_3, back(3))
+    send_3, came_2 = lax.optimization_barrier((send_3, came_2))
+    d_3, mix_13, mix_31 = join(flip(send_3), e, [(keep_3, own_3)], [base_1])
+    from_02 = home(mix_20, straight(2) + crossed(0))
+    from_2 = home(mix_02, crossed(2))
+    came_3 = along(d_3, back(3))
+    from_13 = home(mix_13, straight(1) + crossed(3))
+    from_31 = home(mix_31, straight(3) + crossed(1))
 
     return pl.pallas_call(
         functools.partial(final_kernel, planes),
-        in_specs=[VM] * 13,
+        in_specs=[VM] * 10,
         out_specs=VM,
         out_shape=jax.ShapeDtypeStruct((rows, 2 * cols), BF16),
         scratch_shapes=[pltpu.VMEM((4, rows, cols // 2), BF16)],
         compiler_params=PARAMS,
-    )(slot_col, *[u for u, _ in ways], *[v for _, v in ways], d_0, d_1, d_2, d_3)
+    )(slot_col, base_0, from_02, from_13, from_31, from_2, d_0, came_1, came_2, came_3)
 
 
 def solution(mesh):

time: 95.5 us -> 88.2 us (0.924)
  the two profiles are of different devices: /device:TPU:2 before, /device:TPU:6 now
where the time goes in v4:
time: 88.2 us; the launch traced here: 88 us
  waiting for transfers between devices  44.3 us (50%)
  Pallas kernels  21.6 us (24%)
  starting transfers between devices  21.4 us (24%)
    ppermute x7, waiting for transfers between devices, along(): return lax.ppermute(x, 'adapter', pairs)  28.6 us
    ppermute x7, starting transfers between devices, along(): return lax.ppermute(x, 'adapter', pairs)  11 us
    pallas_call x3, Pallas kernels, stage(): pl.pallas_call(functools.partial(stage_kernel, dims, len(xs), bool(before...  10.5 us
    ppermute x4, waiting for transfers between devices, home(): return lax.ppermute(block, both, pairs)  8 us
    ppermute x4, starting transfers between devices, home(): return lax.ppermute(block, both, pairs)  7.77 us
    ppermute x3, waiting for transfers between devices, flip(): return lax.ppermute(s, 'tensor', [(0, 1), (1, 0)])  7.67 us
    pallas_call x1, Pallas kernels, first_stage(): pl.pallas_call(functools.partial(first_kernel, dims), in_specs=[VM, HB, H...  7.35 us
    ppermute x3, starting transfers between devices, flip(): return lax.ppermute(s, 'tensor', [(0, 1), (1, 0)])  2.58 us
  transfers between devices with their start and end apart: 14, of which 10 were waited for; matrix products, arithmetic and copies ran while one was open for 0% of the time, Pallas kernels for 21%

profile of v4, /device:TPU:6, one launch (start us, length us, event | category | flops | bytes accessed | tf_op | source)
XLA Modules:
  0.0 88.0 jit_solution(15621348830476828506)
XLA Ops:
  0.0 0.0 copy-start.1
  0.0 0.7 copy-done.1
  0.7 1.1 %shard_map.55 = (bf16[64,4224]{1,0:T(8,128)(2,1)S(1)}, s32[64,1]{1,0:T(8,128)S(1)}) custom-call(s32[1,64]{1,0:T(1,128)S(1)} %bitcast.4, bf16[64,4096]{1,0:T(8,128)(2,1)} %x_ref.1), custom_call_target="tpu_custom_call" | custom-call | tf_op jit(solution)/shard_map/pallas_call | solution.py:341
  1.7 2.6 %collective-permute-start = (bf16[64,4224]{1,0:T(8,128)(2,1)S(1)}, bf16[64,4224]{1,0:T(8,128)(2,1)S(1)}, u32[]{:S(2)}, u32[]{:S(2)}) collective-permute-start(bf16[64,4224]{1,0:T(8,128)(2,1)S(1)} %get-tuple-element.61.x_ref), channel_id=1, source_target_pairs={{0,8},{12,4},{4,0},{8,12},{1,9},{13,5},{5,1},{9,13},{2,10},{14,6},... | collective-permute-start | bytes 1622024 | tf_op jit(solution)/shard_map/ppermute | solution.py:330
  4.4 7.3 %shard_map.56 = (bf16[4096,2048]{1,0:T(8,128)(2,1)S(1)}, bf16[128,4096]{1,0:T(8,128)(2,1)S(1)}, bf16[64,1152]{1,0:T(8,128)(2,1)S(1)}, f32[64,1024]{1,0:T(8,128)S(1)}, f32[32,64]{1,0:T(8,128)S(1)}) custom-call(bf16[64,4224]{1,0:T(8,128)(2,1)S(1)} %get-tuple-element.61.x_ref, bf16[128,4096]{1,0:T(8,128)(2,1)} %bitcast.5, bf16[4096,2048]{1,0:T(8,128)(2,1)} %w_hbm.1), custom_call_target="tpu_custom_call" | custom-call | flops 1 | bytes 1 | tf_op jit(solution)/shard_map/pallas_call | solution.py:226
  11.7 4.2 %collective-permute-done.refs_0_ = bf16[64,4224]{1,0:T(8,128)(2,1)S(1)} collective-permute-done((bf16[64,4224]{1,0:T(8,128)(2,1)S(1)}, bf16[64,4224]{1,0:T(8,128)(2,1)S(1)}, u32[]{:S(2)}, u32[]{:S(2)}) %collective-permute-start) | collective-permute-done | bytes 540704 | tf_op jit(solution)/shard_map/ppermute | solution.py:330
  15.9 1.3 %collective-permute-start.1 = (bf16[64,4224]{1,0:T(8,128)(2,1)S(1)}, bf16[64,4224]{1,0:T(8,128)(2,1)S(1)}, u32[]{:S(2)}, u32[]{:S(2)}) collective-permute-start(bf16[64,4224]{1,0:T(8,128)(2,1)S(1)} %collective-permute-done.refs_0_), channel_id=1, source_target_pairs={{4,0},{8,12},{5,1},{9,13},{6,2},{10,14},{7,3},{11,15},{20,16},{24,... | collective-permute-start | bytes 1622024 | tf_op jit(solution)/shard_map/ppermute | solution.py:330
  17.2 0.7 collective-permute-start.3
  17.9 0.0 copy-start
  17.9 3.5 %shard_map.57 = (bf16[128,1152]{1,0:T(8,128)(2,1)S(1)}, f32[64,1024]{1,0:T(8,128)S(1)}, f32[32,64]{1,0:T(8,128)S(1)}) custom-call(bf16[64,4224]{1,0:T(8,128)(2,1)S(1)} %collective-permute-done.refs_0_, bf16[4096,2048]{1,0:T(8,128)(2,1)S(1)} %get-tuple-element.46.refs_1_.refs_2_, bf16[128,4096]{1,0:T(8,128)(2,1)S(1)} %get-tuple-element.47.refs_2_.refs_3_, ...), custom_call_target="tpu_custom_call" | custom-call | flops 1 | bytes 1 | tf_op jit(solution)/shard_map/pallas_call | solution.py:243
  21.4 9.5 %collective-permute-done.1.refs_0_ = bf16[64,4224]{1,0:T(8,128)(2,1)S(1)} collective-permute-done((bf16[64,4224]{1,0:T(8,128)(2,1)S(1)}, bf16[64,4224]{1,0:T(8,128)(2,1)S(1)}, u32[]{:S(2)}, u32[]{:S(2)}) %collective-permute-start.1) | collective-permute-done | bytes 540704 | tf_op jit(solution)/shard_map/ppermute | solution.py:330
  30.9 0.5 collective-permute-start.2
  31.5 0.0 collective-permute-start.6
  31.5 0.0 collective-permute-done.3.refs_1_
  31.5 3.5 %shard_map.59 = (bf16[64,1152]{1,0:T(8,128)(2,1)S(1)}, f32[64,1024]{1,0:T(8,128)S(1)}, f32[32,64]{1,0:T(8,128)S(1)}) custom-call(bf16[64,4224]{1,0:T(8,128)(2,1)S(1)} %collective-permute-done.1.refs_0_, bf16[64,4224]{1,0:T(8,128)(2,1)S(1)} %collective-permute-done.3.refs_1_, bf16[4096,2048]{1,0:T(8,128)(2,1)S(1)} %get-tuple-element.46.refs_1_.refs_2_, ...), custom_call_target="tpu_custom_call" | custom-call | flops 1 | bytes 1 | tf_op jit(solution)/shard_map/pallas_call | solution.py:243
  35.0 1.5 %collective-permute-start.4 = (bf16[64,1152]{1,0:T(8,128)(2,1)S(1)}, bf16[64,1152]{1,0:T(8,128)(2,1)S(1)}, u32[]{:S(2)}, u32[]{:S(2)}) collective-permute-start(bf16[64,1152]{1,0:T(8,128)(2,1)S(1)} %get-tuple-element.57), channel_id=1, source_target_pairs={{0,2},{2,0},{1,3},{3,1},{4,6},{6,4},{5,7},{7,5},{8,10},{10,8},{9,1... | collective-permute-start | bytes 442376 | tf_op jit(solution)/shard_map/ppermute | solution.py:361
  36.5 3.0 %collective-permute-done.2.got_ref = bf16[128,1152]{1,0:T(8,128)(2,1)S(1)} collective-permute-done((bf16[128,1152]{1,0:T(8,128)(2,1)S(1)}, bf16[128,1152]{1,0:T(8,128)(2,1)S(1)}, u32[]{:S(2)}, u32[]{:S(2)}) %collective-permute-start.2) | collective-permute-done | bytes 294944 | tf_op jit(solution)/shard_map/ppermute | solution.py:361
  39.5 0.0 copy-done
  39.5 0.5 shard_map.58
  39.9 1.7 %collective-permute-start.7 = (bf16[32,4096]{1,0:T(8,128)(2,1)S(1)}, bf16[32,4096]{1,0:T(8,128)(2,1)S(1)}, u32[]{:S(2)}, u32[]{:S(2)}) collective-permute-start(bf16[32,4096]{1,0:T(8,128)(2,1)S(1)} %get-tuple-element.62), channel_id=1, source_target_pairs={{0,4},{4,12},{8,0},{12,8},{1,5},{5,13},{9,1},{13,9},{2,6},{6,14},{... | collective-permute-start | bytes 786440 | tf_op jit(solution)/shard_map/ppermute | solution.py:330
  41.6 0.0 collective-permute-done.4.got_ref
  41.6 0.3 shard_map.60
  42.0 2.9 %collective-permute-start.8 = (bf16[32,4096]{1,0:T(8,128)(2,1)S(1)}, bf16[32,4096]{1,0:T(8,128)(2,1)S(1)}, u32[]{:S(2)}, u32[]{:S(2)}) collective-permute-start(bf16[32,4096]{1,0:T(8,128)(2,1)S(1)} %get-tuple-element.65), channel_id=1, source_target_pairs={{0,12},{4,8},{8,4},{12,0},{1,13},{5,9},{9,5},{13,1},{2,14},{6,10},... | collective-permute-start | bytes 786440 | tf_op jit(solution)/shard_map/ppermute | solution.py:330
  44.9 4.4 %collective-permute-done.6.refs_0_ = bf16[64,4224]{1,0:T(8,128)(2,1)S(1)} collective-permute-done((bf16[64,4224]{1,0:T(8,128)(2,1)S(1)}, bf16[64,4224]{1,0:T(8,128)(2,1)S(1)}, u32[]{:S(2)}, u32[]{:S(2)}) %collective-permute-start.6) | collective-permute-done | bytes 540704 | tf_op jit(solution)/shard_map/ppermute | solution.py:330
  49.3 10.5 %collective-permute-done.7.refs_6_ = bf16[32,4096]{1,0:T(8,128)(2,1)S(1)} collective-permute-done((bf16[32,4096]{1,0:T(8,128)(2,1)S(1)}, bf16[32,4096]{1,0:T(8,128)(2,1)S(1)}, u32[]{:S(2)}, u32[]{:S(2)}) %collective-permute-start.7) | collective-permute-done | bytes 262176 | tf_op jit(solution)/shard_map/ppermute | solution.py:330
  59.8 3.5 %shard_map.61 = (bf16[64,1152]{1,0:T(8,128)(2,1)S(1)}, f32[64,1024]{1,0:T(8,128)S(1)}, f32[32,64]{1,0:T(8,128)S(1)}) custom-call(bf16[64,4224]{1,0:T(8,128)(2,1)S(1)} %collective-permute-done.6.refs_0_, bf16[4096,2048]{1,0:T(8,128)(2,1)S(1)} %get-tuple-element.46.refs_1_.refs_2_, bf16[128,4096]{1,0:T(8,128)(2,1)S(1)} %get-tuple-element.47.refs_2_.refs_3_), custom_call_target="tpu_custom_call" | custom-call | flops 1 | bytes 1 | tf_op jit(solution)/shard_map/pallas_call | solution.py:243
  63.3 0.0 collective-permute-done.8.refs_7_
  63.3 0.5 collective-permute-start.9
  63.8 4.7 %collective-permute-done.9.got_ref = bf16[64,1152]{1,0:T(8,128)(2,1)S(1)} collective-permute-done((bf16[64,1152]{1,0:T(8,128)(2,1)S(1)}, bf16[64,1152]{1,0:T(8,128)(2,1)S(1)}, u32[]{:S(2)}, u32[]{:S(2)}) %collective-permute-start.9) | collective-permute-done | bytes 147488 | tf_op jit(solution)/shard_map/ppermute | solution.py:361
  68.5 0.3 shard_map.62
  68.8 1.8 %collective-permute-start.13 = (bf16[32,4096]{1,0:T(8,128)(2,1)S(1)}, bf16[32,4096]{1,0:T(8,128)(2,1)S(1)}, u32[]{:S(2)}, u32[]{:S(2)}) collective-permute-start(bf16[32,4096]{1,0:T(8,128)(2,1)S(1)} %get-tuple-element.76), channel_id=1, source_target_pairs={{0,8},{4,0},{8,12},{12,4},{1,9},{5,1},{9,13},{13,5},{2,10},{6,2},{... | collective-permute-start | bytes 786440 | tf_op jit(solution)/shard_map/ppermute | solution.py:330
  70.6 0.5 collective-permute-start.5
  71.1 4.0 %collective-permute-start.12 = (bf16[64,1024]{1,0:T(8,128)(2,1)S(1)}, bf16[64,1024]{1,0:T(8,128)(2,1)S(1)}, u32[]{:S(2)}, u32[]{:S(2)}) collective-permute-start(bf16[64,1024]{1,0:T(8,128)(2,1)S(1)} %get-tuple-element.72), channel_id=1, source_target_pairs={{2,12},{6,8},{8,6},{12,2},{3,13},{7,9},{9,7},{13,3},{18,28},{22,24... | collective-permute-start | bytes 393224 | tf_op jit(solution)/shard_map/ppermute | solution.py:370
  75.2 0.5 collective-permute-start.10
  75.7 2.7 %collective-permute-start.11 = (bf16[64,1024]{1,0:T(8,128)(2,1)S(1)}, bf16[64,1024]{1,0:T(8,128)(2,1)S(1)}, u32[]{:S(2)}, u32[]{:S(2)}) collective-permute-start(bf16[64,1024]{1,0:T(8,128)(2,1)S(1)} %get-tuple-element.71), channel_id=1, source_target_pairs={{0,8},{4,0},{10,14},{14,6},{2,4},{6,12},{8,2},{12,10},{1,9},{5,1},... | collective-permute-start | bytes 393224 | tf_op jit(solution)/shard_map/ppermute | solution.py:370
  78.4 2.2 %collective-permute-done.5.refs_1_ = bf16[64,1024]{1,0:T(8,128)(2,1)S(1)} collective-permute-done((bf16[64,1024]{1,0:T(8,128)(2,1)S(1)}, bf16[64,1024]{1,0:T(8,128)(2,1)S(1)}, u32[]{:S(2)}, u32[]{:S(2)}) %collective-permute-start.5) | collective-permute-done | bytes 131104 | tf_op jit(solution)/shard_map/ppermute | solution.py:370
  80.5 1.6 %collective-permute-done.12.refs_4_ = bf16[64,1024]{1,0:T(8,128)(2,1)S(1)} collective-permute-done((bf16[64,1024]{1,0:T(8,128)(2,1)S(1)}, bf16[64,1024]{1,0:T(8,128)(2,1)S(1)}, u32[]{:S(2)}, u32[]{:S(2)}) %collective-permute-start.12) | collective-permute-done | bytes 131104 | tf_op jit(solution)/shard_map/ppermute | solution.py:370
  82.1 3.3 %collective-permute-done.10.refs_2_ = bf16[64,1024]{1,0:T(8,128)(2,1)S(1)} collective-permute-done((bf16[64,1024]{1,0:T(8,128)(2,1)S(1)}, bf16[64,1024]{1,0:T(8,128)(2,1)S(1)}, u32[]{:S(2)}, u32[]{:S(2)}) %collective-permute-start.10) | collective-permute-done | bytes 131104 | tf_op jit(solution)/shard_map/ppermute | solution.py:370
  85.4 1.0 %collective-permute-done.11.refs_3_ = bf16[64,1024]{1,0:T(8,128)(2,1)S(1)} collective-permute-done((bf16[64,1024]{1,0:T(8,128)(2,1)S(1)}, bf16[64,1024]{1,0:T(8,128)(2,1)S(1)}, u32[]{:S(2)}, u32[]{:S(2)}) %collective-permute-start.11) | collective-permute-done | bytes 131104 | tf_op jit(solution)/shard_map/ppermute | solution.py:370
  86.4 0.0 collective-permute-done.13.refs_8_
  86.4 1.6 %shard_map.63 = bf16[64,4096]{1,0:T(8,128)(2,1)} custom-call(s32[64,1]{1,0:T(8,128)S(1)} %get-tuple-element.41.slot_ref, bf16[64,1024]{1,0:T(8,128)(2,1)S(1)} %get-tuple-element.55.refs_2_.refs_0_, bf16[64,1024]{1,0:T(8,128)(2,1)S(1)} %collective-permute-done.5.refs_1_, bf16[64,1024]{1,0:T(8,128)(2,1)S(1)} %collective-permute-done.10.refs_2_, ...), custom_call_target="tpu_custom_call" | custom-call | tf_op jit(solution)/shard_map/pallas_call | solution.py:393
Async XLA Ops:
  0.0 0.7 copy-start.1
  1.7 14.2 %collective-permute-start = (bf16[64,4224]{1,0:T(8,128)(2,1)S(1)}, bf16[64,4224]{1,0:T(8,128)(2,1)S(1)}, u32[]{:S(2)}, u32[]{:S(2)}) collective-permute-start(bf16[64,4224]{1,0:T(8,128)(2,1)S(1)} %get-tuple-element.61.x_ref), channel_id=1, source_target_pairs={{0,8},{12,4},{4,0},{8,12},{1,9},{13,5},{5,1},{9,13},{2,10},{14,6},... | collective-permute-start | bytes 1622024 | tf_op jit(solution)/shard_map/ppermute | solution.py:330
  15.9 15.0 %collective-permute-start.1 = (bf16[64,4224]{1,0:T(8,128)(2,1)S(1)}, bf16[64,4224]{1,0:T(8,128)(2,1)S(1)}, u32[]{:S(2)}, u32[]{:S(2)}) collective-permute-start(bf16[64,4224]{1,0:T(8,128)(2,1)S(1)} %collective-permute-done.refs_0_), channel_id=1, source_target_pairs={{4,0},{8,12},{5,1},{9,13},{6,2},{10,14},{7,3},{11,15},{20,16},{24,... | collective-permute-start | bytes 1622024 | tf_op jit(solution)/shard_map/ppermute | solution.py:330
  17.2 14.3 %collective-permute-start.3 = (bf16[64,4224]{1,0:T(8,128)(2,1)S(1)}, bf16[64,4224]{1,0:T(8,128)(2,1)S(1)}, u32[]{:S(2)}, u32[]{:S(2)}) collective-permute-start(bf16[64,4224]{1,0:T(8,128)(2,1)S(1)} %get-tuple-element.61.x_ref), channel_id=1, source_target_pairs={{4,8},{8,4},{5,9},{9,5},{6,10},{10,6},{7,11},{11,7},{20,24},{24,20... | collective-permute-start | bytes 1622024 | tf_op jit(solution)/shard_map/ppermute | solution.py:330
  17.9 21.6 %copy-start = (bf16[2,64,4096]{2,1,0:T(8,128)(2,1)S(1)}, bf16[2,64,4096]{2,1,0:T(8,128)(2,1)}, u32[]{:S(2)}) copy-start(bf16[2,64,4096]{2,1,0:T(8,128)(2,1)} %e_ref.5) | copy-start | bytes 3145732
  30.9 8.5 %collective-permute-start.2 = (bf16[128,1152]{1,0:T(8,128)(2,1)S(1)}, bf16[128,1152]{1,0:T(8,128)(2,1)S(1)}, u32[]{:S(2)}, u32[]{:S(2)}) collective-permute-start(bf16[128,1152]{1,0:T(8,128)(2,1)S(1)} %get-tuple-element.50), channel_id=1, source_target_pairs={{0,2},{2,0},{1,3},{3,1},{4,6},{6,4},{5,7},{7,5},{8,10},{10,8},{9,1... | collective-permute-start | bytes 884744 | tf_op jit(solution)/shard_map/ppermute | solution.py:361
  31.5 17.9 %collective-permute-start.6 = (bf16[64,4224]{1,0:T(8,128)(2,1)S(1)}, bf16[64,4224]{1,0:T(8,128)(2,1)S(1)}, u32[]{:S(2)}, u32[]{:S(2)}) collective-permute-start(bf16[64,4224]{1,0:T(8,128)(2,1)S(1)} %get-tuple-element.61.x_ref), channel_id=1, source_target_pairs={{0,4},{12,8},{8,0},{4,12},{1,5},{13,9},{9,1},{5,13},{2,6},{14,10},... | collective-permute-start | bytes 1622024 | tf_op jit(solution)/shard_map/ppermute | solution.py:330
  35.0 6.7 %collective-permute-start.4 = (bf16[64,1152]{1,0:T(8,128)(2,1)S(1)}, bf16[64,1152]{1,0:T(8,128)(2,1)S(1)}, u32[]{:S(2)}, u32[]{:S(2)}) collective-permute-start(bf16[64,1152]{1,0:T(8,128)(2,1)S(1)} %get-tuple-element.57), channel_id=1, source_target_pairs={{0,2},{2,0},{1,3},{3,1},{4,6},{6,4},{5,7},{7,5},{8,10},{10,8},{9,1... | collective-permute-start | bytes 442376 | tf_op jit(solution)/shard_map/ppermute | solution.py:361
  39.9 19.9 %collective-permute-start.7 = (bf16[32,4096]{1,0:T(8,128)(2,1)S(1)}, bf16[32,4096]{1,0:T(8,128)(2,1)S(1)}, u32[]{:S(2)}, u32[]{:S(2)}) collective-permute-start(bf16[32,4096]{1,0:T(8,128)(2,1)S(1)} %get-tuple-element.62), channel_id=1, source_target_pairs={{0,4},{4,12},{8,0},{12,8},{1,5},{5,13},{9,1},{13,9},{2,6},{6,14},{... | collective-permute-start | bytes 786440 | tf_op jit(solution)/shard_map/ppermute | solution.py:330
  42.0 21.3 %collective-permute-start.8 = (bf16[32,4096]{1,0:T(8,128)(2,1)S(1)}, bf16[32,4096]{1,0:T(8,128)(2,1)S(1)}, u32[]{:S(2)}, u32[]{:S(2)}) collective-permute-start(bf16[32,4096]{1,0:T(8,128)(2,1)S(1)} %get-tuple-element.65), channel_id=1, source_target_pairs={{0,12},{4,8},{8,4},{12,0},{1,13},{5,9},{9,5},{13,1},{2,14},{6,10},... | collective-permute-start | bytes 786440 | tf_op jit(solution)/shard_map/ppermute | solution.py:330
  63.3 5.2 %collective-permute-start.9 = (bf16[64,1152]{1,0:T(8,128)(2,1)S(1)}, bf16[64,1152]{1,0:T(8,128)(2,1)S(1)}, u32[]{:S(2)}, u32[]{:S(2)}) collective-permute-start(bf16[64,1152]{1,0:T(8,128)(2,1)S(1)} %get-tuple-element.66), channel_id=1, source_target_pairs={{0,2},{2,0},{1,3},{3,1},{4,6},{6,4},{5,7},{7,5},{8,10},{10,8},{9,1... | collective-permute-start | bytes 442376 | tf_op jit(solution)/shard_map/ppermute | solution.py:361
  68.8 17.5 %collective-permute-start.13 = (bf16[32,4096]{1,0:T(8,128)(2,1)S(1)}, bf16[32,4096]{1,0:T(8,128)(2,1)S(1)}, u32[]{:S(2)}, u32[]{:S(2)}) collective-permute-start(bf16[32,4096]{1,0:T(8,128)(2,1)S(1)} %get-tuple-element.76), channel_id=1, source_target_pairs={{0,8},{4,0},{8,12},{12,4},{1,9},{5,1},{9,13},{13,5},{2,10},{6,2},{... | collective-permute-start | bytes 786440 | tf_op jit(solution)/shard_map/ppermute | solution.py:330
  70.6 9.9 %collective-permute-start.5 = (bf16[64,1024]{1,0:T(8,128)(2,1)S(1)}, bf16[64,1024]{1,0:T(8,128)(2,1)S(1)}, u32[]{:S(2)}, u32[]{:S(2)}) collective-permute-start(bf16[64,1024]{1,0:T(8,128)(2,1)S(1)} %get-tuple-element.60), channel_id=1, source_target_pairs={{0,12},{4,8},{10,6},{14,2},{2,0},{6,4},{8,10},{12,14},{1,13},{5,9}... | collective-permute-start | bytes 393224 | tf_op jit(solution)/shard_map/ppermute | solution.py:370
  71.1 11.0 %collective-permute-start.12 = (bf16[64,1024]{1,0:T(8,128)(2,1)S(1)}, bf16[64,1024]{1,0:T(8,128)(2,1)S(1)}, u32[]{:S(2)}, u32[]{:S(2)}) collective-permute-start(bf16[64,1024]{1,0:T(8,128)(2,1)S(1)} %get-tuple-element.72), channel_id=1, source_target_pairs={{2,12},{6,8},{8,6},{12,2},{3,13},{7,9},{9,7},{13,3},{18,28},{22,24... | collective-permute-start | bytes 393224 | tf_op jit(solution)/shard_map/ppermute | solution.py:370
  75.2 10.2 %collective-permute-start.10 = (bf16[64,1024]{1,0:T(8,128)(2,1)S(1)}, bf16[64,1024]{1,0:T(8,128)(2,1)S(1)}, u32[]{:S(2)}, u32[]{:S(2)}) collective-permute-start(bf16[64,1024]{1,0:T(8,128)(2,1)S(1)} %get-tuple-element.70), channel_id=1, source_target_pairs={{0,4},{4,12},{10,2},{14,10},{2,8},{6,0},{8,14},{12,6},{1,5},{5,13}... | collective-permute-start | bytes 393224 | tf_op jit(solution)/shard_map/ppermute | solution.py:370
  75.7 10.7 %collective-permute-start.11 = (bf16[64,1024]{1,0:T(8,128)(2,1)S(1)}, bf16[64,1024]{1,0:T(8,128)(2,1)S(1)}, u32[]{:S(2)}, u32[]{:S(2)}) collective-permute-start(bf16[64,1024]{1,0:T(8,128)(2,1)S(1)} %get-tuple-element.71), channel_id=1, source_target_pairs={{0,8},{4,0},{10,14},{14,6},{2,4},{6,12},{8,2},{12,10},{1,9},{5,1},... | collective-permute-start | bytes 393224 | tf_op jit(solution)/shard_map/ppermute | solution.py:370

commit v5 on v4

--- a/solution.py
+++ b/solution.py
@@ -380,10 +380,10 @@
     got_2 = flip(send_2)
     d_2, mix_02, mix_20 = join(got_2, e, [(keep_2, own_2)], [base_0])
     came_2 = along(d_2, back(2))
-    got_c, came_1 = lax.optimization_barrier((got_c, came_1))
+    got_c, _ = lax.optimization_barrier((got_c, d_2))
     send_3, keep_3, own_3 = stage(dims, [got_c], w, s_t)
-    send_3, came_2 = lax.optimization_barrier((send_3, came_2))
-    d_3, mix_13, mix_31 = join(flip(send_3), e, [(keep_3, own_3)], [base_1])
+    got_3, came_1 = lax.optimization_barrier((flip(send_3), came_1))
+    d_3, mix_13, mix_31 = join(got_3, e, [(keep_3, own_3)], [base_1])
     from_02 = home(mix_20, straight(2) + crossed(0))
     from_2 = home(mix_02, crossed(2))
     came_3 = along(d_3, back(3))

time: 88.2 us -> 83.5 us (0.947)
  the two profiles are of different devices: /device:TPU:6 before, /device:TPU:10 now
where the time goes in v5:
time: 83.5 us; the launch traced here: 82.4 us
  waiting for transfers between devices  34.2 us (41%)
  starting transfers between devices  25.9 us (31%)
  Pallas kernels  21.6 us (26%)
    ppermute x7, starting transfers between devices, along(): return lax.ppermute(x, 'adapter', pairs)  20.8 us
    ppermute x4, waiting for transfers between devices, home(): return lax.ppermute(block, both, pairs)  15 us
    ppermute x7, waiting for transfers between devices, along(): return lax.ppermute(x, 'adapter', pairs)  13 us
    pallas_call x3, Pallas kernels, stage(): pl.pallas_call(functools.partial(stage_kernel, dims, len(xs), bool(before...  10.5 us
    pallas_call x1, Pallas kernels, first_stage(): pl.pallas_call(functools.partial(first_kernel, dims), in_specs=[VM, HB, H...  7.35 us
    ppermute x3, waiting for transfers between devices, flip(): return lax.ppermute(s, 'tensor', [(0, 1), (1, 0)])  6.12 us
    ppermute x4, starting transfers between devices, home(): return lax.ppermute(block, both, pairs)  3.52 us
  transfers between devices with their start and end apart: 14, of which 10 were waited for; matrix products, arithmetic and copies ran while one was open for 0% of the time, Pallas kernels for 23%

profile of v5, /device:TPU:10, one launch (start us, length us, event | category | flops | bytes accessed | tf_op | source)
XLA Modules:
  0.0 82.4 jit_solution(14277479270990242870)
XLA Ops:
  0.0 0.0 copy-start.1
  0.0 0.7 copy-done.1
  0.7 1.1 %shard_map.55 = (bf16[64,4224]{1,0:T(8,128)(2,1)S(1)}, s32[64,1]{1,0:T(8,128)S(1)}) custom-call(s32[1,64]{1,0:T(1,128)S(1)} %bitcast.4, bf16[64,4096]{1,0:T(8,128)(2,1)} %x_ref.1), custom_call_target="tpu_custom_call" | custom-call | tf_op jit(solution)/shard_map/pallas_call | solution.py:341
  1.7 0.5 collective-permute-start
  2.2 7.3 %shard_map.56 = (bf16[4096,2048]{1,0:T(8,128)(2,1)S(1)}, bf16[128,4096]{1,0:T(8,128)(2,1)S(1)}, bf16[64,1152]{1,0:T(8,128)(2,1)S(1)}, f32[64,1024]{1,0:T(8,128)S(1)}, f32[32,64]{1,0:T(8,128)S(1)}) custom-call(bf16[64,4224]{1,0:T(8,128)(2,1)S(1)} %get-tuple-element.60.x_ref, bf16[128,4096]{1,0:T(8,128)(2,1)} %bitcast.5, bf16[4096,2048]{1,0:T(8,128)(2,1)} %w_hbm.1), custom_call_target="tpu_custom_call" | custom-call | flops 1 | bytes 1 | tf_op jit(solution)/shard_map/pallas_call | solution.py:226
  9.6 7.1 %collective-permute-done.refs_0_ = bf16[64,4224]{1,0:T(8,128)(2,1)S(1)} collective-permute-done((bf16[64,4224]{1,0:T(8,128)(2,1)S(1)}, bf16[64,4224]{1,0:T(8,128)(2,1)S(1)}, u32[]{:S(2)}, u32[]{:S(2)}) %collective-permute-start) | collective-permute-done | bytes 540704 | tf_op jit(solution)/shard_map/ppermute | solution.py:330
  16.7 1.6 %collective-permute-start.1 = (bf16[64,4224]{1,0:T(8,128)(2,1)S(1)}, bf16[64,4224]{1,0:T(8,128)(2,1)S(1)}, u32[]{:S(2)}, u32[]{:S(2)}) collective-permute-start(bf16[64,4224]{1,0:T(8,128)(2,1)S(1)} %collective-permute-done.refs_0_), channel_id=1, source_target_pairs={{4,0},{8,12},{5,1},{9,13},{6,2},{10,14},{7,3},{11,15},{20,16},{24,... | collective-permute-start | bytes 1622024 | tf_op jit(solution)/shard_map/ppermute | solution.py:330
  18.3 4.5 %collective-permute-start.3 = (bf16[64,4224]{1,0:T(8,128)(2,1)S(1)}, bf16[64,4224]{1,0:T(8,128)(2,1)S(1)}, u32[]{:S(2)}, u32[]{:S(2)}) collective-permute-start(bf16[64,4224]{1,0:T(8,128)(2,1)S(1)} %get-tuple-element.60.x_ref), channel_id=1, source_target_pairs={{4,8},{8,4},{5,9},{9,5},{6,10},{10,6},{7,11},{11,7},{20,24},{24,20... | collective-permute-start | bytes 1622024 | tf_op jit(solution)/shard_map/ppermute | solution.py:330
  22.8 0.0 copy-start
  22.8 3.5 %shard_map.57 = (bf16[128,1152]{1,0:T(8,128)(2,1)S(1)}, f32[64,1024]{1,0:T(8,128)S(1)}, f32[32,64]{1,0:T(8,128)S(1)}) custom-call(bf16[64,4224]{1,0:T(8,128)(2,1)S(1)} %collective-permute-done.refs_0_, bf16[4096,2048]{1,0:T(8,128)(2,1)S(1)} %get-tuple-element.45.refs_1_.refs_2_, bf16[128,4096]{1,0:T(8,128)(2,1)S(1)} %get-tuple-element.46.refs_2_.refs_3_, ...), custom_call_target="tpu_custom_call" | custom-call | flops 1 | bytes 1 | tf_op jit(solution)/shard_map/pallas_call | solution.py:243
  26.3 2.6 %collective-permute-done.1.refs_0_ = bf16[64,4224]{1,0:T(8,128)(2,1)S(1)} collective-permute-done((bf16[64,4224]{1,0:T(8,128)(2,1)S(1)}, bf16[64,4224]{1,0:T(8,128)(2,1)S(1)}, u32[]{:S(2)}, u32[]{:S(2)}) %collective-permute-start.1) | collective-permute-done | bytes 540704 | tf_op jit(solution)/shard_map/ppermute | solution.py:330
  28.9 4.5 %collective-permute-start.6 = (bf16[64,4224]{1,0:T(8,128)(2,1)S(1)}, bf16[64,4224]{1,0:T(8,128)(2,1)S(1)}, u32[]{:S(2)}, u32[]{:S(2)}) collective-permute-start(bf16[64,4224]{1,0:T(8,128)(2,1)S(1)} %get-tuple-element.60.x_ref), channel_id=1, source_target_pairs={{0,4},{12,8},{8,0},{4,12},{1,5},{13,9},{9,1},{5,13},{2,6},{14,10},... | collective-permute-start | bytes 1622024 | tf_op jit(solution)/shard_map/ppermute | solution.py:330
  33.4 0.5 collective-permute-start.2
  33.9 2.0 %collective-permute-done.3.refs_1_ = bf16[64,4224]{1,0:T(8,128)(2,1)S(1)} collective-permute-done((bf16[64,4224]{1,0:T(8,128)(2,1)S(1)}, bf16[64,4224]{1,0:T(8,128)(2,1)S(1)}, u32[]{:S(2)}, u32[]{:S(2)}) %collective-permute-start.3) | collective-permute-done | bytes 540704 | tf_op jit(solution)/shard_map/ppermute | solution.py:330
  36.0 3.5 %shard_map.59 = (bf16[64,1152]{1,0:T(8,128)(2,1)S(1)}, f32[64,1024]{1,0:T(8,128)S(1)}, f32[32,64]{1,0:T(8,128)S(1)}) custom-call(bf16[64,4224]{1,0:T(8,128)(2,1)S(1)} %collective-permute-done.1.refs_0_, bf16[64,4224]{1,0:T(8,128)(2,1)S(1)} %collective-permute-done.3.refs_1_, bf16[4096,2048]{1,0:T(8,128)(2,1)S(1)} %get-tuple-element.45.refs_1_.refs_2_, ...), custom_call_target="tpu_custom_call" | custom-call | flops 1 | bytes 1 | tf_op jit(solution)/shard_map/pallas_call | solution.py:243
  39.5 0.6 collective-permute-start.4
  40.0 1.7 %collective-permute-done.2.got_ref = bf16[128,1152]{1,0:T(8,128)(2,1)S(1)} collective-permute-done((bf16[128,1152]{1,0:T(8,128)(2,1)S(1)}, bf16[128,1152]{1,0:T(8,128)(2,1)S(1)}, u32[]{:S(2)}, u32[]{:S(2)}) %collective-permute-start.2) | collective-permute-done | bytes 294944 | tf_op jit(solution)/shard_map/ppermute | solution.py:361
  41.7 0.0 copy-done
  41.7 0.5 shard_map.58
  42.2 0.3 collective-permute-start.8
  42.4 2.2 %collective-permute-done.4.got_ref = bf16[64,1152]{1,0:T(8,128)(2,1)S(1)} collective-permute-done((bf16[64,1152]{1,0:T(8,128)(2,1)S(1)}, bf16[64,1152]{1,0:T(8,128)(2,1)S(1)}, u32[]{:S(2)}, u32[]{:S(2)}) %collective-permute-start.4) | collective-permute-done | bytes 147488 | tf_op jit(solution)/shard_map/ppermute | solution.py:361
  44.7 0.3 shard_map.60
  45.0 1.3 %collective-permute-done.6.refs_0_ = bf16[64,4224]{1,0:T(8,128)(2,1)S(1)} collective-permute-done((bf16[64,4224]{1,0:T(8,128)(2,1)S(1)}, bf16[64,4224]{1,0:T(8,128)(2,1)S(1)}, u32[]{:S(2)}, u32[]{:S(2)}) %collective-permute-start.6) | collective-permute-done | bytes 540704 | tf_op jit(solution)/shard_map/ppermute | solution.py:330
  46.3 3.5 %shard_map.61 = (bf16[64,1152]{1,0:T(8,128)(2,1)S(1)}, f32[64,1024]{1,0:T(8,128)S(1)}, f32[32,64]{1,0:T(8,128)S(1)}) custom-call(bf16[64,4224]{1,0:T(8,128)(2,1)S(1)} %collective-permute-done.6.refs_0_, bf16[4096,2048]{1,0:T(8,128)(2,1)S(1)} %get-tuple-element.45.refs_1_.refs_2_, bf16[128,4096]{1,0:T(8,128)(2,1)S(1)} %get-tuple-element.46.refs_2_.refs_3_), custom_call_target="tpu_custom_call" | custom-call | flops 1 | bytes 1 | tf_op jit(solution)/shard_map/pallas_call | solution.py:243
  49.8 0.5 collective-permute-start.7
  50.3 0.9 %collective-permute-start.12 = (bf16[32,4096]{1,0:T(8,128)(2,1)S(1)}, bf16[32,4096]{1,0:T(8,128)(2,1)S(1)}, u32[]{:S(2)}, u32[]{:S(2)}) collective-permute-start(bf16[32,4096]{1,0:T(8,128)(2,1)S(1)} %get-tuple-element.61), channel_id=1, source_target_pairs={{0,12},{4,8},{8,4},{12,0},{1,13},{5,9},{9,5},{13,1},{2,14},{6,10},... | collective-permute-start | bytes 786440 | tf_op jit(solution)/shard_map/ppermute | solution.py:330
  51.2 1.6 %collective-permute-start.5 = (bf16[64,1024]{1,0:T(8,128)(2,1)S(1)}, bf16[64,1024]{1,0:T(8,128)(2,1)S(1)}, u32[]{:S(2)}, u32[]{:S(2)}) collective-permute-start(bf16[64,1024]{1,0:T(8,128)(2,1)S(1)} %get-tuple-element.59), channel_id=1, source_target_pairs={{0,12},{4,8},{10,6},{14,2},{2,0},{6,4},{8,10},{12,14},{1,13},{5,9}... | collective-permute-start | bytes 393224 | tf_op jit(solution)/shard_map/ppermute | solution.py:370
  52.7 0.0 collective-permute-done.8.refs_6_
  52.7 2.2 %collective-permute-done.7.got_ref = bf16[64,1152]{1,0:T(8,128)(2,1)S(1)} collective-permute-done((bf16[64,1152]{1,0:T(8,128)(2,1)S(1)}, bf16[64,1152]{1,0:T(8,128)(2,1)S(1)}, u32[]{:S(2)}, u32[]{:S(2)}) %collective-permute-start.7) | collective-permute-done | bytes 147488 | tf_op jit(solution)/shard_map/ppermute | solution.py:361
  55.0 0.3 shard_map.62
  55.3 8.5 %collective-permute-start.13 = (bf16[32,4096]{1,0:T(8,128)(2,1)S(1)}, bf16[32,4096]{1,0:T(8,128)(2,1)S(1)}, u32[]{:S(2)}, u32[]{:S(2)}) collective-permute-start(bf16[32,4096]{1,0:T(8,128)(2,1)S(1)} %get-tuple-element.74), channel_id=1, source_target_pairs={{0,8},{4,0},{8,12},{12,4},{1,9},{5,1},{9,13},{13,5},{2,10},{6,2},{... | collective-permute-start | bytes 786440 | tf_op jit(solution)/shard_map/ppermute | solution.py:330
  63.8 1.9 %collective-permute-start.11 = (bf16[64,1024]{1,0:T(8,128)(2,1)S(1)}, bf16[64,1024]{1,0:T(8,128)(2,1)S(1)}, u32[]{:S(2)}, u32[]{:S(2)}) collective-permute-start(bf16[64,1024]{1,0:T(8,128)(2,1)S(1)} %get-tuple-element.71), channel_id=1, source_target_pairs={{2,12},{6,8},{8,6},{12,2},{3,13},{7,9},{9,7},{13,3},{18,28},{22,24... | collective-permute-start | bytes 393224 | tf_op jit(solution)/shard_map/ppermute | solution.py:370
  65.7 0.1 collective-permute-start.9
  65.8 9.2 %collective-permute-done.5.refs_1_ = bf16[64,1024]{1,0:T(8,128)(2,1)S(1)} collective-permute-done((bf16[64,1024]{1,0:T(8,128)(2,1)S(1)}, bf16[64,1024]{1,0:T(8,128)(2,1)S(1)}, u32[]{:S(2)}, u32[]{:S(2)}) %collective-permute-start.5) | collective-permute-done | bytes 131104 | tf_op jit(solution)/shard_map/ppermute | solution.py:370
  74.9 0.0 collective-permute-start.10
  74.9 2.8 %collective-permute-done.11.refs_4_ = bf16[64,1024]{1,0:T(8,128)(2,1)S(1)} collective-permute-done((bf16[64,1024]{1,0:T(8,128)(2,1)S(1)}, bf16[64,1024]{1,0:T(8,128)(2,1)S(1)}, u32[]{:S(2)}, u32[]{:S(2)}) %collective-permute-start.11) | collective-permute-done | bytes 131104 | tf_op jit(solution)/shard_map/ppermute | solution.py:370
  77.8 0.0 collective-permute-done.12.refs_7_
  77.8 0.0 collective-permute-done.9.refs_2_
  77.8 3.0 %collective-permute-done.10.refs_3_ = bf16[64,1024]{1,0:T(8,128)(2,1)S(1)} collective-permute-done((bf16[64,1024]{1,0:T(8,128)(2,1)S(1)}, bf16[64,1024]{1,0:T(8,128)(2,1)S(1)}, u32[]{:S(2)}, u32[]{:S(2)}) %collective-permute-start.10) | collective-permute-done | bytes 131104 | tf_op jit(solution)/shard_map/ppermute | solution.py:370
  80.8 0.0 collective-permute-done.13.refs_8_
  80.8 1.6 %shard_map.63 = bf16[64,4096]{1,0:T(8,128)(2,1)} custom-call(s32[64,1]{1,0:T(8,128)S(1)} %get-tuple-element.40.slot_ref, bf16[64,1024]{1,0:T(8,128)(2,1)S(1)} %get-tuple-element.54.refs_2_.refs_0_, bf16[64,1024]{1,0:T(8,128)(2,1)S(1)} %collective-permute-done.5.refs_1_, bf16[64,1024]{1,0:T(8,128)(2,1)S(1)} %collective-permute-done.9.refs_2_, ...), custom_call_target="tpu_custom_call" | custom-call | tf_op jit(solution)/shard_map/pallas_call | solution.py:393
Async XLA Ops:
  0.0 0.7 copy-start.1
  1.7 15.0 %collective-permute-start = (bf16[64,4224]{1,0:T(8,128)(2,1)S(1)}, bf16[64,4224]{1,0:T(8,128)(2,1)S(1)}, u32[]{:S(2)}, u32[]{:S(2)}) collective-permute-start(bf16[64,4224]{1,0:T(8,128)(2,1)S(1)} %get-tuple-element.60.x_ref), channel_id=1, source_target_pairs={{0,8},{12,4},{4,0},{8,12},{1,9},{13,5},{5,1},{9,13},{2,10},{14,6},... | collective-permute-start | bytes 1622024 | tf_op jit(solution)/shard_map/ppermute | solution.py:330
  16.7 12.2 %collective-permute-start.1 = (bf16[64,4224]{1,0:T(8,128)(2,1)S(1)}, bf16[64,4224]{1,0:T(8,128)(2,1)S(1)}, u32[]{:S(2)}, u32[]{:S(2)}) collective-permute-start(bf16[64,4224]{1,0:T(8,128)(2,1)S(1)} %collective-permute-done.refs_0_), channel_id=1, source_target_pairs={{4,0},{8,12},{5,1},{9,13},{6,2},{10,14},{7,3},{11,15},{20,16},{24,... | collective-permute-start | bytes 1622024 | tf_op jit(solution)/shard_map/ppermute | solution.py:330
  18.3 17.7 %collective-permute-start.3 = (bf16[64,4224]{1,0:T(8,128)(2,1)S(1)}, bf16[64,4224]{1,0:T(8,128)(2,1)S(1)}, u32[]{:S(2)}, u32[]{:S(2)}) collective-permute-start(bf16[64,4224]{1,0:T(8,128)(2,1)S(1)} %get-tuple-element.60.x_ref), channel_id=1, source_target_pairs={{4,8},{8,4},{5,9},{9,5},{6,10},{10,6},{7,11},{11,7},{20,24},{24,20... | collective-permute-start | bytes 1622024 | tf_op jit(solution)/shard_map/ppermute | solution.py:330
  22.8 18.9 %copy-start = (bf16[2,64,4096]{2,1,0:T(8,128)(2,1)S(1)}, bf16[2,64,4096]{2,1,0:T(8,128)(2,1)}, u32[]{:S(2)}) copy-start(bf16[2,64,4096]{2,1,0:T(8,128)(2,1)} %e_ref.5) | copy-start | bytes 3145732
  28.9 17.4 %collective-permute-start.6 = (bf16[64,4224]{1,0:T(8,128)(2,1)S(1)}, bf16[64,4224]{1,0:T(8,128)(2,1)S(1)}, u32[]{:S(2)}, u32[]{:S(2)}) collective-permute-start(bf16[64,4224]{1,0:T(8,128)(2,1)S(1)} %get-tuple-element.60.x_ref), channel_id=1, source_target_pairs={{0,4},{12,8},{8,0},{4,12},{1,5},{13,9},{9,1},{5,13},{2,6},{14,10},... | collective-permute-start | bytes 1622024 | tf_op jit(solution)/shard_map/ppermute | solution.py:330
  33.4 8.3 %collective-permute-start.2 = (bf16[128,1152]{1,0:T(8,128)(2,1)S(1)}, bf16[128,1152]{1,0:T(8,128)(2,1)S(1)}, u32[]{:S(2)}, u32[]{:S(2)}) collective-permute-start(bf16[128,1152]{1,0:T(8,128)(2,1)S(1)} %get-tuple-element.49), channel_id=1, source_target_pairs={{0,2},{2,0},{1,3},{3,1},{4,6},{6,4},{5,7},{7,5},{8,10},{10,8},{9,1... | collective-permute-start | bytes 884744 | tf_op jit(solution)/shard_map/ppermute | solution.py:361
  39.5 5.2 %collective-permute-start.4 = (bf16[64,1152]{1,0:T(8,128)(2,1)S(1)}, bf16[64,1152]{1,0:T(8,128)(2,1)S(1)}, u32[]{:S(2)}, u32[]{:S(2)}) collective-permute-start(bf16[64,1152]{1,0:T(8,128)(2,1)S(1)} %get-tuple-element.56), channel_id=1, source_target_pairs={{0,2},{2,0},{1,3},{3,1},{4,6},{6,4},{5,7},{7,5},{8,10},{10,8},{9,1... | collective-permute-start | bytes 442376 | tf_op jit(solution)/shard_map/ppermute | solution.py:361
  42.2 10.6 %collective-permute-start.8 = (bf16[32,4096]{1,0:T(8,128)(2,1)S(1)}, bf16[32,4096]{1,0:T(8,128)(2,1)S(1)}, u32[]{:S(2)}, u32[]{:S(2)}) collective-permute-start(bf16[32,4096]{1,0:T(8,128)(2,1)S(1)} %get-tuple-element.64), channel_id=1, source_target_pairs={{0,4},{4,12},{8,0},{12,8},{1,5},{5,13},{9,1},{13,9},{2,6},{6,14},{... | collective-permute-start | bytes 786440 | tf_op jit(solution)/shard_map/ppermute | solution.py:330
  49.8 5.2 %collective-permute-start.7 = (bf16[64,1152]{1,0:T(8,128)(2,1)S(1)}, bf16[64,1152]{1,0:T(8,128)(2,1)S(1)}, u32[]{:S(2)}, u32[]{:S(2)}) collective-permute-start(bf16[64,1152]{1,0:T(8,128)(2,1)S(1)} %get-tuple-element.63), channel_id=1, source_target_pairs={{0,2},{2,0},{1,3},{3,1},{4,6},{6,4},{5,7},{7,5},{8,10},{10,8},{9,1... | collective-permute-start | bytes 442376 | tf_op jit(solution)/shard_map/ppermute | solution.py:361
  50.3 27.5 %collective-permute-start.12 = (bf16[32,4096]{1,0:T(8,128)(2,1)S(1)}, bf16[32,4096]{1,0:T(8,128)(2,1)S(1)}, u32[]{:S(2)}, u32[]{:S(2)}) collective-permute-start(bf16[32,4096]{1,0:T(8,128)(2,1)S(1)} %get-tuple-element.61), channel_id=1, source_target_pairs={{0,12},{4,8},{8,4},{12,0},{1,13},{5,9},{9,5},{13,1},{2,14},{6,10},... | collective-permute-start | bytes 786440 | tf_op jit(solution)/shard_map/ppermute | solution.py:330
  51.2 23.7 %collective-permute-start.5 = (bf16[64,1024]{1,0:T(8,128)(2,1)S(1)}, bf16[64,1024]{1,0:T(8,128)(2,1)S(1)}, u32[]{:S(2)}, u32[]{:S(2)}) collective-permute-start(bf16[64,1024]{1,0:T(8,128)(2,1)S(1)} %get-tuple-element.59), channel_id=1, source_target_pairs={{0,12},{4,8},{10,6},{14,2},{2,0},{6,4},{8,10},{12,14},{1,13},{5,9}... | collective-permute-start | bytes 393224 | tf_op jit(solution)/shard_map/ppermute | solution.py:370
  55.3 25.5 %collective-permute-start.13 = (bf16[32,4096]{1,0:T(8,128)(2,1)S(1)}, bf16[32,4096]{1,0:T(8,128)(2,1)S(1)}, u32[]{:S(2)}, u32[]{:S(2)}) collective-permute-start(bf16[32,4096]{1,0:T(8,128)(2,1)S(1)} %get-tuple-element.74), channel_id=1, source_target_pairs={{0,8},{4,0},{8,12},{12,4},{1,9},{5,1},{9,13},{13,5},{2,10},{6,2},{... | collective-permute-start | bytes 786440 | tf_op jit(solution)/shard_map/ppermute | solution.py:330
  63.8 14.0 %collective-permute-start.11 = (bf16[64,1024]{1,0:T(8,128)(2,1)S(1)}, bf16[64,1024]{1,0:T(8,128)(2,1)S(1)}, u32[]{:S(2)}, u32[]{:S(2)}) collective-permute-start(bf16[64,1024]{1,0:T(8,128)(2,1)S(1)} %get-tuple-element.71), channel_id=1, source_target_pairs={{2,12},{6,8},{8,6},{12,2},{3,13},{7,9},{9,7},{13,3},{18,28},{22,24... | collective-permute-start | bytes 393224 | tf_op jit(solution)/shard_map/ppermute | solution.py:370
  65.7 12.1 %collective-permute-start.9 = (bf16[64,1024]{1,0:T(8,128)(2,1)S(1)}, bf16[64,1024]{1,0:T(8,128)(2,1)S(1)}, u32[]{:S(2)}, u32[]{:S(2)}) collective-permute-start(bf16[64,1024]{1,0:T(8,128)(2,1)S(1)} %get-tuple-element.69), channel_id=1, source_target_pairs={{0,4},{4,12},{10,2},{14,10},{2,8},{6,0},{8,14},{12,6},{1,5},{5,13}... | collective-permute-start | bytes 393224 | tf_op jit(solution)/shard_map/ppermute | solution.py:370
  74.9 5.9 %collective-permute-start.10 = (bf16[64,1024]{1,0:T(8,128)(2,1)S(1)}, bf16[64,1024]{1,0:T(8,128)(2,1)S(1)}, u32[]{:S(2)}, u32[]{:S(2)}) collective-permute-start(bf16[64,1024]{1,0:T(8,128)(2,1)S(1)} %get-tuple-element.70), channel_id=1, source_target_pairs={{0,8},{4,0},{10,14},{14,6},{2,4},{6,12},{8,2},{12,10},{1,9},{5,1},... | collective-permute-start | bytes 393224 | tf_op jit(solution)/shard_map/ppermute | solution.py:370

commit v6 on v5

--- a/solution.py
+++ b/solution.py
@@ -97,10 +97,13 @@
     return pl.CostEstimate(flops=flops, bytes_accessed=nbytes, transcendentals=0)
 
 
-def pack_kernel(most, ids_ref, x_ref, packed_ref, col_ref, sem):
+def pack_kernel(most, ids_hbm, x_ref, packed_ref, col_ref, ids_ref, sems):
     depth = x_ref.shape[1]
-    copy = pltpu.make_async_copy(x_ref, packed_ref.at[:, :depth], sem)
+    copy = pltpu.make_async_copy(x_ref, packed_ref.at[:, :depth], sems.at[0])
+    fetch = pltpu.make_async_copy(ids_hbm, ids_ref, sems.at[1])
+    fetch.start()
     copy.start()
+    fetch.wait()
     ids = ids_ref[...]
     count = ids.shape[1]
     i = lax.broadcasted_iota(jnp.int32, (count, count), 0)
@@ -340,15 +343,15 @@
 
     packed, slot_col = pl.pallas_call(
         functools.partial(pack_kernel, most),
-        in_specs=[VM, HB],
+        in_specs=[HB, HB],
         out_specs=[VM, VM],
         out_shape=[
             pltpu.VMEM((rows, depth + LANES), BF16),
             jax.ShapeDtypeStruct((rows, 1), jnp.int32),
         ],
-        scratch_shapes=[pltpu.SemaphoreType.DMA],
+        scratch_shapes=[pltpu.VMEM((1, rows), jnp.int32), pltpu.SemaphoreType.DMA((2,))],
         compiler_params=PARAMS,
-    )(adapter_ids.reshape(1, rows), hbm(activations))
+    )(hbm(adapter_ids.reshape(1, rows)), hbm(activations))
 
     got_a = along(packed, [(0, 2), (3, 1), (1, 0), (2, 3)])
     s_t = jnp.swapaxes(shrink_weight, 1, 2).reshape(local * rank, -1)

time: 83.5 us -> 82.9 us (level)
  no operation moved by 1% of the time
where the time goes in v6:
time: 82.9 us; the launch traced here: 81.8 us
  waiting for transfers between devices  34.2 us (41%)
  starting transfers between devices  25.9 us (31%)
  Pallas kernels  21.6 us (26%)
    ppermute x7, starting transfers between devices, along(): return lax.ppermute(x, 'adapter', pairs)  20.8 us
    ppermute x4, waiting for transfers between devices, home(): return lax.ppermute(block, both, pairs)  15 us
    ppermute x7, waiting for transfers between devices, along(): return lax.ppermute(x, 'adapter', pairs)  13 us
    pallas_call x3, Pallas kernels, stage(): pl.pallas_call(functools.partial(stage_kernel, dims, len(xs), bool(before...  10.5 us
    pallas_call x1, Pallas kernels, first_stage(): pl.pallas_call(functools.partial(first_kernel, dims), in_specs=[VM, HB, H...  7.35 us
    ppermute x3, waiting for transfers between devices, flip(): return lax.ppermute(s, 'tensor', [(0, 1), (1, 0)])  6.14 us
    ppermute x4, starting transfers between devices, home(): return lax.ppermute(block, both, pairs)  3.51 us
  transfers between devices with their start and end apart: 14, of which 10 were waited for; matrix products, arithmetic and copies ran while one was open for 0% of the time, Pallas kernels for 23%

profile of v6, /device:TPU:10, one launch (start us, length us, event | category | flops | bytes accessed | tf_op | source)
XLA Modules:
  0.0 81.8 jit_solution(11189562235873698557)
XLA Ops:
  0.0 1.1 %shard_map.55 = (bf16[64,4224]{1,0:T(8,128)(2,1)S(1)}, s32[64,1]{1,0:T(8,128)S(1)}) custom-call(s32[1,64]{1,0:T(1,128)} %bitcast.5, bf16[64,4096]{1,0:T(8,128)(2,1)} %x_ref.1), custom_call_target="tpu_custom_call" | custom-call | tf_op jit(solution)/shard_map/pallas_call | solution.py:344
  1.1 0.5 collective-permute-start
  1.6 7.4 %shard_map.56 = (bf16[4096,2048]{1,0:T(8,128)(2,1)S(1)}, bf16[128,4096]{1,0:T(8,128)(2,1)S(1)}, bf16[64,1152]{1,0:T(8,128)(2,1)S(1)}, f32[64,1024]{1,0:T(8,128)S(1)}, f32[32,64]{1,0:T(8,128)S(1)}) custom-call(bf16[64,4224]{1,0:T(8,128)(2,1)S(1)} %get-tuple-element.60.x_ref, bf16[128,4096]{1,0:T(8,128)(2,1)} %bitcast.4, bf16[4096,2048]{1,0:T(8,128)(2,1)} %w_hbm.1), custom_call_target="tpu_custom_call" | custom-call | flops 1 | bytes 1 | tf_op jit(solution)/shard_map/pallas_call | solution.py:229
  8.9 7.1 %collective-permute-done.refs_0_ = bf16[64,4224]{1,0:T(8,128)(2,1)S(1)} collective-permute-done((bf16[64,4224]{1,0:T(8,128)(2,1)S(1)}, bf16[64,4224]{1,0:T(8,128)(2,1)S(1)}, u32[]{:S(2)}, u32[]{:S(2)}) %collective-permute-start) | collective-permute-done | bytes 540704 | tf_op jit(solution)/shard_map/ppermute | solution.py:333
  16.0 1.6 %collective-permute-start.1 = (bf16[64,4224]{1,0:T(8,128)(2,1)S(1)}, bf16[64,4224]{1,0:T(8,128)(2,1)S(1)}, u32[]{:S(2)}, u32[]{:S(2)}) collective-permute-start(bf16[64,4224]{1,0:T(8,128)(2,1)S(1)} %collective-permute-done.refs_0_), channel_id=1, source_target_pairs={{4,0},{8,12},{5,1},{9,13},{6,2},{10,14},{7,3},{11,15},{20,16},{24,... | collective-permute-start | bytes 1622024 | tf_op jit(solution)/shard_map/ppermute | solution.py:333
  17.6 4.5 %collective-permute-start.3 = (bf16[64,4224]{1,0:T(8,128)(2,1)S(1)}, bf16[64,4224]{1,0:T(8,128)(2,1)S(1)}, u32[]{:S(2)}, u32[]{:S(2)}) collective-permute-start(bf16[64,4224]{1,0:T(8,128)(2,1)S(1)} %get-tuple-element.60.x_ref), channel_id=1, source_target_pairs={{4,8},{8,4},{5,9},{9,5},{6,10},{10,6},{7,11},{11,7},{20,24},{24,20... | collective-permute-start | bytes 1622024 | tf_op jit(solution)/shard_map/ppermute | solution.py:333
  22.2 0.0 copy-start
  22.2 3.5 %shard_map.57 = (bf16[128,1152]{1,0:T(8,128)(2,1)S(1)}, f32[64,1024]{1,0:T(8,128)S(1)}, f32[32,64]{1,0:T(8,128)S(1)}) custom-call(bf16[64,4224]{1,0:T(8,128)(2,1)S(1)} %collective-permute-done.refs_0_, bf16[4096,2048]{1,0:T(8,128)(2,1)S(1)} %get-tuple-element.45.refs_1_.refs_2_, bf16[128,4096]{1,0:T(8,128)(2,1)S(1)} %get-tuple-element.46.refs_2_.refs_3_, ...), custom_call_target="tpu_custom_call" | custom-call | flops 1 | bytes 1 | tf_op jit(solution)/shard_map/pallas_call | solution.py:246
  25.7 2.6 %collective-permute-done.1.refs_0_ = bf16[64,4224]{1,0:T(8,128)(2,1)S(1)} collective-permute-done((bf16[64,4224]{1,0:T(8,128)(2,1)S(1)}, bf16[64,4224]{1,0:T(8,128)(2,1)S(1)}, u32[]{:S(2)}, u32[]{:S(2)}) %collective-permute-start.1) | collective-permute-done | bytes 540704 | tf_op jit(solution)/shard_map/ppermute | solution.py:333
  28.3 4.5 %collective-permute-start.6 = (bf16[64,4224]{1,0:T(8,128)(2,1)S(1)}, bf16[64,4224]{1,0:T(8,128)(2,1)S(1)}, u32[]{:S(2)}, u32[]{:S(2)}) collective-permute-start(bf16[64,4224]{1,0:T(8,128)(2,1)S(1)} %get-tuple-element.60.x_ref), channel_id=1, source_target_pairs={{0,4},{12,8},{8,0},{4,12},{1,5},{13,9},{9,1},{5,13},{2,6},{14,10},... | collective-permute-start | bytes 1622024 | tf_op jit(solution)/shard_map/ppermute | solution.py:333
  32.8 0.5 collective-permute-start.2
  33.3 2.0 %collective-permute-done.3.refs_1_ = bf16[64,4224]{1,0:T(8,128)(2,1)S(1)} collective-permute-done((bf16[64,4224]{1,0:T(8,128)(2,1)S(1)}, bf16[64,4224]{1,0:T(8,128)(2,1)S(1)}, u32[]{:S(2)}, u32[]{:S(2)}) %collective-permute-start.3) | collective-permute-done | bytes 540704 | tf_op jit(solution)/shard_map/ppermute | solution.py:333
  35.3 3.5 %shard_map.59 = (bf16[64,1152]{1,0:T(8,128)(2,1)S(1)}, f32[64,1024]{1,0:T(8,128)S(1)}, f32[32,64]{1,0:T(8,128)S(1)}) custom-call(bf16[64,4224]{1,0:T(8,128)(2,1)S(1)} %collective-permute-done.1.refs_0_, bf16[64,4224]{1,0:T(8,128)(2,1)S(1)} %collective-permute-done.3.refs_1_, bf16[4096,2048]{1,0:T(8,128)(2,1)S(1)} %get-tuple-element.45.refs_1_.refs_2_, ...), custom_call_target="tpu_custom_call" | custom-call | flops 1 | bytes 1 | tf_op jit(solution)/shard_map/pallas_call | solution.py:246
  38.8 0.6 collective-permute-start.4
  39.4 1.7 %collective-permute-done.2.got_ref = bf16[128,1152]{1,0:T(8,128)(2,1)S(1)} collective-permute-done((bf16[128,1152]{1,0:T(8,128)(2,1)S(1)}, bf16[128,1152]{1,0:T(8,128)(2,1)S(1)}, u32[]{:S(2)}, u32[]{:S(2)}) %collective-permute-start.2) | collective-permute-done | bytes 294944 | tf_op jit(solution)/shard_map/ppermute | solution.py:364
  41.1 0.0 copy-done
  41.1 0.5 shard_map.58
  41.5 0.3 collective-permute-start.8
  41.8 2.2 %collective-permute-done.4.got_ref = bf16[64,1152]{1,0:T(8,128)(2,1)S(1)} collective-permute-done((bf16[64,1152]{1,0:T(8,128)(2,1)S(1)}, bf16[64,1152]{1,0:T(8,128)(2,1)S(1)}, u32[]{:S(2)}, u32[]{:S(2)}) %collective-permute-start.4) | collective-permute-done | bytes 147488 | tf_op jit(solution)/shard_map/ppermute | solution.py:364
  44.0 0.3 shard_map.60
  44.4 1.3 %collective-permute-done.6.refs_0_ = bf16[64,4224]{1,0:T(8,128)(2,1)S(1)} collective-permute-done((bf16[64,4224]{1,0:T(8,128)(2,1)S(1)}, bf16[64,4224]{1,0:T(8,128)(2,1)S(1)}, u32[]{:S(2)}, u32[]{:S(2)}) %collective-permute-start.6) | collective-permute-done | bytes 540704 | tf_op jit(solution)/shard_map/ppermute | solution.py:333
  45.6 3.5 %shard_map.61 = (bf16[64,1152]{1,0:T(8,128)(2,1)S(1)}, f32[64,1024]{1,0:T(8,128)S(1)}, f32[32,64]{1,0:T(8,128)S(1)}) custom-call(bf16[64,4224]{1,0:T(8,128)(2,1)S(1)} %collective-permute-done.6.refs_0_, bf16[4096,2048]{1,0:T(8,128)(2,1)S(1)} %get-tuple-element.45.refs_1_.refs_2_, bf16[128,4096]{1,0:T(8,128)(2,1)S(1)} %get-tuple-element.46.refs_2_.refs_3_), custom_call_target="tpu_custom_call" | custom-call | flops 1 | bytes 1 | tf_op jit(solution)/shard_map/pallas_call | solution.py:246
  49.1 0.5 collective-permute-start.7
  49.7 0.9 %collective-permute-start.12 = (bf16[32,4096]{1,0:T(8,128)(2,1)S(1)}, bf16[32,4096]{1,0:T(8,128)(2,1)S(1)}, u32[]{:S(2)}, u32[]{:S(2)}) collective-permute-start(bf16[32,4096]{1,0:T(8,128)(2,1)S(1)} %get-tuple-element.61), channel_id=1, source_target_pairs={{0,12},{4,8},{8,4},{12,0},{1,13},{5,9},{9,5},{13,1},{2,14},{6,10},... | collective-permute-start | bytes 786440 | tf_op jit(solution)/shard_map/ppermute | solution.py:333
  50.6 1.5 %collective-permute-start.5 = (bf16[64,1024]{1,0:T(8,128)(2,1)S(1)}, bf16[64,1024]{1,0:T(8,128)(2,1)S(1)}, u32[]{:S(2)}, u32[]{:S(2)}) collective-permute-start(bf16[64,1024]{1,0:T(8,128)(2,1)S(1)} %get-tuple-element.59), channel_id=1, source_target_pairs={{0,12},{4,8},{10,6},{14,2},{2,0},{6,4},{8,10},{12,14},{1,13},{5,9}... | collective-permute-start | bytes 393224 | tf_op jit(solution)/shard_map/ppermute | solution.py:373
  52.1 0.0 collective-permute-done.8.refs_6_
  52.1 2.2 %collective-permute-done.7.got_ref = bf16[64,1152]{1,0:T(8,128)(2,1)S(1)} collective-permute-done((bf16[64,1152]{1,0:T(8,128)(2,1)S(1)}, bf16[64,1152]{1,0:T(8,128)(2,1)S(1)}, u32[]{:S(2)}, u32[]{:S(2)}) %collective-permute-start.7) | collective-permute-done | bytes 147488 | tf_op jit(solution)/shard_map/ppermute | solution.py:364
  54.3 0.3 shard_map.62
  54.7 8.5 %collective-permute-start.13 = (bf16[32,4096]{1,0:T(8,128)(2,1)S(1)}, bf16[32,4096]{1,0:T(8,128)(2,1)S(1)}, u32[]{:S(2)}, u32[]{:S(2)}) collective-permute-start(bf16[32,4096]{1,0:T(8,128)(2,1)S(1)} %get-tuple-element.74), channel_id=1, source_target_pairs={{0,8},{4,0},{8,12},{12,4},{1,9},{5,1},{9,13},{13,5},{2,10},{6,2},{... | collective-permute-start | bytes 786440 | tf_op jit(solution)/shard_map/ppermute | solution.py:333
  63.1 1.9 %collective-permute-start.11 = (bf16[64,1024]{1,0:T(8,128)(2,1)S(1)}, bf16[64,1024]{1,0:T(8,128)(2,1)S(1)}, u32[]{:S(2)}, u32[]{:S(2)}) collective-permute-start(bf16[64,1024]{1,0:T(8,128)(2,1)S(1)} %get-tuple-element.71), channel_id=1, source_target_pairs={{2,12},{6,8},{8,6},{12,2},{3,13},{7,9},{9,7},{13,3},{18,28},{22,24... | collective-permute-start | bytes 393224 | tf_op jit(solution)/shard_map/ppermute | solution.py:373
  65.1 0.1 collective-permute-start.9
  65.1 9.2 %collective-permute-done.5.refs_1_ = bf16[64,1024]{1,0:T(8,128)(2,1)S(1)} collective-permute-done((bf16[64,1024]{1,0:T(8,128)(2,1)S(1)}, bf16[64,1024]{1,0:T(8,128)(2,1)S(1)}, u32[]{:S(2)}, u32[]{:S(2)}) %collective-permute-start.5) | collective-permute-done | bytes 131104 | tf_op jit(solution)/shard_map/ppermute | solution.py:373
  74.3 0.0 collective-permute-start.10
  74.3 2.8 %collective-permute-done.11.refs_4_ = bf16[64,1024]{1,0:T(8,128)(2,1)S(1)} collective-permute-done((bf16[64,1024]{1,0:T(8,128)(2,1)S(1)}, bf16[64,1024]{1,0:T(8,128)(2,1)S(1)}, u32[]{:S(2)}, u32[]{:S(2)}) %collective-permute-start.11) | collective-permute-done | bytes 131104 | tf_op jit(solution)/shard_map/ppermute | solution.py:373
  77.1 0.0 collective-permute-done.12.refs_7_
  77.1 0.0 collective-permute-done.9.refs_2_
  77.1 3.0 %collective-permute-done.10.refs_3_ = bf16[64,1024]{1,0:T(8,128)(2,1)S(1)} collective-permute-done((bf16[64,1024]{1,0:T(8,128)(2,1)S(1)}, bf16[64,1024]{1,0:T(8,128)(2,1)S(1)}, u32[]{:S(2)}, u32[]{:S(2)}) %collective-permute-start.10) | collective-permute-done | bytes 131104 | tf_op jit(solution)/shard_map/ppermute | solution.py:373
  80.2 0.0 collective-permute-done.13.refs_8_
  80.2 1.6 %shard_map.63 = bf16[64,4096]{1,0:T(8,128)(2,1)} custom-call(s32[64,1]{1,0:T(8,128)S(1)} %get-tuple-element.40.slot_ref, bf16[64,1024]{1,0:T(8,128)(2,1)S(1)} %get-tuple-element.54.refs_2_.refs_0_, bf16[64,1024]{1,0:T(8,128)(2,1)S(1)} %collective-permute-done.5.refs_1_, bf16[64,1024]{1,0:T(8,128)(2,1)S(1)} %collective-permute-done.9.refs_2_, ...), custom_call_target="tpu_custom_call" | custom-call | tf_op jit(solution)/shard_map/pallas_call | solution.py:396
Async XLA Ops:
  1.1 15.0 %collective-permute-start = (bf16[64,4224]{1,0:T(8,128)(2,1)S(1)}, bf16[64,4224]{1,0:T(8,128)(2,1)S(1)}, u32[]{:S(2)}, u32[]{:S(2)}) collective-permute-start(bf16[64,4224]{1,0:T(8,128)(2,1)S(1)} %get-tuple-element.60.x_ref), channel_id=1, source_target_pairs={{0,8},{12,4},{4,0},{8,12},{1,9},{13,5},{5,1},{9,13},{2,10},{14,6},... | collective-permute-start | bytes 1622024 | tf_op jit(solution)/shard_map/ppermute | solution.py:333
  16.0 12.2 %collective-permute-start.1 = (bf16[64,4224]{1,0:T(8,128)(2,1)S(1)}, bf16[64,4224]{1,0:T(8,128)(2,1)S(1)}, u32[]{:S(2)}, u32[]{:S(2)}) collective-permute-start(bf16[64,4224]{1,0:T(8,128)(2,1)S(1)} %collective-permute-done.refs_0_), channel_id=1, source_target_pairs={{4,0},{8,12},{5,1},{9,13},{6,2},{10,14},{7,3},{11,15},{20,16},{24,... | collective-permute-start | bytes 1622024 | tf_op jit(solution)/shard_map/ppermute | solution.py:333
  17.6 17.7 %collective-permute-start.3 = (bf16[64,4224]{1,0:T(8,128)(2,1)S(1)}, bf16[64,4224]{1,0:T(8,128)(2,1)S(1)}, u32[]{:S(2)}, u32[]{:S(2)}) collective-permute-start(bf16[64,4224]{1,0:T(8,128)(2,1)S(1)} %get-tuple-element.60.x_ref), channel_id=1, source_target_pairs={{4,8},{8,4},{5,9},{9,5},{6,10},{10,6},{7,11},{11,7},{20,24},{24,20... | collective-permute-start | bytes 1622024 | tf_op jit(solution)/shard_map/ppermute | solution.py:333
  22.2 18.9 %copy-start = (bf16[2,64,4096]{2,1,0:T(8,128)(2,1)S(1)}, bf16[2,64,4096]{2,1,0:T(8,128)(2,1)}, u32[]{:S(2)}) copy-start(bf16[2,64,4096]{2,1,0:T(8,128)(2,1)} %e_ref.5) | copy-start | bytes 3145732
  28.3 17.4 %collective-permute-start.6 = (bf16[64,4224]{1,0:T(8,128)(2,1)S(1)}, bf16[64,4224]{1,0:T(8,128)(2,1)S(1)}, u32[]{:S(2)}, u32[]{:S(2)}) collective-permute-start(bf16[64,4224]{1,0:T(8,128)(2,1)S(1)} %get-tuple-element.60.x_ref), channel_id=1, source_target_pairs={{0,4},{12,8},{8,0},{4,12},{1,5},{13,9},{9,1},{5,13},{2,6},{14,10},... | collective-permute-start | bytes 1622024 | tf_op jit(solution)/shard_map/ppermute | solution.py:333
  32.8 8.3 %collective-permute-start.2 = (bf16[128,1152]{1,0:T(8,128)(2,1)S(1)}, bf16[128,1152]{1,0:T(8,128)(2,1)S(1)}, u32[]{:S(2)}, u32[]{:S(2)}) collective-permute-start(bf16[128,1152]{1,0:T(8,128)(2,1)S(1)} %get-tuple-element.49), channel_id=1, source_target_pairs={{0,2},{2,0},{1,3},{3,1},{4,6},{6,4},{5,7},{7,5},{8,10},{10,8},{9,1... | collective-permute-start | bytes 884744 | tf_op jit(solution)/shard_map/ppermute | solution.py:364
  38.8 5.2 %collective-permute-start.4 = (bf16[64,1152]{1,0:T(8,128)(2,1)S(1)}, bf16[64,1152]{1,0:T(8,128)(2,1)S(1)}, u32[]{:S(2)}, u32[]{:S(2)}) collective-permute-start(bf16[64,1152]{1,0:T(8,128)(2,1)S(1)} %get-tuple-element.56), channel_id=1, source_target_pairs={{0,2},{2,0},{1,3},{3,1},{4,6},{6,4},{5,7},{7,5},{8,10},{10,8},{9,1... | collective-permute-start | bytes 442376 | tf_op jit(solution)/shard_map/ppermute | solution.py:364
  41.5 10.6 %collective-permute-start.8 = (bf16[32,4096]{1,0:T(8,128)(2,1)S(1)}, bf16[32,4096]{1,0:T(8,128)(2,1)S(1)}, u32[]{:S(2)}, u32[]{:S(2)}) collective-permute-start(bf16[32,4096]{1,0:T(8,128)(2,1)S(1)} %get-tuple-element.64), channel_id=1, source_target_pairs={{0,4},{4,12},{8,0},{12,8},{1,5},{5,13},{9,1},{13,9},{2,6},{6,14},{... | collective-permute-start | bytes 786440 | tf_op jit(solution)/shard_map/ppermute | solution.py:333
  49.1 5.2 %collective-permute-start.7 = (bf16[64,1152]{1,0:T(8,128)(2,1)S(1)}, bf16[64,1152]{1,0:T(8,128)(2,1)S(1)}, u32[]{:S(2)}, u32[]{:S(2)}) collective-permute-start(bf16[64,1152]{1,0:T(8,128)(2,1)S(1)} %get-tuple-element.63), channel_id=1, source_target_pairs={{0,2},{2,0},{1,3},{3,1},{4,6},{6,4},{5,7},{7,5},{8,10},{10,8},{9,1... | collective-permute-start | bytes 442376 | tf_op jit(solution)/shard_map/ppermute | solution.py:364
  49.7 27.5 %collective-permute-start.12 = (bf16[32,4096]{1,0:T(8,128)(2,1)S(1)}, bf16[32,4096]{1,0:T(8,128)(2,1)S(1)}, u32[]{:S(2)}, u32[]{:S(2)}) collective-permute-start(bf16[32,4096]{1,0:T(8,128)(2,1)S(1)} %get-tuple-element.61), channel_id=1, source_target_pairs={{0,12},{4,8},{8,4},{12,0},{1,13},{5,9},{9,5},{13,1},{2,14},{6,10},... | collective-permute-start | bytes 786440 | tf_op jit(solution)/shard_map/ppermute | solution.py:333
  50.6 23.7 %collective-permute-start.5 = (bf16[64,1024]{1,0:T(8,128)(2,1)S(1)}, bf16[64,1024]{1,0:T(8,128)(2,1)S(1)}, u32[]{:S(2)}, u32[]{:S(2)}) collective-permute-start(bf16[64,1024]{1,0:T(8,128)(2,1)S(1)} %get-tuple-element.59), channel_id=1, source_target_pairs={{0,12},{4,8},{10,6},{14,2},{2,0},{6,4},{8,10},{12,14},{1,13},{5,9}... | collective-permute-start | bytes 393224 | tf_op jit(solution)/shard_map/ppermute | solution.py:373
  54.7 25.5 %collective-permute-start.13 = (bf16[32,4096]{1,0:T(8,128)(2,1)S(1)}, bf16[32,4096]{1,0:T(8,128)(2,1)S(1)}, u32[]{:S(2)}, u32[]{:S(2)}) collective-permute-start(bf16[32,4096]{1,0:T(8,128)(2,1)S(1)} %get-tuple-element.74), channel_id=1, source_target_pairs={{0,8},{4,0},{8,12},{12,4},{1,9},{5,1},{9,13},{13,5},{2,10},{6,2},{... | collective-permute-start | bytes 786440 | tf_op jit(solution)/shard_map/ppermute | solution.py:333
  63.1 14.0 %collective-permute-start.11 = (bf16[64,1024]{1,0:T(8,128)(2,1)S(1)}, bf16[64,1024]{1,0:T(8,128)(2,1)S(1)}, u32[]{:S(2)}, u32[]{:S(2)}) collective-permute-start(bf16[64,1024]{1,0:T(8,128)(2,1)S(1)} %get-tuple-element.71), channel_id=1, source_target_pairs={{2,12},{6,8},{8,6},{12,2},{3,13},{7,9},{9,7},{13,3},{18,28},{22,24... | collective-permute-start | bytes 393224 | tf_op jit(solution)/shard_map/ppermute | solution.py:373
  65.1 12.1 %collective-permute-start.9 = (bf16[64,1024]{1,0:T(8,128)(2,1)S(1)}, bf16[64,1024]{1,0:T(8,128)(2,1)S(1)}, u32[]{:S(2)}, u32[]{:S(2)}) collective-permute-start(bf16[64,1024]{1,0:T(8,128)(2,1)S(1)} %get-tuple-element.69), channel_id=1, source_target_pairs={{0,4},{4,12},{10,2},{14,10},{2,8},{6,0},{8,14},{12,6},{1,5},{5,13}... | collective-permute-start | bytes 393224 | tf_op jit(solution)/shard_map/ppermute | solution.py:373
  74.3 5.9 %collective-permute-start.10 = (bf16[64,1024]{1,0:T(8,128)(2,1)S(1)}, bf16[64,1024]{1,0:T(8,128)(2,1)S(1)}, u32[]{:S(2)}, u32[]{:S(2)}) collective-permute-start(bf16[64,1024]{1,0:T(8,128)(2,1)S(1)} %get-tuple-element.70), channel_id=1, source_target_pairs={{0,8},{4,0},{10,14},{14,6},{2,4},{6,12},{8,2},{12,10},{1,9},{5,1},... | collective-permute-start | bytes 393224 | tf_op jit(solution)/shard_map/ppermute | solution.py:373

commit v7 on v5

--- a/solution.py
+++ b/solution.py
@@ -382,10 +382,11 @@
     came_2 = along(d_2, back(2))
     got_c, _ = lax.optimization_barrier((got_c, d_2))
     send_3, keep_3, own_3 = stage(dims, [got_c], w, s_t)
-    got_3, came_1 = lax.optimization_barrier((flip(send_3), came_1))
+    got_3 = flip(send_3)
     d_3, mix_13, mix_31 = join(got_3, e, [(keep_3, own_3)], [base_1])
     from_02 = home(mix_20, straight(2) + crossed(0))
     from_2 = home(mix_02, crossed(2))
+    d_3, came_1 = lax.optimization_barrier((d_3, came_1))
     came_3 = along(d_3, back(3))
     from_13 = home(mix_13, straight(1) + crossed(3))
     from_31 = home(mix_31, straight(3) + crossed(1))

time: 83.5 us -> 83.5 us (level)
  no operation moved by 1% of the time
where the time goes in v7:
time: 83.5 us; the launch traced here: 82.4 us
  waiting for transfers between devices  34.5 us (41%)
  starting transfers between devices  25.5 us (31%)
  Pallas kernels  21.6 us (26%)
    ppermute x7, starting transfers between devices, along(): return lax.ppermute(x, 'adapter', pairs)  20.4 us
    ppermute x4, waiting for transfers between devices, home(): return lax.ppermute(block, both, pairs)  15.4 us
    ppermute x7, waiting for transfers between devices, along(): return lax.ppermute(x, 'adapter', pairs)  13 us
    pallas_call x3, Pallas kernels, stage(): pl.pallas_call(functools.partial(stage_kernel, dims, len(xs), bool(before...  10.5 us
    pallas_call x1, Pallas kernels, first_stage(): pl.pallas_call(functools.partial(first_kernel, dims), in_specs=[VM, HB, H...  7.35 us
    ppermute x3, waiting for transfers between devices, flip(): return lax.ppermute(s, 'tensor', [(0, 1), (1, 0)])  6.13 us
    ppermute x4, starting transfers between devices, home(): return lax.ppermute(block, both, pairs)  3.52 us
  transfers between devices with their start and end apart: 14, of which 10 were waited for; matrix products, arithmetic and copies ran while one was open for 0% of the time, Pallas kernels for 23%

profile of v7, /device:TPU:10, one launch (start us, length us, event | category | flops | bytes accessed | tf_op | source)
XLA Modules:
  0.0 82.4 jit_solution(14971417910205993021)
XLA Ops:
  0.0 0.0 copy-start.1
  0.0 0.7 copy-done.1
  0.7 1.1 %shard_map.55 = (bf16[64,4224]{1,0:T(8,128)(2,1)S(1)}, s32[64,1]{1,0:T(8,128)S(1)}) custom-call(s32[1,64]{1,0:T(1,128)S(1)} %bitcast.4, bf16[64,4096]{1,0:T(8,128)(2,1)} %x_ref.1), custom_call_target="tpu_custom_call" | custom-call | tf_op jit(solution)/shard_map/pallas_call | solution.py:341
  1.7 0.5 collective-permute-start
  2.2 7.3 %shard_map.56 = (bf16[4096,2048]{1,0:T(8,128)(2,1)S(1)}, bf16[128,4096]{1,0:T(8,128)(2,1)S(1)}, bf16[64,1152]{1,0:T(8,128)(2,1)S(1)}, f32[64,1024]{1,0:T(8,128)S(1)}, f32[32,64]{1,0:T(8,128)S(1)}) custom-call(bf16[64,4224]{1,0:T(8,128)(2,1)S(1)} %get-tuple-element.60.x_ref, bf16[128,4096]{1,0:T(8,128)(2,1)} %bitcast.5, bf16[4096,2048]{1,0:T(8,128)(2,1)} %w_hbm.1), custom_call_target="tpu_custom_call" | custom-call | flops 1 | bytes 1 | tf_op jit(solution)/shard_map/pallas_call | solution.py:226
  9.6 7.1 %collective-permute-done.refs_0_ = bf16[64,4224]{1,0:T(8,128)(2,1)S(1)} collective-permute-done((bf16[64,4224]{1,0:T(8,128)(2,1)S(1)}, bf16[64,4224]{1,0:T(8,128)(2,1)S(1)}, u32[]{:S(2)}, u32[]{:S(2)}) %collective-permute-start) | collective-permute-done | bytes 540704 | tf_op jit(solution)/shard_map/ppermute | solution.py:330
  16.7 1.6 %collective-permute-start.1 = (bf16[64,4224]{1,0:T(8,128)(2,1)S(1)}, bf16[64,4224]{1,0:T(8,128)(2,1)S(1)}, u32[]{:S(2)}, u32[]{:S(2)}) collective-permute-start(bf16[64,4224]{1,0:T(8,128)(2,1)S(1)} %collective-permute-done.refs_0_), channel_id=1, source_target_pairs={{4,0},{8,12},{5,1},{9,13},{6,2},{10,14},{7,3},{11,15},{20,16},{24,... | collective-permute-start | bytes 1622024 | tf_op jit(solution)/shard_map/ppermute | solution.py:330
  18.3 4.5 %collective-permute-start.3 = (bf16[64,4224]{1,0:T(8,128)(2,1)S(1)}, bf16[64,4224]{1,0:T(8,128)(2,1)S(1)}, u32[]{:S(2)}, u32[]{:S(2)}) collective-permute-start(bf16[64,4224]{1,0:T(8,128)(2,1)S(1)} %get-tuple-element.60.x_ref), channel_id=1, source_target_pairs={{4,8},{8,4},{5,9},{9,5},{6,10},{10,6},{7,11},{11,7},{20,24},{24,20... | collective-permute-start | bytes 1622024 | tf_op jit(solution)/shard_map/ppermute | solution.py:330
  22.8 0.0 copy-start
  22.8 3.5 %shard_map.57 = (bf16[128,1152]{1,0:T(8,128)(2,1)S(1)}, f32[64,1024]{1,0:T(8,128)S(1)}, f32[32,64]{1,0:T(8,128)S(1)}) custom-call(bf16[64,4224]{1,0:T(8,128)(2,1)S(1)} %collective-permute-done.refs_0_, bf16[4096,2048]{1,0:T(8,128)(2,1)S(1)} %get-tuple-element.45.refs_1_.refs_2_, bf16[128,4096]{1,0:T(8,128)(2,1)S(1)} %get-tuple-element.46.refs_2_.refs_3_, ...), custom_call_target="tpu_custom_call" | custom-call | flops 1 | bytes 1 | tf_op jit(solution)/shard_map/pallas_call | solution.py:243
  26.3 2.6 %collective-permute-done.1.refs_0_ = bf16[64,4224]{1,0:T(8,128)(2,1)S(1)} collective-permute-done((bf16[64,4224]{1,0:T(8,128)(2,1)S(1)}, bf16[64,4224]{1,0:T(8,128)(2,1)S(1)}, u32[]{:S(2)}, u32[]{:S(2)}) %collective-permute-start.1) | collective-permute-done | bytes 540704 | tf_op jit(solution)/shard_map/ppermute | solution.py:330
  28.9 4.5 %collective-permute-start.6 = (bf16[64,4224]{1,0:T(8,128)(2,1)S(1)}, bf16[64,4224]{1,0:T(8,128)(2,1)S(1)}, u32[]{:S(2)}, u32[]{:S(2)}) collective-permute-start(bf16[64,4224]{1,0:T(8,128)(2,1)S(1)} %get-tuple-element.60.x_ref), channel_id=1, source_target_pairs={{0,4},{12,8},{8,0},{4,12},{1,5},{13,9},{9,1},{5,13},{2,6},{14,10},... | collective-permute-start | bytes 1622024 | tf_op jit(solution)/shard_map/ppermute | solution.py:330
  33.4 0.5 collective-permute-start.2
  33.9 2.0 %collective-permute-done.3.refs_1_ = bf16[64,4224]{1,0:T(8,128)(2,1)S(1)} collective-permute-done((bf16[64,4224]{1,0:T(8,128)(2,1)S(1)}, bf16[64,4224]{1,0:T(8,128)(2,1)S(1)}, u32[]{:S(2)}, u32[]{:S(2)}) %collective-permute-start.3) | collective-permute-done | bytes 540704 | tf_op jit(solution)/shard_map/ppermute | solution.py:330
  36.0 3.5 %shard_map.59 = (bf16[64,1152]{1,0:T(8,128)(2,1)S(1)}, f32[64,1024]{1,0:T(8,128)S(1)}, f32[32,64]{1,0:T(8,128)S(1)}) custom-call(bf16[64,4224]{1,0:T(8,128)(2,1)S(1)} %collective-permute-done.1.refs_0_, bf16[64,4224]{1,0:T(8,128)(2,1)S(1)} %collective-permute-done.3.refs_1_, bf16[4096,2048]{1,0:T(8,128)(2,1)S(1)} %get-tuple-element.45.refs_1_.refs_2_, ...), custom_call_target="tpu_custom_call" | custom-call | flops 1 | bytes 1 | tf_op jit(solution)/shard_map/pallas_call | solution.py:243
  39.5 0.6 collective-permute-start.4
  40.0 1.7 %collective-permute-done.2.got_ref = bf16[128,1152]{1,0:T(8,128)(2,1)S(1)} collective-permute-done((bf16[128,1152]{1,0:T(8,128)(2,1)S(1)}, bf16[128,1152]{1,0:T(8,128)(2,1)S(1)}, u32[]{:S(2)}, u32[]{:S(2)}) %collective-permute-start.2) | collective-permute-done | bytes 294944 | tf_op jit(solution)/shard_map/ppermute | solution.py:361
  41.7 0.0 copy-done
  41.7 0.5 shard_map.58
  42.2 0.3 collective-permute-start.11
  42.4 2.2 %collective-permute-done.4.got_ref = bf16[64,1152]{1,0:T(8,128)(2,1)S(1)} collective-permute-done((bf16[64,1152]{1,0:T(8,128)(2,1)S(1)}, bf16[64,1152]{1,0:T(8,128)(2,1)S(1)}, u32[]{:S(2)}, u32[]{:S(2)}) %collective-permute-start.4) | collective-permute-done | bytes 147488 | tf_op jit(solution)/shard_map/ppermute | solution.py:361
  44.7 0.3 shard_map.60
  45.0 1.3 %collective-permute-done.6.refs_0_ = bf16[64,4224]{1,0:T(8,128)(2,1)S(1)} collective-permute-done((bf16[64,4224]{1,0:T(8,128)(2,1)S(1)}, bf16[64,4224]{1,0:T(8,128)(2,1)S(1)}, u32[]{:S(2)}, u32[]{:S(2)}) %collective-permute-start.6) | collective-permute-done | bytes 540704 | tf_op jit(solution)/shard_map/ppermute | solution.py:330
  46.3 3.5 %shard_map.61 = (bf16[64,1152]{1,0:T(8,128)(2,1)S(1)}, f32[64,1024]{1,0:T(8,128)S(1)}, f32[32,64]{1,0:T(8,128)S(1)}) custom-call(bf16[64,4224]{1,0:T(8,128)(2,1)S(1)} %collective-permute-done.6.refs_0_, bf16[4096,2048]{1,0:T(8,128)(2,1)S(1)} %get-tuple-element.45.refs_1_.refs_2_, bf16[128,4096]{1,0:T(8,128)(2,1)S(1)} %get-tuple-element.46.refs_2_.refs_3_), custom_call_target="tpu_custom_call" | custom-call | flops 1 | bytes 1 | tf_op jit(solution)/shard_map/pallas_call | solution.py:243
  49.8 0.5 collective-permute-start.7
  50.3 0.9 %collective-permute-start.12 = (bf16[32,4096]{1,0:T(8,128)(2,1)S(1)}, bf16[32,4096]{1,0:T(8,128)(2,1)S(1)}, u32[]{:S(2)}, u32[]{:S(2)}) collective-permute-start(bf16[32,4096]{1,0:T(8,128)(2,1)S(1)} %get-tuple-element.61), channel_id=1, source_target_pairs={{0,12},{4,8},{8,4},{12,0},{1,13},{5,9},{9,5},{13,1},{2,14},{6,10},... | collective-permute-start | bytes 786440 | tf_op jit(solution)/shard_map/ppermute | solution.py:330
  51.2 1.6 %collective-permute-start.5 = (bf16[64,1024]{1,0:T(8,128)(2,1)S(1)}, bf16[64,1024]{1,0:T(8,128)(2,1)S(1)}, u32[]{:S(2)}, u32[]{:S(2)}) collective-permute-start(bf16[64,1024]{1,0:T(8,128)(2,1)S(1)} %get-tuple-element.59), channel_id=1, source_target_pairs={{0,12},{4,8},{10,6},{14,2},{2,0},{6,4},{8,10},{12,14},{1,13},{5,9}... | collective-permute-start | bytes 393224 | tf_op jit(solution)/shard_map/ppermute | solution.py:370
  52.7 2.2 %collective-permute-done.7.got_ref = bf16[64,1152]{1,0:T(8,128)(2,1)S(1)} collective-permute-done((bf16[64,1152]{1,0:T(8,128)(2,1)S(1)}, bf16[64,1152]{1,0:T(8,128)(2,1)S(1)}, u32[]{:S(2)}, u32[]{:S(2)}) %collective-permute-start.7) | collective-permute-done | bytes 147488 | tf_op jit(solution)/shard_map/ppermute | solution.py:361
  55.0 0.3 shard_map.62
  55.3 0.0 collective-permute-done.11.refs_6_
  55.3 8.1 %collective-permute-start.13 = (bf16[32,4096]{1,0:T(8,128)(2,1)S(1)}, bf16[32,4096]{1,0:T(8,128)(2,1)S(1)}, u32[]{:S(2)}, u32[]{:S(2)}) collective-permute-start(bf16[32,4096]{1,0:T(8,128)(2,1)S(1)} %get-tuple-element.74), channel_id=1, source_target_pairs={{0,8},{4,0},{8,12},{12,4},{1,9},{5,1},{9,13},{13,5},{2,10},{6,2},{... | collective-permute-start | bytes 786440 | tf_op jit(solution)/shard_map/ppermute | solution.py:330
  63.4 1.9 %collective-permute-start.10 = (bf16[64,1024]{1,0:T(8,128)(2,1)S(1)}, bf16[64,1024]{1,0:T(8,128)(2,1)S(1)}, u32[]{:S(2)}, u32[]{:S(2)}) collective-permute-start(bf16[64,1024]{1,0:T(8,128)(2,1)S(1)} %get-tuple-element.69), channel_id=1, source_target_pairs={{2,12},{6,8},{8,6},{12,2},{3,13},{7,9},{9,7},{13,3},{18,28},{22,24... | collective-permute-start | bytes 393224 | tf_op jit(solution)/shard_map/ppermute | solution.py:370
  65.3 0.1 collective-permute-start.8
  65.4 9.6 %collective-permute-done.5.refs_1_ = bf16[64,1024]{1,0:T(8,128)(2,1)S(1)} collective-permute-done((bf16[64,1024]{1,0:T(8,128)(2,1)S(1)}, bf16[64,1024]{1,0:T(8,128)(2,1)S(1)}, u32[]{:S(2)}, u32[]{:S(2)}) %collective-permute-start.5) | collective-permute-done | bytes 131104 | tf_op jit(solution)/shard_map/ppermute | solution.py:370
  74.9 0.0 collective-permute-start.9
  74.9 2.8 %collective-permute-done.10.refs_4_ = bf16[64,1024]{1,0:T(8,128)(2,1)S(1)} collective-permute-done((bf16[64,1024]{1,0:T(8,128)(2,1)S(1)}, bf16[64,1024]{1,0:T(8,128)(2,1)S(1)}, u32[]{:S(2)}, u32[]{:S(2)}) %collective-permute-start.10) | collective-permute-done | bytes 131104 | tf_op jit(solution)/shard_map/ppermute | solution.py:370
  77.8 0.0 collective-permute-done.12.refs_7_
  77.8 0.0 collective-permute-done.8.refs_2_
  77.8 3.0 %collective-permute-done.9.refs_3_ = bf16[64,1024]{1,0:T(8,128)(2,1)S(1)} collective-permute-done((bf16[64,1024]{1,0:T(8,128)(2,1)S(1)}, bf16[64,1024]{1,0:T(8,128)(2,1)S(1)}, u32[]{:S(2)}, u32[]{:S(2)}) %collective-permute-start.9) | collective-permute-done | bytes 131104 | tf_op jit(solution)/shard_map/ppermute | solution.py:370
  80.8 0.0 collective-permute-done.13.refs_8_
  80.8 1.6 %shard_map.63 = bf16[64,4096]{1,0:T(8,128)(2,1)} custom-call(s32[64,1]{1,0:T(8,128)S(1)} %get-tuple-element.40.slot_ref, bf16[64,1024]{1,0:T(8,128)(2,1)S(1)} %get-tuple-element.54.refs_2_.refs_0_, bf16[64,1024]{1,0:T(8,128)(2,1)S(1)} %collective-permute-done.5.refs_1_, bf16[64,1024]{1,0:T(8,128)(2,1)S(1)} %collective-permute-done.8.refs_2_, ...), custom_call_target="tpu_custom_call" | custom-call | tf_op jit(solution)/shard_map/pallas_call | solution.py:394
Async XLA Ops:
  0.0 0.7 copy-start.1
  1.7 15.0 %collective-permute-start = (bf16[64,4224]{1,0:T(8,128)(2,1)S(1)}, bf16[64,4224]{1,0:T(8,128)(2,1)S(1)}, u32[]{:S(2)}, u32[]{:S(2)}) collective-permute-start(bf16[64,4224]{1,0:T(8,128)(2,1)S(1)} %get-tuple-element.60.x_ref), channel_id=1, source_target_pairs={{0,8},{12,4},{4,0},{8,12},{1,9},{13,5},{5,1},{9,13},{2,10},{14,6},... | collective-permute-start | bytes 1622024 | tf_op jit(solution)/shard_map/ppermute | solution.py:330
  16.7 12.2 %collective-permute-start.1 = (bf16[64,4224]{1,0:T(8,128)(2,1)S(1)}, bf16[64,4224]{1,0:T(8,128)(2,1)S(1)}, u32[]{:S(2)}, u32[]{:S(2)}) collective-permute-start(bf16[64,4224]{1,0:T(8,128)(2,1)S(1)} %collective-permute-done.refs_0_), channel_id=1, source_target_pairs={{4,0},{8,12},{5,1},{9,13},{6,2},{10,14},{7,3},{11,15},{20,16},{24,... | collective-permute-start | bytes 1622024 | tf_op jit(solution)/shard_map/ppermute | solution.py:330
  18.3 17.7 %collective-permute-start.3 = (bf16[64,4224]{1,0:T(8,128)(2,1)S(1)}, bf16[64,4224]{1,0:T(8,128)(2,1)S(1)}, u32[]{:S(2)}, u32[]{:S(2)}) collective-permute-start(bf16[64,4224]{1,0:T(8,128)(2,1)S(1)} %get-tuple-element.60.x_ref), channel_id=1, source_target_pairs={{4,8},{8,4},{5,9},{9,5},{6,10},{10,6},{7,11},{11,7},{20,24},{24,20... | collective-permute-start | bytes 1622024 | tf_op jit(solution)/shard_map/ppermute | solution.py:330
  22.8 18.9 %copy-start = (bf16[2,64,4096]{2,1,0:T(8,128)(2,1)S(1)}, bf16[2,64,4096]{2,1,0:T(8,128)(2,1)}, u32[]{:S(2)}) copy-start(bf16[2,64,4096]{2,1,0:T(8,128)(2,1)} %e_ref.5) | copy-start | bytes 3145732
  28.9 17.4 %collective-permute-start.6 = (bf16[64,4224]{1,0:T(8,128)(2,1)S(1)}, bf16[64,4224]{1,0:T(8,128)(2,1)S(1)}, u32[]{:S(2)}, u32[]{:S(2)}) collective-permute-start(bf16[64,4224]{1,0:T(8,128)(2,1)S(1)} %get-tuple-element.60.x_ref), channel_id=1, source_target_pairs={{0,4},{12,8},{8,0},{4,12},{1,5},{13,9},{9,1},{5,13},{2,6},{14,10},... | collective-permute-start | bytes 1622024 | tf_op jit(solution)/shard_map/ppermute | solution.py:330
  33.4 8.3 %collective-permute-start.2 = (bf16[128,1152]{1,0:T(8,128)(2,1)S(1)}, bf16[128,1152]{1,0:T(8,128)(2,1)S(1)}, u32[]{:S(2)}, u32[]{:S(2)}) collective-permute-start(bf16[128,1152]{1,0:T(8,128)(2,1)S(1)} %get-tuple-element.49), channel_id=1, source_target_pairs={{0,2},{2,0},{1,3},{3,1},{4,6},{6,4},{5,7},{7,5},{8,10},{10,8},{9,1... | collective-permute-start | bytes 884744 | tf_op jit(solution)/shard_map/ppermute | solution.py:361
  39.5 5.2 %collective-permute-start.4 = (bf16[64,1152]{1,0:T(8,128)(2,1)S(1)}, bf16[64,1152]{1,0:T(8,128)(2,1)S(1)}, u32[]{:S(2)}, u32[]{:S(2)}) collective-permute-start(bf16[64,1152]{1,0:T(8,128)(2,1)S(1)} %get-tuple-element.56), channel_id=1, source_target_pairs={{0,2},{2,0},{1,3},{3,1},{4,6},{6,4},{5,7},{7,5},{8,10},{10,8},{9,1... | collective-permute-start | bytes 442376 | tf_op jit(solution)/shard_map/ppermute | solution.py:361
  42.2 13.1 %collective-permute-start.11 = (bf16[32,4096]{1,0:T(8,128)(2,1)S(1)}, bf16[32,4096]{1,0:T(8,128)(2,1)S(1)}, u32[]{:S(2)}, u32[]{:S(2)}) collective-permute-start(bf16[32,4096]{1,0:T(8,128)(2,1)S(1)} %get-tuple-element.72), channel_id=1, source_target_pairs={{0,4},{4,12},{8,0},{12,8},{1,5},{5,13},{9,1},{13,9},{2,6},{6,14},{... | collective-permute-start | bytes 786440 | tf_op jit(solution)/shard_map/ppermute | solution.py:330
  49.8 5.2 %collective-permute-start.7 = (bf16[64,1152]{1,0:T(8,128)(2,1)S(1)}, bf16[64,1152]{1,0:T(8,128)(2,1)S(1)}, u32[]{:S(2)}, u32[]{:S(2)}) collective-permute-start(bf16[64,1152]{1,0:T(8,128)(2,1)S(1)} %get-tuple-element.63), channel_id=1, source_target_pairs={{0,2},{2,0},{1,3},{3,1},{4,6},{6,4},{5,7},{7,5},{8,10},{10,8},{9,1... | collective-permute-start | bytes 442376 | tf_op jit(solution)/shard_map/ppermute | solution.py:361
  50.3 27.5 %collective-permute-start.12 = (bf16[32,4096]{1,0:T(8,128)(2,1)S(1)}, bf16[32,4096]{1,0:T(8,128)(2,1)S(1)}, u32[]{:S(2)}, u32[]{:S(2)}) collective-permute-start(bf16[32,4096]{1,0:T(8,128)(2,1)S(1)} %get-tuple-element.61), channel_id=1, source_target_pairs={{0,12},{4,8},{8,4},{12,0},{1,13},{5,9},{9,5},{13,1},{2,14},{6,10},... | collective-permute-start | bytes 786440 | tf_op jit(solution)/shard_map/ppermute | solution.py:330
  51.2 23.7 %collective-permute-start.5 = (bf16[64,1024]{1,0:T(8,128)(2,1)S(1)}, bf16[64,1024]{1,0:T(8,128)(2,1)S(1)}, u32[]{:S(2)}, u32[]{:S(2)}) collective-permute-start(bf16[64,1024]{1,0:T(8,128)(2,1)S(1)} %get-tuple-element.59), channel_id=1, source_target_pairs={{0,12},{4,8},{10,6},{14,2},{2,0},{6,4},{8,10},{12,14},{1,13},{5,9}... | collective-permute-start | bytes 393224 | tf_op jit(solution)/shard_map/ppermute | solution.py:370
  55.3 25.5 %collective-permute-start.13 = (bf16[32,4096]{1,0:T(8,128)(2,1)S(1)}, bf16[32,4096]{1,0:T(8,128)(2,1)S(1)}, u32[]{:S(2)}, u32[]{:S(2)}) collective-permute-start(bf16[32,4096]{1,0:T(8,128)(2,1)S(1)} %get-tuple-element.74), channel_id=1, source_target_pairs={{0,8},{4,0},{8,12},{12,4},{1,9},{5,1},{9,13},{13,5},{2,10},{6,2},{... | collective-permute-start | bytes 786440 | tf_op jit(solution)/shard_map/ppermute | solution.py:330
  63.4 14.4 %collective-permute-start.10 = (bf16[64,1024]{1,0:T(8,128)(2,1)S(1)}, bf16[64,1024]{1,0:T(8,128)(2,1)S(1)}, u32[]{:S(2)}, u32[]{:S(2)}) collective-permute-start(bf16[64,1024]{1,0:T(8,128)(2,1)S(1)} %get-tuple-element.69), channel_id=1, source_target_pairs={{2,12},{6,8},{8,6},{12,2},{3,13},{7,9},{9,7},{13,3},{18,28},{22,24... | collective-permute-start | bytes 393224 | tf_op jit(solution)/shard_map/ppermute | solution.py:370
  65.3 12.4 %collective-permute-start.8 = (bf16[64,1024]{1,0:T(8,128)(2,1)S(1)}, bf16[64,1024]{1,0:T(8,128)(2,1)S(1)}, u32[]{:S(2)}, u32[]{:S(2)}) collective-permute-start(bf16[64,1024]{1,0:T(8,128)(2,1)S(1)} %get-tuple-element.67), channel_id=1, source_target_pairs={{0,4},{4,12},{10,2},{14,10},{2,8},{6,0},{8,14},{12,6},{1,5},{5,13}... | collective-permute-start | bytes 393224 | tf_op jit(solution)/shard_map/ppermute | solution.py:370
  74.9 5.9 %collective-permute-start.9 = (bf16[64,1024]{1,0:T(8,128)(2,1)S(1)}, bf16[64,1024]{1,0:T(8,128)(2,1)S(1)}, u32[]{:S(2)}, u32[]{:S(2)}) collective-permute-start(bf16[64,1024]{1,0:T(8,128)(2,1)S(1)} %get-tuple-element.68), channel_id=1, source_target_pairs={{0,8},{4,0},{10,14},{14,6},{2,4},{6,12},{8,2},{12,10},{1,9},{5,1},... | collective-permute-start | bytes 393224 | tf_op jit(solution)/shard_map/ppermute | solution.py:370
